TPU v7x, 1024 devices: a whole 8x8x8 slice. The times are simulated.
1024 devices in a mesh: rep: 8 (over x), node: 16 (over y, core), local: 8 (over z).
Axes of the slice: x: 8, y: 8, z: 8, core: 2. Of those that a mesh axis runs over, the one named last changes fastest.
Arguments:
- tokens: bfloat16 [16384, 2048], P(('rep', 'node', 'local')), may hold values from -6 to 6
- grads_out: bfloat16 [16384, 2048], P(('rep', 'node', 'local')), may hold values from -6 to 6
- expert_ids: int32 [16384, 8], P(('rep', 'node', 'local')), may hold values from 0 to 127, all different within a row; in each aligned block of 16 rows (0 to 15, 16 to 31, ...) at most 2 rows name the same one
- gates: bfloat16 [16384, 8], P(('rep', 'node', 'local')), may hold values from 0.019897461 to 0.29882812
- w_gate: bfloat16 [128, 2048, 384], P(('node', 'local')), may hold values from -0.125 to 0.125
- w_up: bfloat16 [128, 2048, 384], P(('node', 'local')), may hold values from -0.125 to 0.125
- w_down: bfloat16 [128, 384, 2048], P(('node', 'local')), may hold values from -0.3125 to 0.3125
Outputs:
- grad_tokens: bfloat16 [16384, 2048], P(('rep', 'node', 'local'))
- grad_gates: bfloat16 [16384, 8], P(('rep', 'node', 'local'))
- grad_w_gate: bfloat16 [128, 2048, 384], P(('node', 'local'), 'rep')
- grad_w_up: bfloat16 [128, 2048, 384], P(('node', 'local'), 'rep')
- grad_w_down: bfloat16 [128, 384, 2048], P(('node', 'local'), 'rep')
Inputs may be any that keep to these rules, and one draw needn't show every extreme that they name: `expert_ids`: each row names 8 different experts. Among the 16 rows of one device no expert is named more than 2 times, and in some device's rows some expert is named exactly 2 times.
All inputs are finite; a program needn't handle non-finite values.
Results may differ from a plain program's by a relative error of at most 0.019.
Values may be sent and summed in bfloat16 or wider, within the bound.
No kernel may reach another device: no remote copies, remote signals or barrier semaphores. Data moves between devices by JAX's collectives and lax.ppermute only.
A program may use at most 64 MiB of HBM per device.

v0:
```python
import jax
import jax.numpy as jnp
from jax import lax
from jax.sharding import PartitionSpec as P


def expert_pass(routed_rows, incoming, weights, w_gate, w_up, w_down):
    gate_pre = jnp.dot(routed_rows, w_gate, preferred_element_type=jnp.float32)
    up_pre = jnp.dot(routed_rows, w_up, preferred_element_type=jnp.float32)
    sigmoid_gate = jax.nn.sigmoid(gate_pre)
    hidden_act = (gate_pre * sigmoid_gate * up_pre).astype(jnp.bfloat16)
    expert_out = jnp.dot(hidden_act, w_down, preferred_element_type=jnp.float32)
    gate_grads = jnp.sum(incoming.astype(jnp.float32) * expert_out, axis=-1).astype(jnp.bfloat16)
    cotangent = (weights.astype(jnp.float32)[:, None] * incoming.astype(jnp.float32)).astype(
        jnp.bfloat16
    )
    grad_act = lax.dot_general(
        cotangent, w_down, (((1,), (1,)), ((), ())), preferred_element_type=jnp.float32
    )
    grad_gate = (grad_act * up_pre * sigmoid_gate * (1.0 + gate_pre * (1.0 - sigmoid_gate))).astype(
        jnp.bfloat16
    )
    grad_up = (grad_act * gate_pre * sigmoid_gate).astype(jnp.bfloat16)
    grad_rows = lax.dot_general(
        grad_gate, w_gate, (((1,), (1,)), ((), ())), preferred_element_type=jnp.float32
    )
    grad_rows = grad_rows + lax.dot_general(
        grad_up, w_up, (((1,), (1,)), ((), ())), preferred_element_type=jnp.float32
    )
    return (hidden_act, cotangent, grad_gate, grad_up, gate_grads, grad_rows.astype(jnp.bfloat16))


def contract_rows(left_rows, right_rows):
    return lax.dot_general(
        left_rows, right_rows, (((0,), (0,)), ((), ())), preferred_element_type=jnp.float32
    )


def carry_rows(row_block, per_slot):
    within = (
        lax.all_to_all(row_block, "local", split_axis=1, concat_axis=1, tiled=True),
        lax.all_to_all(per_slot, "local", split_axis=1, concat_axis=1, tiled=True),
    )
    return (
        lax.all_to_all(within[0], "node", split_axis=0, concat_axis=0, tiled=True),
        lax.all_to_all(within[1], "node", split_axis=0, concat_axis=0, tiled=True),
    )


def shards(tokens, grads_out, expert_ids, gates, w_gate, w_up, w_down):
    node_count = lax.axis_size("node")
    local_count = lax.axis_size("local")
    experts = node_count * local_count
    tok_dev, top_count = expert_ids.shape
    model_width = tokens.shape[1]
    hidden = w_gate.shape[2]
    capacity = max(1, 2 * tok_dev * top_count // experts)
    slot_count = experts * capacity
    flat_ids = expert_ids.reshape(-1)
    onehot = (flat_ids[:, None] == lax.iota(jnp.int32, experts)[None, :]).astype(jnp.int32)
    before = jnp.cumsum(onehot, axis=0) - onehot
    slot_index = flat_ids * capacity + jnp.sum(before * onehot, axis=1)
    placed = (lax.iota(jnp.int32, slot_count)[:, None] == slot_index[None, :]).astype(jnp.bfloat16)
    owners = lax.iota(jnp.int32, tok_dev * top_count) // top_count
    owned = (owners[:, None] == lax.iota(jnp.int32, tok_dev)[None, :]).astype(jnp.bfloat16)
    spread = jnp.dot(placed, owned, preferred_element_type=jnp.float32).astype(jnp.bfloat16)
    paired = jnp.concatenate((tokens, grads_out), axis=1)
    outgoing = jnp.dot(spread, paired, preferred_element_type=jnp.float32).astype(jnp.bfloat16)
    weights_out = jnp.dot(placed, gates.reshape(-1), preferred_element_type=jnp.float32).astype(
        jnp.bfloat16
    )
    arrived, arrived_weights = carry_rows(
        outgoing.reshape(node_count, local_count, capacity, 2 * model_width),
        weights_out.reshape(node_count, local_count, capacity),
    )
    arrived = arrived.reshape(slot_count, 2 * model_width)
    routed_rows = arrived[:, :model_width]
    incoming = arrived[:, model_width:]
    hidden_act, cotangent, grad_gate, grad_up, gate_grads, grad_rows = expert_pass(
        routed_rows, incoming, arrived_weights.reshape(slot_count), w_gate[0], w_up[0], w_down[0]
    )
    returned, returned_weights = carry_rows(
        grad_rows.reshape(node_count, local_count, capacity, model_width),
        gate_grads.reshape(node_count, local_count, capacity),
    )
    grad_tokens = contract_rows(spread, returned.reshape(slot_count, model_width)).astype(
        jnp.bfloat16
    )
    grad_gates = jnp.dot(
        returned_weights.reshape(slot_count), placed, preferred_element_type=jnp.float32
    )
    grad_gates = grad_gates.reshape(tok_dev, top_count).astype(jnp.bfloat16)
    gate_up = jnp.concatenate((grad_gate, grad_up), axis=1)
    gate_up_sum, down_sum = (
        lax.psum_scatter(
            contract_rows(routed_rows, gate_up).astype(jnp.bfloat16),
            "rep",
            scatter_dimension=0,
            tiled=True,
        ).astype(jnp.float32),
        lax.psum_scatter(
            contract_rows(hidden_act, cotangent).astype(jnp.bfloat16),
            "rep",
            scatter_dimension=0,
            tiled=True,
        ).astype(jnp.float32),
    )
    grad_w_gate = gate_up_sum[:, :hidden].astype(jnp.bfloat16)[None]
    grad_w_up = gate_up_sum[:, hidden:].astype(jnp.bfloat16)[None]
    grad_w_down = down_sum.astype(jnp.bfloat16)[None]
    return (grad_tokens, grad_gates, grad_w_gate, grad_w_up, grad_w_down)


def solution(mesh):
    placed = (
        P(("rep", "node", "local"), None),
        P(("rep", "node", "local"), None),
        P(("rep", "node", "local"), None),
        P(("rep", "node", "local"), None),
        P(("node", "local"), None, None),
        P(("node", "local"), None, None),
        P(("node", "local"), None, None),
    )
    return jax.shard_map(
        shards,
        mesh=mesh,
        in_specs=placed,
        out_specs=(
            P(("rep", "node", "local"), None),
            P(("rep", "node", "local"), None),
            P(("node", "local"), "rep", None),
            P(("node", "local"), "rep", None),
            P(("node", "local"), "rep", None),
        ),
        check_vma=False,
    )
```

profile of v0, /device:TPU:1, one launch (start us, length us, event | category | flops | bytes accessed | tf_op | source)
XLA Modules:
  0.0 288.4 jit_solution(6405128068478675538)
XLA Ops:
  10.5 17.2 %all-to-all-start = ((bf16[16,8,2]{0,2,1:T(2,128)(2,1)}), bf16[16,8,2]{0,2,1:T(2,128)(2,1)S(1)}, u32[]{:S(2)}, u32[]{:S(2)}) async-start(bf16[16,8,2]{0,2,1:T(2,128)(2,1)} %copy.53), calls=%async_computation | async-start | bytes 8192 | tf_op jit(solution)/shard_map/all_to_all | solution.py:42
  28.0 3.0 %convolution_convert_fusion = bf16[256,4096]{1,0:T(8,128)(2,1)} fusion(bf16[256,16]{0,1:T(8,128)(2,1)S(1)} %convolution_convert_fusion.4, bf16[16,2048]{1,0:T(8,128)(2,1)} %param.8, bf16[16,2048]{1,0:T(8,128)(2,1)} %param.7), kind=kOutput, calls=%fused_computation | convolution fusion | flops 34865152 | bytes 2236416 | tf_op jit(solution)/shard_map/dot_general | solution.py:68
  31.0 4.4 %reshape.96 = bf16[16,8,2,4096]{3,2,1,0:T(2,128)(2,1)} reshape(bf16[256,4096]{1,0:T(8,128)(2,1)} %convolution_convert_fusion) | data formatting | bytes 4194304 | tf_op jit(solution)/shard_map/reshape | solution.py:73
  35.4 5.6 %copy.57 = bf16[16,8,2,4096]{3,2,0,1:T(2,128)(2,1)} copy(bf16[16,8,2,4096]{3,2,1,0:T(2,128)(2,1)} %reshape.96) | data formatting | bytes 4194304 | tf_op jit(solution)/shard_map/reshape | solution.py:73
  41.0 6.6 %all-to-all-start.2 = ((bf16[16,8,2,4096]{3,2,0,1:T(2,128)(2,1)}), bf16[16,8,2,4096]{3,2,0,1:T(2,128)(2,1)}, u32[]{:S(2)}, u32[]{:S(2)}) async-start(bf16[16,8,2,4096]{3,2,0,1:T(2,128)(2,1)} %copy.57), calls=%async_computation.2 | async-start | bytes 4194304 | tf_op jit(solution)/shard_map/all_to_all | solution.py:41
  48.3 50.7 %all-to-all-done.2 = bf16[16,8,2,4096]{3,2,0,1:T(2,128)(2,1)} async-done(((bf16[16,8,2,4096]{3,2,0,1:T(2,128)(2,1)}), bf16[16,8,2,4096]{3,2,0,1:T(2,128)(2,1)}, u32[]{:S(2)}, u32[]{:S(2)}) %all-to-all-start.2) | async-done | bytes 2097184 | tf_op jit(solution)/shard_map/all_to_all | solution.py:41
  99.0 8.5 %all-to-all-start.1 = ((bf16[16,8,2]{1,2,0:T(2,128)(2,1)}), bf16[16,8,2]{1,2,0:T(2,128)(2,1)S(1)}, u32[]{:S(2)}, u32[]{:S(2)}) async-start(bf16[16,8,2]{1,2,0:T(2,128)(2,1)} %copy.54), calls=%async_computation.1 | async-start | bytes 16384 | tf_op jit(solution)/shard_map/all_to_all | solution.py:46
  107.6 5.7 %copy.58 = bf16[16,8,2,4096]{3,2,1,0:T(2,128)(2,1)} copy(bf16[16,8,2,4096]{3,2,0,1:T(2,128)(2,1)} %all-to-all-done.2) | data formatting | bytes 4194304 | tf_op jit(solution)/shard_map/all_to_all | solution.py:41
  114.5 6.0 %all-to-all-start.3 = ((bf16[16,8,2,4096]{3,2,1,0:T(2,128)(2,1)}), bf16[16,8,2,4096]{3,2,1,0:T(2,128)(2,1)}, u32[]{:S(2)}, u32[]{:S(2)}) async-start(bf16[16,8,2,4096]{3,2,1,0:T(2,128)(2,1)} %copy.58), calls=%async_computation.3 | async-start | bytes 4194304 | tf_op jit(solution)/shard_map/all_to_all | solution.py:45
  120.9 48.6 %all-to-all-done.3 = bf16[16,8,2,4096]{3,2,1,0:T(2,128)(2,1)} async-done(((bf16[16,8,2,4096]{3,2,1,0:T(2,128)(2,1)}), bf16[16,8,2,4096]{3,2,1,0:T(2,128)(2,1)}, u32[]{:S(2)}, u32[]{:S(2)}) %all-to-all-start.3) | async-done | bytes 2097184 | tf_op jit(solution)/shard_map/all_to_all | solution.py:45
  169.5 4.1 %reshape.97 = bf16[256,4096]{1,0:T(8,128)(2,1)} reshape(bf16[16,8,2,4096]{3,2,1,0:T(2,128)(2,1)} %all-to-all-done.3) | data formatting | bytes 4194304 | tf_op jit(solution)/shard_map/reshape | solution.py:76
  175.7 2.1 fusion.10
  179.4 2.7 convolution_convert_fusion.1
  182.1 2.5 fusion.12
  187.0 3.5 %all-to-all-start.6 = ((bf16[16,8,2]{0,2,1:T(2,128)(2,1)}), bf16[16,8,2]{0,2,1:T(2,128)(2,1)S(1)}, u32[]{:S(2)}, u32[]{:S(2)}) async-start(bf16[16,8,2]{0,2,1:T(2,128)(2,1)} %copy.61), calls=%async_computation.6 | async-start | bytes 8192 | tf_op jit(solution)/shard_map/all_to_all | solution.py:42
  193.5 3.1 %copy.59 = bf16[16,8,2,2048]{3,2,0,1:T(2,128)(2,1)} copy(bf16[16,8,2,2048]{3,2,1,0:T(2,128)(2,1)} %reshape.98) | data formatting | bytes 2097152 | tf_op jit(solution)/shard_map/reshape | solution.py:83
  196.6 6.5 %all-to-all-start.4 = ((bf16[16,8,2,2048]{3,2,0,1:T(2,128)(2,1)}), bf16[16,8,2,2048]{3,2,0,1:T(2,128)(2,1)S(1)}, u32[]{:S(2)}, u32[]{:S(2)}) async-start(bf16[16,8,2,2048]{3,2,0,1:T(2,128)(2,1)} %copy.59), calls=%async_computation.4 | async-start | bytes 2097152 | tf_op jit(solution)/shard_map/all_to_all | solution.py:41
  203.2 3.1 %convolution_convert_fusion.2 = bf16[384,2048]{1,0:T(8,128)(2,1)} fusion(bf16[256,384]{1,0:T(8,128)(2,1)S(1)} %copy-done.5, f32[256]{0:T(256)S(1)} %reshape.101, bf16[256,4096]{1,0:T(8,128)(2,1)} %reshape.97), kind=kOutput, calls=%fused_computation.2 | convolution fusion | flops 405012480 | bytes 2819072 | tf_op jit(solution)/shard_map/dot_general | solution.py:34
  207.0 25.4 %all-to-all-done.4 = bf16[16,8,2,2048]{3,2,0,1:T(2,128)(2,1)S(1)} async-done(((bf16[16,8,2,2048]{3,2,0,1:T(2,128)(2,1)}), bf16[16,8,2,2048]{3,2,0,1:T(2,128)(2,1)S(1)}, u32[]{:S(2)}, u32[]{:S(2)}) %all-to-all-start.4) | async-done | bytes 1048608 | tf_op jit(solution)/shard_map/all_to_all | solution.py:41
  232.3 5.0 %all-to-all-start.7 = ((bf16[16,8,2]{1,2,0:T(2,128)(2,1)}), bf16[16,8,2]{1,2,0:T(2,128)(2,1)S(1)}, u32[]{:S(2)}, u32[]{:S(2)}) async-start(bf16[16,8,2]{1,2,0:T(2,128)(2,1)} %copy.62), calls=%async_computation.7 | async-start | bytes 16384 | tf_op jit(solution)/shard_map/all_to_all | solution.py:46
  239.4 4.9 %all-to-all-done.7 = bf16[16,8,2]{1,2,0:T(2,128)(2,1)S(1)} async-done(((bf16[16,8,2]{1,2,0:T(2,128)(2,1)}), bf16[16,8,2]{1,2,0:T(2,128)(2,1)S(1)}, u32[]{:S(2)}, u32[]{:S(2)}) %all-to-all-start.7) | async-done | bytes 544 | tf_op jit(solution)/shard_map/all_to_all | solution.py:46
  244.3 4.1 %all-to-all-start.5 = ((bf16[16,8,2,2048]{3,2,1,0:T(2,128)(2,1)}), bf16[16,8,2,2048]{3,2,1,0:T(2,128)(2,1)S(1)}, u32[]{:S(2)}, u32[]{:S(2)}) async-start(bf16[16,8,2,2048]{3,2,1,0:T(2,128)(2,1)} %copy.60), calls=%async_computation.5 | async-start | bytes 2097152 | tf_op jit(solution)/shard_map/all_to_all | solution.py:45
  249.7 26.6 %all-to-all-done.5 = bf16[16,8,2,2048]{3,2,1,0:T(2,128)(2,1)S(1)} async-done(((bf16[16,8,2,2048]{3,2,1,0:T(2,128)(2,1)}), bf16[16,8,2,2048]{3,2,1,0:T(2,128)(2,1)S(1)}, u32[]{:S(2)}, u32[]{:S(2)}) %all-to-all-start.5) | async-done | bytes 1048608 | tf_op jit(solution)/shard_map/all_to_all | solution.py:45
  277.6 2.1 convolution_convert_fusion.3
  (53 shorter events, 22.0 us)
Async XLA Ops:
  7.2 170.7 %copy-start = (bf16[1,2048,384]{2,1,0:T(8,128)(2,1)S(1)}, bf16[1,2048,384]{2,1,0:T(8,128)(2,1)}, u32[]{:S(2)}) copy-start(bf16[1,2048,384]{2,1,0:T(8,128)(2,1)} %param.12) | copy-start | bytes 4718596
  9.5 25.9 %copy-start.3 = (s32[128]{0:T(128)}, s32[128]{0:T(128)S(1)}, u32[]{:S(2)}) copy-start(s32[128]{0:T(128)S(1)} %get-tuple-element.11) | copy-start | bytes 1540
  10.5 30.5 %all-to-all-start = ((bf16[16,8,2]{0,2,1:T(2,128)(2,1)}), bf16[16,8,2]{0,2,1:T(2,128)(2,1)S(1)}, u32[]{:S(2)}, u32[]{:S(2)}) async-start(bf16[16,8,2]{0,2,1:T(2,128)(2,1)} %copy.53), calls=%async_computation | async-start | bytes 8192 | tf_op jit(solution)/shard_map/all_to_all | solution.py:42
  41.0 58.0 %all-to-all-start.2 = ((bf16[16,8,2,4096]{3,2,0,1:T(2,128)(2,1)}), bf16[16,8,2,4096]{3,2,0,1:T(2,128)(2,1)}, u32[]{:S(2)}, u32[]{:S(2)}) async-start(bf16[16,8,2,4096]{3,2,0,1:T(2,128)(2,1)} %copy.57), calls=%async_computation.2 | async-start | bytes 4194304 | tf_op jit(solution)/shard_map/all_to_all | solution.py:41
  99.0 15.5 %all-to-all-start.1 = ((bf16[16,8,2]{1,2,0:T(2,128)(2,1)}), bf16[16,8,2]{1,2,0:T(2,128)(2,1)S(1)}, u32[]{:S(2)}, u32[]{:S(2)}) async-start(bf16[16,8,2]{1,2,0:T(2,128)(2,1)} %copy.54), calls=%async_computation.1 | async-start | bytes 16384 | tf_op jit(solution)/shard_map/all_to_all | solution.py:46
  114.5 55.0 %all-to-all-start.3 = ((bf16[16,8,2,4096]{3,2,1,0:T(2,128)(2,1)}), bf16[16,8,2,4096]{3,2,1,0:T(2,128)(2,1)}, u32[]{:S(2)}, u32[]{:S(2)}) async-start(bf16[16,8,2,4096]{3,2,1,0:T(2,128)(2,1)} %copy.58), calls=%async_computation.3 | async-start | bytes 4194304 | tf_op jit(solution)/shard_map/all_to_all | solution.py:45
  120.5 159.3 %reduce-scatter.3.cloned.1.call-start = ((), (), s32[]{:S(2)}) async-start(), calls=%async_computation.10 | async-start | bytes 3538944 | tf_op jit(solution)/shard_map/reduce_scatter | solution.py:95
  120.9 52.8 %copy-start.2 = (bf16[1,2048,384]{2,1,0:T(8,128)(2,1)S(1)}, bf16[1,2048,384]{2,1,0:T(8,128)(2,1)}, u32[]{:S(2)}) copy-start(bf16[1,2048,384]{2,1,0:T(8,128)(2,1)} %param.11) | copy-start | bytes 4718596
  173.6 2.1 copy-start.1
  187.0 9.7 %all-to-all-start.6 = ((bf16[16,8,2]{0,2,1:T(2,128)(2,1)}), bf16[16,8,2]{0,2,1:T(2,128)(2,1)S(1)}, u32[]{:S(2)}, u32[]{:S(2)}) async-start(bf16[16,8,2]{0,2,1:T(2,128)(2,1)} %copy.61), calls=%async_computation.6 | async-start | bytes 8192 | tf_op jit(solution)/shard_map/all_to_all | solution.py:42
  193.5 9.7 %copy-start.5 = (bf16[256,384]{1,0:T(8,128)(2,1)S(1)}, bf16[256,384]{1,0:T(8,128)(2,1)}, u32[]{:S(2)}) copy-start(bf16[256,384]{1,0:T(8,128)(2,1)} %get-tuple-element.5) | copy-start | bytes 589828
  196.6 35.7 %all-to-all-start.4 = ((bf16[16,8,2,2048]{3,2,0,1:T(2,128)(2,1)}), bf16[16,8,2,2048]{3,2,0,1:T(2,128)(2,1)S(1)}, u32[]{:S(2)}, u32[]{:S(2)}) async-start(bf16[16,8,2,2048]{3,2,0,1:T(2,128)(2,1)} %copy.59), calls=%async_computation.4 | async-start | bytes 2097152 | tf_op jit(solution)/shard_map/all_to_all | solution.py:41
  203.1 78.4 %reduce-scatter.5.cloned.1.call-start = ((), (), s32[]{:S(2)}) async-start(), calls=%async_computation.11 | async-start | bytes 1769472 | tf_op jit(solution)/shard_map/reduce_scatter | solution.py:101
  232.3 12.0 %all-to-all-start.7 = ((bf16[16,8,2]{1,2,0:T(2,128)(2,1)}), bf16[16,8,2]{1,2,0:T(2,128)(2,1)S(1)}, u32[]{:S(2)}, u32[]{:S(2)}) async-start(bf16[16,8,2]{1,2,0:T(2,128)(2,1)} %copy.62), calls=%async_computation.7 | async-start | bytes 16384 | tf_op jit(solution)/shard_map/all_to_all | solution.py:46
  237.4 11.4 %copy-start.4 = (s32[128]{0:T(128)S(1)}, s32[128]{0:T(128)}, u32[]{:S(2)}) copy-start(s32[128]{0:T(128)} %copy-done.3) | copy-start | bytes 1540
  244.3 32.1 %all-to-all-start.5 = ((bf16[16,8,2,2048]{3,2,1,0:T(2,128)(2,1)}), bf16[16,8,2,2048]{3,2,1,0:T(2,128)(2,1)S(1)}, u32[]{:S(2)}, u32[]{:S(2)}) async-start(bf16[16,8,2,2048]{3,2,1,0:T(2,128)(2,1)} %copy.60), calls=%async_computation.5 | async-start | bytes 2097152 | tf_op jit(solution)/shard_map/all_to_all | solution.py:45
Sparse Core Ops, SparseCore 0:
  182.3 42.4 reduce-scatter.2
  228.7 44.8 reduce-scatter.4
where the time goes:
time: 289 us; the launch traced here: 288 us
  waiting for transfers between devices  158 us (55%)
  starting transfers between devices  57.5 us (20%)
  local copies, waits for them, and re-layouts  37.2 us (13%)
  matrix products  21.3 us (7%)
  between operations  14.2 us (5%)
    all_to_all x2, waiting for transfers between devices, carry_rows(): lax.all_to_all(row_block, 'local', split_axis=1, concat_axis=1, tiled=True)  76.1 us
    all_to_all x2, waiting for transfers between devices, carry_rows(): lax.all_to_all(within[0], 'node', split_axis=0, concat_axis=0, tiled=True)  75.3 us
    all_to_all x2, starting transfers between devices, carry_rows(): lax.all_to_all(per_slot, 'local', split_axis=1, concat_axis=1, tiled=True)  20.7 us
    all_to_all x2, starting transfers between devices, carry_rows(): lax.all_to_all(within[1], 'node', split_axis=0, concat_axis=0, tiled=True)  13.6 us
    all_to_all x2, starting transfers between devices, carry_rows(): lax.all_to_all(row_block, 'local', split_axis=1, concat_axis=1, tiled=True)  13.1 us
    all_to_all x2, starting transfers between devices, carry_rows(): lax.all_to_all(within[0], 'node', split_axis=0, concat_axis=0, tiled=True)  10.1 us
    reshape x2, local copies, waits for them, and re-layouts, shards(): outgoing.reshape(node_count, local_count, capacity, 2 * model_width)  10 us
    dot_general x3, matrix products, contract_rows(): lax.dot_general(left_rows, right_rows, (((0,), (0,)), ((), ())), preferre...  7.9 us
  transfers between devices with their start and end apart: 10, of which 7 were waited for; matrix products, arithmetic and copies ran while one was open for 15% of the time, Pallas kernels for 0%

commit v1 on v0

v1 whole, which is shorter than its diff:
```python
import jax
import jax.numpy as jnp
from jax import lax
from jax.sharding import PartitionSpec as P

PLANE = ("node", "local")


def exchange(blocks):
    return lax.all_to_all(blocks, PLANE, split_axis=0, concat_axis=0, tiled=True)


def dot(left, right, left_dim, right_dim):
    return lax.dot_general(
        left, right, (((left_dim,), (right_dim,)), ((), ())), preferred_element_type=jnp.float32
    )


def shards(tokens, grads_out, expert_ids, gates, w_gate, w_up, w_down):
    experts = lax.axis_size("node") * lax.axis_size("local")
    tok_dev, top_count = expert_ids.shape
    model_width = tokens.shape[1]
    hidden = w_gate.shape[2]
    pairs = tok_dev * top_count
    capacity = max(1, 2 * pairs // experts)
    slot_count = experts * capacity
    w_gate, w_up, w_down = w_gate[0], w_up[0], w_down[0]

    flat_ids = expert_ids.reshape(-1)
    earlier = lax.iota(jnp.int32, pairs)[:, None] > lax.iota(jnp.int32, pairs)[None, :]
    same = flat_ids[:, None] == flat_ids[None, :]
    rank = jnp.sum((same & earlier).astype(jnp.int32), axis=1)
    slot_index = flat_ids * capacity + rank
    placed = lax.iota(jnp.int32, slot_count)[:, None] == slot_index[None, :]
    placed = placed.astype(jnp.bfloat16)
    owners = lax.iota(jnp.int32, pairs) // top_count
    owned = owners[:, None] == lax.iota(jnp.int32, tok_dev)[None, :]
    flat_gates = gates.reshape(-1)
    zero = jnp.zeros((), jnp.bfloat16)
    spread = dot(placed, owned.astype(jnp.bfloat16), 1, 0).astype(jnp.bfloat16)
    weighted = dot(placed, jnp.where(owned, flat_gates[:, None], zero), 1, 0).astype(jnp.bfloat16)

    def send(spreader, rows):
        blocks = dot(spreader, rows, 1, 0).astype(jnp.bfloat16)
        blocks = blocks.reshape(experts, capacity, model_width)
        return exchange(blocks).reshape(slot_count, model_width)

    routed = send(spread, tokens)
    cotangent = send(weighted, grads_out)

    gate_pre = dot(routed, w_gate, 1, 0)
    up_pre = dot(routed, w_up, 1, 0)
    sigmoid_gate = jax.nn.sigmoid(gate_pre)
    silu_gate = gate_pre * sigmoid_gate
    hidden_act = (silu_gate * up_pre).astype(jnp.bfloat16)
    slope = up_pre * sigmoid_gate * (1.0 + gate_pre * (1.0 - sigmoid_gate))

    grad_act = dot(cotangent, w_down, 1, 1)
    grad_gate = (grad_act * slope).astype(jnp.bfloat16)
    grad_up = (grad_act * silu_gate).astype(jnp.bfloat16)

    def reduce(partial):
        return lax.psum_scatter(
            partial.astype(jnp.bfloat16), "rep", scatter_dimension=0, tiled=True
        )

    gate_up = jnp.concatenate((grad_gate, grad_up), axis=1)
    gate_up_sum = reduce(dot(routed, gate_up, 0, 0))
    down_sum = reduce(dot(hidden_act, cotangent, 0, 0))

    gate_score = jnp.sum(hidden_act.astype(jnp.float32) * grad_act, axis=1).astype(jnp.bfloat16)
    grad_rows = (dot(grad_gate, w_gate, 1, 1) + dot(grad_up, w_up, 1, 1)).astype(jnp.bfloat16)
    returned_score = exchange(gate_score.reshape(experts, capacity)).reshape(slot_count)
    returned = exchange(grad_rows.reshape(experts, capacity, model_width))
    returned = returned.reshape(slot_count, model_width)

    grad_tokens = dot(spread, returned, 0, 0).astype(jnp.bfloat16)
    score = dot(returned_score[None, :], placed, 1, 0).reshape(tok_dev, top_count)
    grad_gates = (score / gates.astype(jnp.float32)).astype(jnp.bfloat16)
    return (
        grad_tokens,
        grad_gates,
        gate_up_sum[None, :, :hidden],
        gate_up_sum[None, :, hidden:],
        down_sum[None],
    )


def solution(mesh):
    rows = P(("rep", "node", "local"), None)
    weights = P(PLANE, None, None)
    sharded = P(PLANE, "rep", None)
    return jax.shard_map(
        shards,
        mesh=mesh,
        in_specs=(rows, rows, rows, rows, weights, weights, weights),
        out_specs=(rows, rows, sharded, sharded, sharded),
        check_vma=False,
    )
```

time: 289 us -> 215 us (0.74)
  waiting for transfers between devices: 158 us -> 118 us
  local copies, waits for them, and re-layouts: 37.2 us -> 16.1 us
  starting transfers between devices: 57.5 us -> 45.6 us
  matrix products: 21.3 us -> 17.1 us
    all_to_all x8 -> x4, waiting for transfers between devices: 158 us -> 89.9 us  [exchange(): lax.all_to_all(blocks, PLANE, split_axis=0, concat_axis=0, tiled=True)]
    reduce_scatter x2, waiting for transfers between devices: 0.01 us -> 27.7 us  [reduce(): lax.psum_scatter(partial.astype(jnp.bfloat16), 'rep', scatter_dimension=0...]
    all_to_all x8 -> x4, starting transfers between devices: 57.4 us -> 45.4 us  [exchange(): lax.all_to_all(blocks, PLANE, split_axis=0, concat_axis=0, tiled=True)]
    reshape x10 -> x7, local copies, waits for them, and re-layouts: 21.1 us -> 10.6 us  [the longest x2 4.02 us: send(): blocks = blocks.reshape(experts, capacity, model_width)]
    all_to_all x6 -> x0, local copies, waits for them, and re-layouts: 9.33 us -> none  [the longest x2 7.7 us: carry_rows(): lax.all_to_all(row_block, 'local', split_axis=1, concat_axis=1, tiled=True)]
    dot_general x13 -> x12, matrix products: 21.3 us -> 17.1 us  [dot(): lax.dot_general(left, right, (((left_dim,), (right_dim,)), ((), ())), pre...]
  transfers between devices with their start and end apart: 10 -> 6, of which waited for: 7 -> 5; matrix products, arithmetic and copies ran while one was open for 15% -> 10% of each run, Pallas kernels for 0% -> 0%
where the time goes in v1:
time: 215 us; the launch traced here: 211 us
  waiting for transfers between devices  118 us (55%)
  starting transfers between devices  45.6 us (21%)
  matrix products  17.1 us (8%)
  local copies, waits for them, and re-layouts  16.1 us (7%)
  between operations  14.2 us (7%)
    all_to_all x4, waiting for transfers between devices, exchange(): lax.all_to_all(blocks, PLANE, split_axis=0, concat_axis=0, tiled=True)  89.9 us
    all_to_all x4, starting transfers between devices, exchange(): lax.all_to_all(blocks, PLANE, split_axis=0, concat_axis=0, tiled=True)  45.4 us
    reduce_scatter x2, waiting for transfers between devices, reduce(): lax.psum_scatter(partial.astype(jnp.bfloat16), 'rep', scatter_dimension=0...  27.7 us
    dot_general x12, matrix products, dot(): lax.dot_general(left, right, (((left_dim,), (right_dim,)), ((), ())), pre...  17.1 us
  transfers between devices with their start and end apart: 6, of which 5 were waited for; matrix products, arithmetic and copies ran while one was open for 10% of the time, Pallas kernels for 0%

profile of v1, /device:TPU:1, one launch (start us, length us, event | category | flops | bytes accessed | tf_op | source)
XLA Modules:
  0.0 211.5 jit_solution(9668621423139646252)
XLA Ops:
  8.6 1.3 convolution_convert_fusion.2
  9.9 1.5 reshape.106
  11.4 25.4 %all-to-all-start.1 = ((bf16[128,2,2048]{2,1,0:T(2,128)(2,1)}), bf16[128,2,2048]{2,1,0:T(2,128)(2,1)S(1)}, u32[]{:S(2)}, u32[]{:S(2)}) async-start(bf16[128,2,2048]{2,1,0:T(2,128)(2,1)} %reshape.106), calls=%async_computation.1 | async-start | bytes 2097152 | tf_op jit(solution)/shard_map/all_to_all | solution.py:10
  37.0 1.7 convolution_convert_fusion.3
  38.7 2.5 %reshape.104 = bf16[128,2,2048]{2,1,0:T(2,128)(2,1)} reshape(bf16[256,2048]{1,0:T(8,128)(2,1)} %convolution_convert_fusion.3) | data formatting | bytes 2097152 | tf_op jit(solution)/shard_map/reshape | solution.py:45
  41.2 27.6 %all-to-all-done.1 = bf16[128,2,2048]{2,1,0:T(2,128)(2,1)S(1)} async-done(((bf16[128,2,2048]{2,1,0:T(2,128)(2,1)}), bf16[128,2,2048]{2,1,0:T(2,128)(2,1)S(1)}, u32[]{:S(2)}, u32[]{:S(2)}) %all-to-all-start.1) | async-done | bytes 1048608 | tf_op jit(solution)/shard_map/all_to_all | solution.py:10
  68.8 6.4 %all-to-all-start = ((bf16[128,2,2048]{2,1,0:T(2,128)(2,1)}), bf16[128,2,2048]{2,1,0:T(2,128)(2,1)}, u32[]{:S(2)}, u32[]{:S(2)}) async-start(bf16[128,2,2048]{2,1,0:T(2,128)(2,1)} %reshape.104), calls=%async_computation | async-start | bytes 2097152 | tf_op jit(solution)/shard_map/all_to_all | solution.py:10
  75.4 1.5 reshape.107
  78.3 1.5 fusion.6
  79.7 26.4 %all-to-all-done = bf16[128,2,2048]{2,1,0:T(2,128)(2,1)} async-done(((bf16[128,2,2048]{2,1,0:T(2,128)(2,1)}), bf16[128,2,2048]{2,1,0:T(2,128)(2,1)}, u32[]{:S(2)}, u32[]{:S(2)}) %all-to-all-start) | async-done | bytes 1048608 | tf_op jit(solution)/shard_map/all_to_all | solution.py:10
  106.2 2.2 %reshape.105 = bf16[256,2048]{1,0:T(8,128)(2,1)} reshape(bf16[128,2,2048]{2,1,0:T(2,128)(2,1)} %all-to-all-done) | data formatting | bytes 2097152 | tf_op jit(solution)/shard_map/reshape | solution.py:46
  108.4 3.3 %multiply_reduce_fusion = (bf16[256]{0:T(256)(128)(2,1)S(1)}, bf16[256,384]{1,0:T(8,128)(2,1)}, bf16[256,384]{1,0:T(8,128)(2,1)S(1)}, bf16[256,384]{1,0:T(8,128)(2,1)S(1)}) fusion(f32[256,384]{1,0:T(8,128)} %fusion.6, f32[256,384]{1,0:T(8,128)S(1)} %fusion.3, bf16[256,2048]{1,0:T(8,128)(2,1)} %reshape.105, bf16[1,384,2048]{2,1,0:T(8,128)(2,1)} %param.13), kind=kOutput, calls=%fused_computation.21 | convolution fusion | flops 404422400 | bytes 3998208 | tf_op jit(solution)/shard_map/dot_general | solution.py:14
  111.7 2.7 %convolution_convert_fusion = bf16[2048,768]{1,0:T(8,128)(2,1)} fusion(bf16[256,2048]{1,0:T(8,128)(2,1)S(1)} %reshape.107, bf16[256,384]{1,0:T(8,128)(2,1)S(1)} %get-tuple-element.8, bf16[256,384]{1,0:T(8,128)(2,1)S(1)} %get-tuple-element.7), kind=kOutput, calls=%fused_computation | convolution fusion | flops 807665664 | bytes 4587520 | tf_op jit(solution)/shard_map/dot_general | solution.py:14
  115.2 5.3 %all-to-all-start.3 = ((bf16[128,1,2]{2,1,0:T(2,128)(2,1)}), bf16[128,1,2]{2,1,0:T(2,128)(2,1)S(1)}, u32[]{:S(2)}, u32[]{:S(2)}) async-start(bf16[128,1,2]{2,1,0:T(2,128)(2,1)} %convert_element_type.78), calls=%async_computation.3 | async-start | bytes 131072 | tf_op jit(solution)/shard_map/all_to_all | solution.py:10
  120.7 1.8 convolution_convert_fusion.1
  123.2 0.9 copy-done.2
  124.9 1.5 reshape.108
  126.4 5.1 %all-to-all-done.3 = bf16[128,1,2]{2,1,0:T(2,128)(2,1)S(1)} async-done(((bf16[128,1,2]{2,1,0:T(2,128)(2,1)}), bf16[128,1,2]{2,1,0:T(2,128)(2,1)S(1)}, u32[]{:S(2)}, u32[]{:S(2)}) %all-to-all-start.3) | async-done | bytes 544 | tf_op jit(solution)/shard_map/all_to_all | solution.py:10
  131.5 8.3 %all-to-all-start.2 = ((bf16[128,2,2048]{2,1,0:T(2,128)(2,1)}), bf16[128,2,2048]{2,1,0:T(2,128)(2,1)S(1)}, u32[]{:S(2)}, u32[]{:S(2)}) async-start(bf16[128,2,2048]{2,1,0:T(2,128)(2,1)} %reshape.108), calls=%async_computation.2 | async-start | bytes 2097152 | tf_op jit(solution)/shard_map/all_to_all | solution.py:10
  141.1 30.7 %all-to-all-done.2 = bf16[128,2,2048]{2,1,0:T(2,128)(2,1)S(1)} async-done(((bf16[128,2,2048]{2,1,0:T(2,128)(2,1)}), bf16[128,2,2048]{2,1,0:T(2,128)(2,1)S(1)}, u32[]{:S(2)}, u32[]{:S(2)}) %all-to-all-start.2) | async-done | bytes 1048608 | tf_op jit(solution)/shard_map/all_to_all | solution.py:10
  171.8 1.2 reshape.109
  173.1 2.1 convolution_convert_fusion.4
  175.2 1.8 slice_bitcast_fusion
  177.0 27.7 %reduce-scatter.5.cloned.1.call-done = bf16[48,2048]{1,0:T(8,128)(2,1)} async-done(((bf16[384,2048]{1,0:T(8,128)(2,1)}), bf16[48,2048]{1,0:T(8,128)(2,1)}) %reduce-scatter.5.cloned.1.call-update) | async-done | bytes 196624 | tf_op jit(solution)/shard_map/reduce_scatter | solution.py:63
  (36 shorter events, 6.9 us)
Async XLA Ops:
  7.2 69.7 %copy-start = (bf16[1,2048,384]{2,1,0:T(8,128)(2,1)S(1)}, bf16[1,2048,384]{2,1,0:T(8,128)(2,1)}, u32[]{:S(2)}) copy-start(bf16[1,2048,384]{2,1,0:T(8,128)(2,1)} %param.11) | copy-start | bytes 4718596
  11.4 25.4 %copy-start.7 = (bf16[16,8]{0,1:T(8,128)(2,1)S(1)}, bf16[16,8]{0,1:T(8,128)(2,1)}, u32[]{:S(2)}) copy-start(bf16[16,8]{0,1:T(8,128)(2,1)} %param.10) | copy-start | bytes 772
  11.4 25.6 %copy-start.6 = (bf16[16,2048]{1,0:T(8,128)(2,1)S(1)}, bf16[16,2048]{1,0:T(8,128)(2,1)}, u32[]{:S(2)}) copy-start(bf16[16,2048]{1,0:T(8,128)(2,1)} %param.8) | copy-start | bytes 196612
  11.4 57.4 %all-to-all-start.1 = ((bf16[128,2,2048]{2,1,0:T(2,128)(2,1)}), bf16[128,2,2048]{2,1,0:T(2,128)(2,1)S(1)}, u32[]{:S(2)}, u32[]{:S(2)}) async-start(bf16[128,2,2048]{2,1,0:T(2,128)(2,1)} %reshape.106), calls=%async_computation.1 | async-start | bytes 2097152 | tf_op jit(solution)/shard_map/all_to_all | solution.py:10
  68.8 6.5 %copy-start.3 = (bf16[128,2,2048]{2,1,0:T(2,128)(2,1)}, bf16[128,2,2048]{2,1,0:T(2,128)(2,1)S(1)}, u32[]{:S(2)}) copy-start(bf16[128,2,2048]{2,1,0:T(2,128)(2,1)S(1)} %all-to-all-done.1) | copy-start | bytes 3145732
  68.8 37.3 %all-to-all-start = ((bf16[128,2,2048]{2,1,0:T(2,128)(2,1)}), bf16[128,2,2048]{2,1,0:T(2,128)(2,1)}, u32[]{:S(2)}, u32[]{:S(2)}) async-start(bf16[128,2,2048]{2,1,0:T(2,128)(2,1)} %reshape.104), calls=%async_computation | async-start | bytes 2097152 | tf_op jit(solution)/shard_map/all_to_all | solution.py:10
  75.3 99.9 %reduce-scatter.3.cloned.1.call-start = ((), (), s32[]{:S(2)}) async-start(), calls=%async_computation.6 | async-start | bytes 3538944 | tf_op jit(solution)/shard_map/reduce_scatter | solution.py:63
  76.8 1.4 copy-start.1
  114.3 6.3 %copy-start.4 = (bf16[256,2048]{1,0:T(8,128)(2,1)S(1)}, bf16[256,2048]{1,0:T(8,128)(2,1)}, u32[]{:S(2)}) copy-start(bf16[256,2048]{1,0:T(8,128)(2,1)} %reshape.105) | copy-start | bytes 3145732
  114.3 6.4 %copy-start.5 = (bf16[256,384]{1,0:T(8,128)(2,1)S(1)}, bf16[256,384]{1,0:T(8,128)(2,1)}, u32[]{:S(2)}) copy-start(bf16[256,384]{1,0:T(8,128)(2,1)} %get-tuple-element.6) | copy-start | bytes 589828
  115.2 16.4 %all-to-all-start.3 = ((bf16[128,1,2]{2,1,0:T(2,128)(2,1)}), bf16[128,1,2]{2,1,0:T(2,128)(2,1)S(1)}, u32[]{:S(2)}, u32[]{:S(2)}) async-start(bf16[128,1,2]{2,1,0:T(2,128)(2,1)} %convert_element_type.78), calls=%async_computation.3 | async-start | bytes 131072 | tf_op jit(solution)/shard_map/all_to_all | solution.py:10
  120.4 84.2 %reduce-scatter.5.cloned.1.call-start = ((), (), s32[]{:S(2)}) async-start(), calls=%async_computation.7 | async-start | bytes 1769472 | tf_op jit(solution)/shard_map/reduce_scatter | solution.py:63
  122.5 1.6 copy-start.2
  131.5 40.3 %all-to-all-start.2 = ((bf16[128,2,2048]{2,1,0:T(2,128)(2,1)}), bf16[128,2,2048]{2,1,0:T(2,128)(2,1)S(1)}, u32[]{:S(2)}, u32[]{:S(2)}) async-start(bf16[128,2,2048]{2,1,0:T(2,128)(2,1)} %reshape.108), calls=%async_computation.2 | async-start | bytes 2097152 | tf_op jit(solution)/shard_map/all_to_all | solution.py:10
Sparse Core Ops, SparseCore 0:
  114.5 41.3 reduce-scatter.2
  159.9 44.7 reduce-scatter.4

commit v2 on v1

v2 whole, which is shorter than its diff:
```python
import jax
import jax.numpy as jnp
from jax import lax
from jax.experimental import pallas as pl
from jax.experimental.pallas import tpu as pltpu
from jax.sharding import PartitionSpec as P

PLANE = ("node", "local")
BF16, F32, I32 = jnp.bfloat16, jnp.float32, jnp.int32
VMEM_LIMIT = 48 << 20
CAP, PIECES, WIDE = 2, 8, 256
BLOCK = CAP * PIECES
GROUP = 16
GROUP_SLOTS = GROUP * CAP
LANES = 128


def iota(shape, dim):
    return lax.broadcasted_iota(I32, shape, dim)


def dot(left, right, left_dim, right_dim):
    return lax.dot_general(
        left, right, (((left_dim,), (right_dim,)), ((), ())), preferred_element_type=F32
    )


def whole(count):
    return [pl.BlockSpec(memory_space=pltpu.VMEM)] * count


def call(body, outs, in_specs, out_specs, scratch=(), cost=None):
    return pl.pallas_call(
        body,
        out_shape=outs,
        in_specs=in_specs,
        out_specs=out_specs,
        scratch_shapes=scratch,
        cost_estimate=cost,
        compiler_params=pltpu.CompilerParams(vmem_limit_bytes=VMEM_LIMIT),
    )


def route_body(ids_ref, gates_ref, tokens_ref, grads_ref, out_ref, spread_ref):
    top, tok = ids_ref.shape
    slots = spread_ref.shape[0]
    ids = jnp.concatenate([ids_ref[...]] * (LANES // tok), axis=1)
    weights = jnp.concatenate([gates_ref[...].astype(F32)] * (LANES // tok), axis=1)
    expert = iota((slots, LANES), 0) // CAP
    named = jnp.zeros((slots, LANES), F32)
    weight = jnp.zeros((slots, LANES), F32)
    for k in range(top):
        hit = expert == ids[k : k + 1]
        named = named + jnp.where(hit, 1.0, 0.0)
        weight = weight + jnp.where(hit, weights[k : k + 1], 0.0)
    before, after = iota((LANES, LANES), 0), iota((LANES, LANES), 1)
    earlier = (before // tok == after // tok) & (before < after)
    rank = dot(named.astype(BF16), jnp.where(earlier, 1.0, 0.0).astype(BF16), 1, 0)
    mine = rank == (iota((slots, LANES), 0) % CAP).astype(F32)
    spread = jnp.where(mine, named, 0.0).astype(BF16)
    weighted = jnp.where(mine, weight, 0.0).astype(BF16)
    spread_ref[...] = spread
    rows = GROUP * BLOCK
    row = iota((rows, GROUP_SLOTS), 0)
    expand = (row // BLOCK) * CAP + row % CAP == iota((rows, GROUP_SLOTS), 1)
    expand = jnp.where(expand, 1.0, 0.0).astype(BF16)
    piece = (iota((rows, LANES), 0) % BLOCK) // CAP == iota((rows, LANES), 1) // tok
    for part, (chosen, ref) in enumerate(((spread, tokens_ref), (weighted, grads_ref))):
        pieces = [ref[:, j * WIDE : (j + 1) * WIDE] for j in range(PIECES)]
        source = jnp.concatenate(pieces, axis=0)
        for g in range(slots // GROUP_SLOTS):
            picked = chosen[g * GROUP_SLOTS : (g + 1) * GROUP_SLOTS]
            select = jnp.where(piece, dot(expand, picked, 1, 0), 0.0).astype(BF16)
            block = dot(select, source, 1, 0).astype(BF16)
            out_ref[g * GROUP : (g + 1) * GROUP, part * BLOCK : (part + 1) * BLOCK, :] = (
                block.reshape(GROUP, BLOCK, WIDE)
            )


def expert_body(
    arrived_ref, gate_hbm, up_hbm, down_hbm,
    partial_hbm, slopes_ref, score_ref,
    rows_ref, w_gate, w_up, w_down, packed, load_sems, store_sems,
):
    loads = [
        pltpu.make_async_copy(source, target, load_sems.at[i])
        for i, (source, target) in enumerate(
            ((gate_hbm, w_gate), (up_hbm, w_up), (down_hbm, w_down))
        )
    ]
    for load in loads:
        load.start()
    slots = rows_ref.shape[1]
    hidden = w_gate.shape[1]
    order = iota((GROUP * BLOCK, GROUP * BLOCK), 0)
    wanted = (order // CAP % GROUP) * BLOCK + (order // GROUP_SLOTS) * CAP + order % CAP
    shuffle = jnp.where(wanted == iota(order.shape, 1), 1.0, 0.0).astype(BF16)
    for part in range(2):
        for g in range(slots // GROUP_SLOTS):
            block = arrived_ref[g * GROUP : (g + 1) * GROUP, part * BLOCK : (part + 1) * BLOCK, :]
            block = dot(shuffle, block.reshape(GROUP * BLOCK, WIDE), 1, 0).astype(BF16)
            for j in range(PIECES):
                rows_ref[
                    part, g * GROUP_SLOTS : (g + 1) * GROUP_SLOTS, j * WIDE : (j + 1) * WIDE
                ] = block[j * GROUP_SLOTS : (j + 1) * GROUP_SLOTS]
    loads[0].wait()
    gate_pre = dot(rows_ref[0], w_gate[...], 1, 0)
    loads[1].wait()
    up_pre = dot(rows_ref[0], w_up[...], 1, 0)
    loads[2].wait()
    grad_act = dot(rows_ref[1], w_down[...], 1, 1)
    sigmoid_gate = 1.0 / (1.0 + jnp.exp(-gate_pre))
    silu_gate = gate_pre * sigmoid_gate
    hidden_act = (silu_gate * up_pre).astype(BF16)
    slope = up_pre * sigmoid_gate * (1.0 + gate_pre * (1.0 - sigmoid_gate))
    slopes_ref[:, :hidden] = (grad_act * slope).astype(BF16)
    slopes_ref[:, hidden:] = (grad_act * silu_gate).astype(BF16)
    score = jnp.sum(hidden_act.astype(F32) * grad_act, axis=1, keepdims=True)
    score_ref[...] = jnp.broadcast_to(score, score_ref.shape).astype(BF16)

    shards = packed.shape[0]
    share = hidden // shards
    gate_up_rows = 2 * hidden // LANES * WIDE
    for n in range(PIECES):
        down = dot(hidden_act, rows_ref[1, :, n * WIDE : (n + 1) * WIDE], 0, 0).astype(BF16)
        for s in range(shards):
            for b in range(WIDE // LANES):
                at = gate_up_rows + (n * (WIDE // LANES) + b) * share
                packed[s, at : at + share, :] = down[
                    s * share : (s + 1) * share, b * LANES : (b + 1) * LANES
                ]
    stores = []
    for s in range(shards):
        columns = slice(s * WIDE, (s + 1) * WIDE)
        gate_up = dot(rows_ref[0, :, columns], slopes_ref[...], 0, 0).astype(BF16)
        for b in range(2 * hidden // LANES):
            packed[s, b * WIDE : (b + 1) * WIDE, :] = gate_up[:, b * LANES : (b + 1) * LANES]
        store = pltpu.make_async_copy(packed.at[s], partial_hbm.at[s], store_sems.at[s])
        store.start()
        stores.append(store)
    for store in stores:
        store.wait()


def rows_body(slopes_ref, score_ref, gate_ref, up_ref, out_ref):
    hidden = gate_ref.shape[1]
    width = gate_ref.shape[0]
    for j in range(width // WIDE):
        columns = slice(j * WIDE, (j + 1) * WIDE)
        rows = dot(slopes_ref[:, :hidden], gate_ref[columns, :], 1, 1)
        rows = rows + dot(slopes_ref[:, hidden:], up_ref[columns, :], 1, 1)
        out_ref[:, columns] = rows.astype(BF16)
    out_ref[:, width:] = score_ref[...]


def combine_body(returned_ref, spread_ref, ids_ref, gates_ref, tokens_ref, out_gates_ref):
    top, tok = ids_ref.shape
    width = tokens_ref.shape[1]
    slots = spread_ref.shape[0]
    spread = spread_ref[:, :tok]
    for j in range(width // WIDE):
        columns = slice(j * WIDE, (j + 1) * WIDE)
        tokens_ref[:, columns] = dot(spread, returned_ref[:, columns], 0, 0).astype(BF16)
    score = returned_ref[:, width : width + tok].astype(F32) * spread.astype(F32)
    expert = iota((slots, tok), 0) // CAP
    gates = gates_ref[...].astype(F32)
    sums = [
        jnp.sum(jnp.where(expert == ids_ref[k : k + 1, :], score, 0.0), axis=0, keepdims=True)
        for k in range(top)
    ]
    out_gates_ref[...] = (jnp.concatenate(sums, axis=0) / gates).astype(BF16)


def unpack_body(sums_ref, gate_ref, up_ref, down_ref):
    hidden = gate_ref.shape[1]
    share = down_ref.shape[0]
    blocks = hidden // LANES
    for b in range(blocks):
        columns = slice(b * LANES, (b + 1) * LANES)
        gate_ref[:, columns] = sums_ref[b * WIDE : (b + 1) * WIDE, :]
        up_ref[:, columns] = sums_ref[(blocks + b) * WIDE : (blocks + b + 1) * WIDE, :]
    for b in range(down_ref.shape[1] // LANES):
        at = 2 * blocks * WIDE + b * share
        down_ref[:, b * LANES : (b + 1) * LANES] = sums_ref[at : at + share, :]


def shaped(*shape, dtype=BF16):
    return jax.ShapeDtypeStruct(shape, dtype)


def cost(flops, bytes_accessed):
    return pl.CostEstimate(flops=flops, bytes_accessed=bytes_accessed, transcendentals=0)


def exchange(blocks):
    return lax.all_to_all(blocks, PLANE, split_axis=0, concat_axis=0, tiled=True)


def shards(tokens, grads_out, expert_ids, gates, w_gate, w_up, w_down):
    experts = lax.axis_size("node") * lax.axis_size("local")
    reps = lax.axis_size("rep")
    tok, top = expert_ids.shape
    width = tokens.shape[1]
    hidden = w_gate.shape[2]
    slots = experts * CAP
    w_gate, w_up, w_down = w_gate[0], w_up[0], w_down[0]
    ids_t, gates_t = expert_ids.T, gates.T
    packed_rows = (2 * hidden * (width // reps) + (hidden // reps) * width) // LANES
    product = 2 * slots * width * hidden

    outgoing, spread = call(
        route_body,
        (shaped(experts, 2 * BLOCK, WIDE), shaped(slots, LANES)),
        whole(4),
        whole(2),
        cost=cost(4 * slots * LANES * width, 4 * slots * width),
    )(ids_t, gates_t, tokens, grads_out)
    arrived = exchange(outgoing)

    hbm = pl.BlockSpec(memory_space=pl.ANY)
    partial, slopes, score = call(
        expert_body,
        (
            shaped(reps, packed_rows, LANES),
            shaped(slots, 2 * hidden),
            shaped(slots, LANES),
        ),
        whole(1) + [hbm] * 3,
        [hbm] + whole(2),
        scratch=(
            pltpu.VMEM((2, slots, width), BF16),
            pltpu.VMEM((width, hidden), BF16),
            pltpu.VMEM((width, hidden), BF16),
            pltpu.VMEM((hidden, width), BF16),
            pltpu.VMEM((reps, packed_rows, LANES), BF16),
            pltpu.SemaphoreType.DMA((3,)),
            pltpu.SemaphoreType.DMA((reps,)),
        ),
        cost=cost(6 * product, 12 << 20),
    )(arrived, w_gate, w_up, w_down)

    sums = lax.psum_scatter(
        partial.reshape(reps * packed_rows, LANES), "rep", scatter_dimension=0, tiled=True
    )

    rows = call(
        rows_body,
        shaped(slots, width + LANES),
        whole(4),
        whole(1)[0],
        cost=cost(2 * product, 5 << 20),
    )(slopes, score, w_gate, w_up)
    returned = exchange(rows.reshape(experts, CAP, width + LANES)).reshape(slots, width + LANES)
    grad_tokens, grad_gates = call(
        combine_body,
        (shaped(tok, width), shaped(top, tok)),
        whole(4),
        whole(2),
        cost=cost(2 * slots * tok * width, 2 << 20),
    )(returned, spread, ids_t, gates_t)

    grad_w_gate, grad_w_up, grad_w_down = call(
        unpack_body,
        (
            shaped(width // reps, hidden),
            shaped(width // reps, hidden),
            shaped(hidden // reps, width),
        ),
        whole(1),
        whole(3),
        cost=cost(0, 2 << 20),
    )(sums)
    return (
        grad_tokens,
        grad_gates.T,
        grad_w_gate[None],
        grad_w_up[None],
        grad_w_down[None],
    )


def solution(mesh):
    rows = P(("rep", "node", "local"), None)
    weights = P(PLANE, None, None)
    sharded = P(PLANE, "rep", None)
    return jax.shard_map(
        shards,
        mesh=mesh,
        in_specs=(rows, rows, rows, rows, weights, weights, weights),
        out_specs=(rows, rows, sharded, sharded, sharded),
        check_vma=False,
    )
```

time: 215 us -> 166 us (0.77); the launches traced: 211 us -> 166 us
  blocking collectives: 0 us -> 118 us
  waiting for transfers between devices: 118 us -> 14.1 us
  starting transfers between devices: 45.6 us -> 0.04 us
  matrix products: 17.1 us -> 0 us
  Pallas kernels: 0 us -> 12.7 us
  local copies, waits for them, and re-layouts: 16.1 us -> 6.68 us
    all_to_all x0 -> x2, blocking collectives: none -> 118 us  [exchange(): lax.all_to_all(blocks, PLANE, split_axis=0, concat_axis=0, tiled=True)]
    all_to_all x4 -> x0, waiting for transfers between devices: 89.9 us -> none  [exchange(): lax.all_to_all(blocks, PLANE, split_axis=0, concat_axis=0, tiled=True)]
    all_to_all x4 -> x0, starting transfers between devices: 45.4 us -> none  [exchange(): lax.all_to_all(blocks, PLANE, split_axis=0, concat_axis=0, tiled=True)]
    dot_general x12 -> x0, matrix products: 17.1 us -> none  [dot(): lax.dot_general(left, right, (((left_dim,), (right_dim,)), ((), ())), pre...]
    reduce_scatter x2 -> x1, waiting for transfers between devices: 27.7 us -> 14.1 us  [shards(): lax.psum_scatter(partial.reshape(reps * packed_rows, LANES), 'rep', scatt...]
    pallas_call x0 -> x5, Pallas kernels: none -> 12.7 us  [the longest x1 7.58 us: shards(): call(expert_body, (shaped(reps, packed_rows, LANES), shaped(slots, 2 * hi...]
    reshape x8 -> x2, local copies, waits for them, and re-layouts: 10.7 us -> 0.91 us  [the longest x1 0.47 us: shards(): rows.reshape(experts, CAP, width + LANES)]
    unnamed x18 -> x22, local copies, waits for them, and re-layouts: 2.57 us -> 5.77 us
  transfers between devices with their start and end apart: 6 -> 1, of which waited for: 5 -> 1; matrix products, arithmetic and copies ran while one was open for 10% -> 1% of each run, Pallas kernels for 0% -> 1%
where the time goes in v2:
time: 166 us
  blocking collectives  118 us (71%)
  waiting for transfers between devices  14.1 us (8%)
  between operations  14.1 us (8%)
  Pallas kernels  12.7 us (8%)
  local copies, waits for them, and re-layouts  6.68 us (4%)
    all_to_all x2, blocking collectives, exchange(): lax.all_to_all(blocks, PLANE, split_axis=0, concat_axis=0, tiled=True)  118 us
    reduce_scatter x1, waiting for transfers between devices, shards(): lax.psum_scatter(partial.reshape(reps * packed_rows, LANES), 'rep', scatt...  14.1 us
    pallas_call x1, Pallas kernels, shards(): call(expert_body, (shaped(reps, packed_rows, LANES), shaped(slots, 2 * hi...  7.58 us
    unnamed x22, local copies, waits for them, and re-layouts  5.77 us
  transfers between devices with their start and end apart: 1, of which 1 were waited for; matrix products, arithmetic and copies ran while one was open for 1% of the time, Pallas kernels for 1%

profile of v2, /device:TPU:1, one launch (start us, length us, event | category | flops | bytes accessed | tf_op | source)
XLA Modules:
  0.0 165.9 jit_solution(4795884428833269685)
XLA Ops:
  7.2 0.0 reduce-scatter.2.cloned.1.call-start
  7.2 0.0 copy-start.4
  7.2 0.7 copy-done.4
  7.9 0.7 copy-done.6
  8.6 0.8 copy-done.9
  9.4 0.8 copy-done.10
  10.3 1.9 %shard_map.110 = (bf16[128,32,256]{2,1,0:T(8,128)(2,1)S(1)}, bf16[256,128]{1,0:T(8,128)(2,1)S(1)}) custom-call(s32[8,16]{1,0:T(8,128)S(1)} %bitcast.14, bf16[8,16]{1,0:T(8,128)(2,1)S(1)} %bitcast.16, bf16[16,2048]{1,0:T(8,128)(2,1)S(1)} %copy-done.9, bf16[16,2048]{1,0:T(8,128)(2,1)S(1)} %copy-done.10), custom_call_target="tpu_custom_call" | custom-call | flops 268435456 | bytes 2097152 | tf_op jit(solution)/shard_map/pallas_call | solution.py:211
  12.2 0.0 copy-start
  12.2 0.0 copy-start.1
  12.2 79.6 %all_to_all.10.arrived_ref = bf16[128,32,256]{2,1,0:T(8,128)(2,1)} all-to-all(bf16[128,32,256]{2,1,0:T(8,128)(2,1)S(1)} %get-tuple-element.15), channel_id=1, replica_groups=mesh['rep'=8,'node'=16,'local'=8] {'node','local'}, dimensions={0} | all-to-all | bytes 4194304 | tf_op jit(solution)/shard_map/all_to_all | solution.py:196
  91.8 7.6 %shard_map.111 = (bf16[8,2304,128]{2,1,0:T(8,128)(2,1)}, bf16[256,768]{1,0:T(8,128)(2,1)S(1)}, bf16[256,128]{1,0:T(8,128)(2,1)S(1)}) custom-call(bf16[128,32,256]{2,1,0:T(8,128)(2,1)} %all_to_all.10.arrived_ref, bf16[2048,384]{1,0:T(8,128)(2,1)S(1)} %bitcast.10, bf16[2048,384]{1,0:T(8,128)(2,1)S(1)} %bitcast.12, bf16[384,2048]{1,0:T(8,128)(2,1)S(1)} %bitcast.18), custom_call_target="tpu_custom_call" | custom-call | flops 2415919104 | bytes 12582912 | tf_op jit(solution)/shard_map/pallas_call | solution.py:221
  99.4 0.0 reduce-scatter.2.cloned.1.call-update
  99.5 0.0 copy-start.2
  99.5 1.4 copy-done.2
  100.9 1.3 shard_map.112
  102.2 0.5 reshape.19
  102.6 38.7 %all_to_all.11 = bf16[128,2,2176]{2,1,0:T(2,128)(2,1)S(1)} all-to-all(bf16[128,2,2176]{2,1,0:T(2,128)(2,1)S(1)} %reshape.19), channel_id=1, replica_groups=mesh['rep'=8,'node'=16,'local'=8] {'node','local'}, dimensions={0} | all-to-all | bytes 2228224 | tf_op jit(solution)/shard_map/all_to_all | solution.py:196
  141.4 0.4 reshape.20.returned_ref
  141.8 0.2 copy-done.5
  142.0 0.0 copy-done.7
  142.1 1.0 shard_map.113
  143.0 14.1 %reduce-scatter.2.cloned.1.call-done.sums_ref = bf16[2304,128]{1,0:T(8,128)(2,1)} async-done(((bf16[18432,128]{1,0:T(8,128)(2,1)}), bf16[2304,128]{1,0:T(8,128)(2,1)}) %reduce-scatter.2.cloned.1.call-update) | async-done | bytes 589840 | tf_op jit(solution)/shard_map/reduce_scatter | solution.py:242
  157.1 1.1 copy-done.3
  158.2 0.9 shard_map.114
  (10 shorter events, 0.0 us)
Async XLA Ops:
  7.2 150.0 %reduce-scatter.2.cloned.1.call-start = ((), (), s32[]{:S(2)}) async-start(), calls=%async_computation.3 | async-start | bytes 5308416 | tf_op jit(solution)/shard_map/reduce_scatter | solution.py:242
  7.2 0.7 copy-start.4
  7.9 0.7 copy-start.6
  8.6 0.8 copy-start.9
  9.4 0.8 copy-start.10
  10.3 81.6 %copy-start.8 = (bf16[1,384,2048]{2,1,0:T(8,128)(2,1)S(1)}, bf16[1,384,2048]{2,1,0:T(8,128)(2,1)}, u32[]{:S(2)}) copy-start(bf16[1,384,2048]{2,1,0:T(8,128)(2,1)} %param.13) | copy-start | bytes 4718596
  12.2 79.6 %copy-start = (bf16[1,2048,384]{2,1,0:T(8,128)(2,1)S(1)}, bf16[1,2048,384]{2,1,0:T(8,128)(2,1)}, u32[]{:S(2)}) copy-start(bf16[1,2048,384]{2,1,0:T(8,128)(2,1)} %param.11) | copy-start | bytes 4718596
  12.2 79.6 %copy-start.1 = (bf16[1,2048,384]{2,1,0:T(8,128)(2,1)S(1)}, bf16[1,2048,384]{2,1,0:T(8,128)(2,1)}, u32[]{:S(2)}) copy-start(bf16[1,2048,384]{2,1,0:T(8,128)(2,1)} %param.12) | copy-start | bytes 4718596
  99.5 1.4 copy-start.2
  141.4 0.7 copy-start.5
  141.4 0.7 copy-start.7
  157.1 1.1 copy-start.3
Sparse Core Ops, SparseCore 0:
  99.6 57.5 reduce-scatter.1

commit v3 on v2

--- a/solution.py
+++ b/solution.py
@@ -41,8 +41,20 @@
     )
 
 
-def route_body(ids_ref, gates_ref, tokens_ref, grads_ref, out_ref, spread_ref):
+def route_body(
+    ids_hbm, gates_ref, tokens_hbm, grads_hbm, out_ref, spread_ref,
+    ids_ref, tokens_ref, grads_ref, sems,
+):
+    loads = [
+        pltpu.make_async_copy(source, target, sems.at[i])
+        for i, (source, target) in enumerate(
+            ((ids_hbm, ids_ref), (tokens_hbm, tokens_ref), (grads_hbm, grads_ref))
+        )
+    ]
+    for load in loads:
+        load.start()
     top, tok = ids_ref.shape
+    loads[0].wait()
     slots = spread_ref.shape[0]
     ids = jnp.concatenate([ids_ref[...]] * (LANES // tok), axis=1)
     weights = jnp.concatenate([gates_ref[...].astype(F32)] * (LANES // tok), axis=1)
@@ -66,6 +78,7 @@
     expand = jnp.where(expand, 1.0, 0.0).astype(BF16)
     piece = (iota((rows, LANES), 0) % BLOCK) // CAP == iota((rows, LANES), 1) // tok
     for part, (chosen, ref) in enumerate(((spread, tokens_ref), (weighted, grads_ref))):
+        loads[part + 1].wait()
         pieces = [ref[:, j * WIDE : (j + 1) * WIDE] for j in range(PIECES)]
         source = jnp.concatenate(pieces, axis=0)
         for g in range(slots // GROUP_SLOTS):
@@ -78,10 +91,10 @@
 
 
 def expert_body(
-    arrived_ref, gate_hbm, up_hbm, down_hbm,
-    partial_hbm, slopes_ref, score_ref,
-    rows_ref, w_gate, w_up, w_down, packed, load_sems, store_sems,
+    order_ref, arrived_ref, gate_hbm, up_hbm, down_hbm,
+    slopes_ref, score_ref, far_ahead, far_behind, *refs,
 ):
+    near, (rows_ref, w_gate, w_up, w_down, down_ref, load_sems) = refs[:-6], refs[-6:]
     loads = [
         pltpu.make_async_copy(source, target, load_sems.at[i])
         for i, (source, target) in enumerate(
@@ -118,28 +131,32 @@
     score = jnp.sum(hidden_act.astype(F32) * grad_act, axis=1, keepdims=True)
     score_ref[...] = jnp.broadcast_to(score, score_ref.shape).astype(BF16)
 
-    shards = packed.shape[0]
+    shards = order_ref.shape[0]
     share = hidden // shards
-    gate_up_rows = 2 * hidden // LANES * WIDE
     for n in range(PIECES):
-        down = dot(hidden_act, rows_ref[1, :, n * WIDE : (n + 1) * WIDE], 0, 0).astype(BF16)
-        for s in range(shards):
-            for b in range(WIDE // LANES):
-                at = gate_up_rows + (n * (WIDE // LANES) + b) * share
-                packed[s, at : at + share, :] = down[
-                    s * share : (s + 1) * share, b * LANES : (b + 1) * LANES
-                ]
-    stores = []
-    for s in range(shards):
-        columns = slice(s * WIDE, (s + 1) * WIDE)
+        columns = slice(n * WIDE, (n + 1) * WIDE)
+        down_ref[:, columns] = dot(hidden_act, rows_ref[1, :, columns], 0, 0).astype(BF16)
+    far = shards // 2
+    for offset in (far, *range(far), *range(far + 1, shards)):
+        target = order_ref[offset]
+        columns = pl.ds(pl.multiple_of(target * WIDE, WIDE), WIDE)
         gate_up = dot(rows_ref[0, :, columns], slopes_ref[...], 0, 0).astype(BF16)
-        for b in range(2 * hidden // LANES):
-            packed[s, b * WIDE : (b + 1) * WIDE, :] = gate_up[:, b * LANES : (b + 1) * LANES]
-        store = pltpu.make_async_copy(packed.at[s], partial_hbm.at[s], store_sems.at[s])
-        store.start()
-        stores.append(store)
-    for store in stores:
-        store.wait()
+        down = down_ref[pl.ds(pl.multiple_of(target * share, 16), share), :]
+        pieces = [gate_up[:, b * LANES : (b + 1) * LANES] for b in range(2 * hidden // LANES)]
+        pieces += [down[:, b * LANES : (b + 1) * LANES] for b in range(down.shape[1] // LANES)]
+        at = 0
+        for piece in pieces:
+            rows = piece.shape[0]
+            if offset != far:
+                near[offset - (offset > far)][at : at + rows, :] = piece
+            else:
+                split = far_ahead.shape[0]
+                first = min(max(split - at, 0), rows)
+                if first:
+                    far_ahead[at : at + first, :] = piece[:first]
+                if first < rows:
+                    far_behind[at + first - split : at + rows - split, :] = piece[first:]
+            at += rows
 
 
 def rows_body(slopes_ref, score_ref, gate_ref, up_ref, out_ref):
@@ -171,17 +188,23 @@
     out_gates_ref[...] = (jnp.concatenate(sums, axis=0) / gates).astype(BF16)
 
 
-def unpack_body(sums_ref, gate_ref, up_ref, down_ref):
+def unpack_body(own_ref, ahead_ref, behind_ref, gate_ref, up_ref, down_ref):
     hidden = gate_ref.shape[1]
     share = down_ref.shape[0]
     blocks = hidden // LANES
+
+    def total(at, rows):
+        at = slice(at, at + rows)
+        parts = [ref[at, :].astype(F32) for ref in (own_ref, ahead_ref, behind_ref)]
+        return (parts[0] + parts[1] + parts[2]).astype(BF16)
+
     for b in range(blocks):
         columns = slice(b * LANES, (b + 1) * LANES)
-        gate_ref[:, columns] = sums_ref[b * WIDE : (b + 1) * WIDE, :]
-        up_ref[:, columns] = sums_ref[(blocks + b) * WIDE : (blocks + b + 1) * WIDE, :]
+        gate_ref[:, columns] = total(b * WIDE, WIDE)
+        up_ref[:, columns] = total((blocks + b) * WIDE, WIDE)
     for b in range(down_ref.shape[1] // LANES):
         at = 2 * blocks * WIDE + b * share
-        down_ref[:, b * LANES : (b + 1) * LANES] = sums_ref[at : at + share, :]
+        down_ref[:, b * LANES : (b + 1) * LANES] = total(at, share)
 
 
 def shaped(*shape, dtype=BF16):
@@ -194,6 +217,36 @@
 
 def exchange(blocks):
     return lax.all_to_all(blocks, PLANE, split_axis=0, concat_axis=0, tiled=True)
+
+
+def ring(phase):
+    reps, nodes = lax.axis_size("rep"), lax.axis_size("node")
+    pairs = []
+    for r in range(reps):
+        for n in range(nodes):
+            step = 1 if n % 2 == phase else -1
+            pairs.append((r * nodes + n, (r + step) % reps * nodes + n))
+    return lambda message: lax.ppermute(message, ("rep", "node"), pairs)
+
+
+def add(left, right):
+    return (left.astype(F32) + right.astype(F32)).astype(BF16)
+
+
+def reduce_scatter(far_ahead, far_behind, near):
+    forward, backward = ring(0), ring(1)
+    half = far_ahead.shape[0]
+    ahead, behind = forward(far_ahead), backward(far_behind)
+    last = len(near) // 2
+    for d in range(last, 0, -1):
+        to_ahead, to_behind = near[d], near[len(near) - d]
+        if d == last:
+            to_ahead = jnp.concatenate((add(to_ahead[:half], ahead), to_ahead[half:]))
+            to_behind = jnp.concatenate((to_behind[:half], add(to_behind[half:], behind)))
+        else:
+            to_ahead, to_behind = add(to_ahead, ahead), add(to_behind, behind)
+        ahead, behind = forward(to_ahead), backward(to_behind)
+    return near[0], ahead, behind
 
 
 def shards(tokens, grads_out, expert_ids, gates, w_gate, w_up, w_down):
@@ -208,40 +261,46 @@
     packed_rows = (2 * hidden * (width // reps) + (hidden // reps) * width) // LANES
     product = 2 * slots * width * hidden
 
+    hbm = pl.BlockSpec(memory_space=pl.ANY)
     outgoing, spread = call(
         route_body,
         (shaped(experts, 2 * BLOCK, WIDE), shaped(slots, LANES)),
-        whole(4),
+        [hbm] + whole(1) + [hbm] * 2,
         whole(2),
+        scratch=(
+            pltpu.VMEM((top, tok), I32),
+            pltpu.VMEM((tok, width), BF16),
+            pltpu.VMEM((tok, width), BF16),
+            pltpu.SemaphoreType.DMA((3,)),
+        ),
         cost=cost(4 * slots * LANES * width, 4 * slots * width),
     )(ids_t, gates_t, tokens, grads_out)
     arrived = exchange(outgoing)
 
-    hbm = pl.BlockSpec(memory_space=pl.ANY)
-    partial, slopes, score = call(
+    direction = 1 - 2 * (lax.axis_index("node") % 2)
+    order = (lax.axis_index("rep") + direction * lax.iota(I32, reps) + reps) % reps
+    slopes, score, far_ahead, far_behind, *near = call(
         expert_body,
         (
-            shaped(reps, packed_rows, LANES),
             shaped(slots, 2 * hidden),
             shaped(slots, LANES),
+            *[shaped(packed_rows // 2, LANES)] * 2,
+            *[shaped(packed_rows, LANES)] * (reps - 1),
         ),
-        whole(1) + [hbm] * 3,
-        [hbm] + whole(2),
+        [pl.BlockSpec(memory_space=pltpu.SMEM)] + whole(1) + [hbm] * 3,
+        whole(4 + reps - 1),
         scratch=(
             pltpu.VMEM((2, slots, width), BF16),
             pltpu.VMEM((width, hidden), BF16),
             pltpu.VMEM((width, hidden), BF16),
             pltpu.VMEM((hidden, width), BF16),
-            pltpu.VMEM((reps, packed_rows, LANES), BF16),
+            pltpu.VMEM((hidden, width), BF16),
             pltpu.SemaphoreType.DMA((3,)),
-            pltpu.SemaphoreType.DMA((reps,)),
         ),
         cost=cost(6 * product, 12 << 20),
-    )(arrived, w_gate, w_up, w_down)
-
-    sums = lax.psum_scatter(
-        partial.reshape(reps * packed_rows, LANES), "rep", scatter_dimension=0, tiled=True
-    )
+    )(order, arrived, w_gate, w_up, w_down)
+
+    sums = reduce_scatter(far_ahead, far_behind, near)
 
     rows = call(
         rows_body,
@@ -266,10 +325,10 @@
             shaped(width // reps, hidden),
             shaped(hidden // reps, width),
         ),
-        whole(1),
+        whole(3),
         whole(3),
         cost=cost(0, 2 << 20),
-    )(sums)
+    )(*sums)
     return (
         grad_tokens,
         grad_gates.T,

time: 166 us -> 172 us (1.036)
  blocking collectives: 118 us -> 0 us
  waiting for transfers between devices: 14.1 us -> 86.2 us
  starting transfers between devices: 0.04 us -> 59.6 us
  between operations: 14.1 us -> 0.97 us
  other arithmetic: 0 us -> 2.85 us
  Pallas kernels: 12.7 us -> 14.5 us
    all_to_all x2 -> x0, blocking collectives: 118 us -> none  [exchange(): lax.all_to_all(blocks, PLANE, split_axis=0, concat_axis=0, tiled=True)]
    all_to_all x0 -> x2, waiting for transfers between devices: none -> 53.8 us  [exchange(): lax.all_to_all(blocks, PLANE, split_axis=0, concat_axis=0, tiled=True)]
    ppermute x0 -> x8, waiting for transfers between devices: none -> 32.4 us  [ring(): return lambda message: lax.ppermute(message, ('rep', 'node'), pairs)]
    all_to_all x0 -> x2, starting transfers between devices: none -> 32.2 us  [exchange(): lax.all_to_all(blocks, PLANE, split_axis=0, concat_axis=0, tiled=True)]
    ppermute x0 -> x8, starting transfers between devices: none -> 27.4 us  [ring(): return lambda message: lax.ppermute(message, ('rep', 'node'), pairs)]
    reduce_scatter x1 -> x0, waiting for transfers between devices: 14.1 us -> none  [shards(): lax.psum_scatter(partial.reshape(reps * packed_rows, LANES), 'rep', scatt...]
    convert_element_type x0 -> x6, other arithmetic: none -> 2.76 us  [add(): return (left.astype(F32) + right.astype(F32)).astype(BF16)]
    unnamed x22 -> x32, local copies, waits for them, and re-layouts: 5.77 us -> 3.09 us
  transfers between devices with their start and end apart: 1 -> 10, of which waited for: 1 -> 7; matrix products, arithmetic and copies ran while one was open for 1% -> 3% of each run, Pallas kernels for 1% -> 1%
where the time goes in v3:
time: 172 us; the launch traced here: 171 us
  waiting for transfers between devices  86.2 us (50%)
  starting transfers between devices  59.6 us (35%)
  Pallas kernels  14.5 us (8%)
  local copies, waits for them, and re-layouts  7.33 us (4%)
  other arithmetic  2.85 us (2%)
    all_to_all x2, waiting for transfers between devices, exchange(): lax.all_to_all(blocks, PLANE, split_axis=0, concat_axis=0, tiled=True)  53.8 us
    ppermute x8, waiting for transfers between devices, ring(): return lambda message: lax.ppermute(message, ('rep', 'node'), pairs)  32.4 us
    all_to_all x2, starting transfers between devices, exchange(): lax.all_to_all(blocks, PLANE, split_axis=0, concat_axis=0, tiled=True)  32.2 us
    ppermute x8, starting transfers between devices, ring(): return lambda message: lax.ppermute(message, ('rep', 'node'), pairs)  27.4 us
    pallas_call x1, Pallas kernels, shards(): call(expert_body, (shaped(slots, 2 * hidden), shaped(slots, LANES), *[sha...  7.57 us
    pallas_call x1, Pallas kernels, shards(): call(route_body, (shaped(experts, 2 * BLOCK, WIDE), shaped(slots, LANES))...  3.72 us
  transfers between devices with their start and end apart: 10, of which 7 were waited for; matrix products, arithmetic and copies ran while one was open for 3% of the time, Pallas kernels for 1%

profile of v3, /device:TPU:1, one launch (start us, length us, event | category | flops | bytes accessed | tf_op | source)
XLA Modules:
  0.0 171.4 jit_solution(7370200702624201028)
XLA Ops:
  3.7 3.7 %shard_map.110 = (bf16[128,32,256]{2,1,0:T(8,128)(2,1)}, bf16[256,128]{1,0:T(8,128)(2,1)S(1)}) custom-call(s32[8,16]{1,0:T(8,128)S(1)} %bitcast.13, bf16[8,16]{1,0:T(8,128)(2,1)S(1)} %bitcast.15, bf16[16,2048]{1,0:T(8,128)(2,1)S(1)} %copy-done.12, bf16[16,2048]{1,0:T(8,128)(2,1)S(1)} %copy-done.13), custom_call_target="tpu_custom_call" | custom-call | flops 268435456 | bytes 2097152 | tf_op jit(solution)/shard_map/pallas_call | solution.py:265
  7.4 25.7 %all-to-all-start = ((bf16[128,32,256]{2,1,0:T(8,128)(2,1)}), bf16[128,32,256]{2,1,0:T(8,128)(2,1)}, u32[]{:S(2)}, u32[]{:S(2)}) async-start(bf16[128,32,256]{2,1,0:T(8,128)(2,1)} %get-tuple-element.23), calls=%async_computation | async-start | bytes 4194304 | tf_op jit(solution)/shard_map/all_to_all | solution.py:219
  33.2 53.8 %all-to-all-done.arrived_ref = bf16[128,32,256]{2,1,0:T(8,128)(2,1)} async-done(((bf16[128,32,256]{2,1,0:T(8,128)(2,1)}), bf16[128,32,256]{2,1,0:T(8,128)(2,1)}, u32[]{:S(2)}, u32[]{:S(2)}) %all-to-all-start) | async-done | bytes 2097184 | tf_op jit(solution)/shard_map/all_to_all | solution.py:219
  87.0 7.6 %shard_map.111 = (bf16[256,768]{1,0:T(8,128)(2,1)S(1)}, bf16[256,128]{1,0:T(8,128)(2,1)S(1)}, bf16[1152,128]{1,0:T(8,128)(2,1)}, bf16[1152,128]{1,0:T(8,128)(2,1...) custom-call(s32[8]{0:T(128)S(1)} %and_select_fusion.order_ref, ...), custom_call_target="tpu_custom_call" | custom-call | flops 2415919104 | bytes 12582912 | tf_op jit(solution)/shard_map/pallas_call | solution.py:282
  94.6 3.1 %collective-permute-start.4 = (bf16[1152,128]{1,0:T(8,128)(2,1)}, bf16[1152,128]{1,0:T(8,128)(2,1)}, u32[]{:S(2)}, u32[]{:S(2)}) collective-permute-start(bf16[1152,128]{1,0:T(8,128)(2,1)} %get-tuple-element.37), channel_id=1, source_target_pairs={{0,896},{8,136},{16,912},{24,152},{32,928},{40,168},{48,944},{56,1... | collective-permute-start | bytes 884744 | tf_op jit(solution)/shard_map/ppermute | solution.py:229
  99.2 3.4 %collective-permute-start = (bf16[1152,128]{1,0:T(8,128)(2,1)}, bf16[1152,128]{1,0:T(8,128)(2,1)}, u32[]{:S(2)}, u32[]{:S(2)}) collective-permute-start(bf16[1152,128]{1,0:T(8,128)(2,1)} %get-tuple-element.33), channel_id=1, source_target_pairs={{0,128},{8,904},{16,144},{24,920},{32,160},{40,936},{48,176},{56,9... | collective-permute-start | bytes 884744 | tf_op jit(solution)/shard_map/ppermute | solution.py:229
  102.6 1.3 shard_map.112
  103.9 1.3 reshape.16
  105.1 6.5 %all-to-all-start.1 = ((bf16[128,2,2176]{2,1,0:T(2,128)(2,1)}), bf16[128,2,2176]{2,1,0:T(2,128)(2,1)}, u32[]{:S(2)}, u32[]{:S(2)}) async-start(bf16[128,2,2176]{2,1,0:T(2,128)(2,1)} %reshape.16), calls=%async_computation.1 | async-start | bytes 2228224 | tf_op jit(solution)/shard_map/all_to_all | solution.py:219
  111.7 1.1 add_convert_fusion.4
  112.9 2.1 %collective-permute-start.5 = (bf16[2304,128]{1,0:T(8,128)(2,1)S(1)}, bf16[2304,128]{1,0:T(8,128)(2,1)S(1)}, u32[]{:S(2)}, u32[]{:S(2)}) collective-permute-start(bf16[2304,128]{1,0:T(8,128)(2,1)S(1)} %pad_maximum_fusion.1), channel_id=1, source_target_pairs={{0,896},{8,136},{16,912},{24,152},{32,928},{40,168},{48,944},{56,1... | collective-permute-start | bytes 1769480 | tf_op jit(solution)/shard_map/ppermute | solution.py:229
  115.0 1.0 add_convert_fusion.5
  116.1 4.5 %collective-permute-start.1 = (bf16[2304,128]{1,0:T(8,128)(2,1)S(1)}, bf16[2304,128]{1,0:T(8,128)(2,1)S(1)}, u32[]{:S(2)}, u32[]{:S(2)}) collective-permute-start(bf16[2304,128]{1,0:T(8,128)(2,1)S(1)} %pad_maximum_fusion), channel_id=1, source_target_pairs={{0,128},{8,904},{16,144},{24,920},{32,160},{40,936},{48,176},{56,9... | collective-permute-start | bytes 1769480 | tf_op jit(solution)/shard_map/ppermute | solution.py:229
  120.6 4.6 %collective-permute-done.5 = bf16[2304,128]{1,0:T(8,128)(2,1)S(1)} collective-permute-done((bf16[2304,128]{1,0:T(8,128)(2,1)S(1)}, bf16[2304,128]{1,0:T(8,128)(2,1)S(1)}, u32[]{:S(2)}, u32[]{:S(2)}) %collective-permute-start.5) | collective-permute-done | bytes 589856 | tf_op jit(solution)/shard_map/ppermute | solution.py:229
  125.4 1.9 %collective-permute-start.6 = (bf16[2304,128]{1,0:T(8,128)(2,1)S(1)}, bf16[2304,128]{1,0:T(8,128)(2,1)S(1)}, u32[]{:S(2)}, u32[]{:S(2)}) collective-permute-start(bf16[2304,128]{1,0:T(8,128)(2,1)S(1)} %add_convert_fusion.1), channel_id=1, source_target_pairs={{0,896},{8,136},{16,912},{24,152},{32,928},{40,168},{48,944},{56,1... | collective-permute-start | bytes 1769480 | tf_op jit(solution)/shard_map/ppermute | solution.py:229
  127.3 4.8 %collective-permute-done.1 = bf16[2304,128]{1,0:T(8,128)(2,1)S(1)} collective-permute-done((bf16[2304,128]{1,0:T(8,128)(2,1)S(1)}, bf16[2304,128]{1,0:T(8,128)(2,1)S(1)}, u32[]{:S(2)}, u32[]{:S(2)}) %collective-permute-start.1) | collective-permute-done | bytes 589856 | tf_op jit(solution)/shard_map/ppermute | solution.py:229
  132.2 5.4 %collective-permute-start.2 = (bf16[2304,128]{1,0:T(8,128)(2,1)S(1)}, bf16[2304,128]{1,0:T(8,128)(2,1)S(1)}, u32[]{:S(2)}, u32[]{:S(2)}) collective-permute-start(bf16[2304,128]{1,0:T(8,128)(2,1)S(1)} %add_convert_fusion.3), channel_id=1, source_target_pairs={{0,128},{8,904},{16,144},{24,920},{32,160},{40,936},{48,176},{56,9... | collective-permute-start | bytes 1769480 | tf_op jit(solution)/shard_map/ppermute | solution.py:229
  137.7 1.2 collective-permute-done.6
  139.1 1.9 %collective-permute-start.7 = (bf16[2304,128]{1,0:T(8,128)(2,1)S(1)}, bf16[2304,128]{1,0:T(8,128)(2,1)S(1)}, u32[]{:S(2)}, u32[]{:S(2)}) collective-permute-start(bf16[2304,128]{1,0:T(8,128)(2,1)S(1)} %add_convert_fusion), channel_id=1, source_target_pairs={{0,896},{8,136},{16,912},{24,152},{32,928},{40,168},{48,944},{56,1... | collective-permute-start | bytes 1769480 | tf_op jit(solution)/shard_map/ppermute | solution.py:229
  141.0 8.8 %collective-permute-done.2 = bf16[2304,128]{1,0:T(8,128)(2,1)S(1)} collective-permute-done((bf16[2304,128]{1,0:T(8,128)(2,1)S(1)}, bf16[2304,128]{1,0:T(8,128)(2,1)S(1)}, u32[]{:S(2)}, u32[]{:S(2)}) %collective-permute-start.2) | collective-permute-done | bytes 589856 | tf_op jit(solution)/shard_map/ppermute | solution.py:229
  150.0 5.0 %collective-permute-start.3 = (bf16[2304,128]{1,0:T(8,128)(2,1)S(1)}, bf16[2304,128]{1,0:T(8,128)(2,1)S(1)}, u32[]{:S(2)}, u32[]{:S(2)}) collective-permute-start(bf16[2304,128]{1,0:T(8,128)(2,1)S(1)} %add_convert_fusion.2), channel_id=1, source_target_pairs={{0,128},{8,904},{16,144},{24,920},{32,160},{40,936},{48,176},{56,9... | collective-permute-start | bytes 1769480 | tf_op jit(solution)/shard_map/ppermute | solution.py:229
  155.3 12.6 %collective-permute-done.3.ahead_ref = bf16[2304,128]{1,0:T(8,128)(2,1)S(1)} collective-permute-done((bf16[2304,128]{1,0:T(8,128)(2,1)S(1)}, bf16[2304,128]{1,0:T(8,128)(2,1)S(1)}, u32[]{:S(2)}, u32[]{:S(2)}) %collective-permute-start.3) | collective-permute-done | bytes 589856 | tf_op jit(solution)/shard_map/ppermute | solution.py:229
  168.0 1.0 shard_map.114
  168.9 1.5 reshape.17.returned_ref
  (46 shorter events, 6.5 us)
Async XLA Ops:
  2.0 0.8 copy-start.12
  2.8 0.8 copy-start.13
  7.4 79.5 %all-to-all-start = ((bf16[128,32,256]{2,1,0:T(8,128)(2,1)}), bf16[128,32,256]{2,1,0:T(8,128)(2,1)}, u32[]{:S(2)}, u32[]{:S(2)}) async-start(bf16[128,32,256]{2,1,0:T(8,128)(2,1)} %get-tuple-element.23), calls=%async_computation | async-start | bytes 4194304 | tf_op jit(solution)/shard_map/all_to_all | solution.py:219
  87.0 15.6 %copy-start = (bf16[1,2048,384]{2,1,0:T(8,128)(2,1)S(1)}, bf16[1,2048,384]{2,1,0:T(8,128)(2,1)}, u32[]{:S(2)}) copy-start(bf16[1,2048,384]{2,1,0:T(8,128)(2,1)} %param.11) | copy-start | bytes 4718596
  87.0 15.6 %copy-start.1 = (bf16[1,2048,384]{2,1,0:T(8,128)(2,1)S(1)}, bf16[1,2048,384]{2,1,0:T(8,128)(2,1)}, u32[]{:S(2)}) copy-start(bf16[1,2048,384]{2,1,0:T(8,128)(2,1)} %param.12) | copy-start | bytes 4718596
  94.5 8.0 %copy-start.2 = (bf16[2304,128]{1,0:T(8,128)(2,1)}, bf16[2304,128]{1,0:T(8,128)(2,1)S(1)}, u32[]{:S(2)}) copy-start(bf16[2304,128]{1,0:T(8,128)(2,1)S(1)} %get-tuple-element.35) | copy-start | bytes 1769476
  94.5 8.0 %copy-start.4 = (bf16[2304,128]{1,0:T(8,128)(2,1)}, bf16[2304,128]{1,0:T(8,128)(2,1)S(1)}, u32[]{:S(2)}) copy-start(bf16[2304,128]{1,0:T(8,128)(2,1)S(1)} %get-tuple-element.32) | copy-start | bytes 1769476
  94.6 8.0 %copy-start.6 = (bf16[2304,128]{1,0:T(8,128)(2,1)}, bf16[2304,128]{1,0:T(8,128)(2,1)S(1)}, u32[]{:S(2)}) copy-start(bf16[2304,128]{1,0:T(8,128)(2,1)S(1)} %get-tuple-element.36) | copy-start | bytes 1769476
  94.6 17.1 %collective-permute-start.4 = (bf16[1152,128]{1,0:T(8,128)(2,1)}, bf16[1152,128]{1,0:T(8,128)(2,1)}, u32[]{:S(2)}, u32[]{:S(2)}) collective-permute-start(bf16[1152,128]{1,0:T(8,128)(2,1)} %get-tuple-element.37), channel_id=1, source_target_pairs={{0,896},{8,136},{16,912},{24,152},{32,928},{40,168},{48,944},{56,1... | collective-permute-start | bytes 884744 | tf_op jit(solution)/shard_map/ppermute | solution.py:229
  99.2 15.8 %collective-permute-start = (bf16[1152,128]{1,0:T(8,128)(2,1)}, bf16[1152,128]{1,0:T(8,128)(2,1)}, u32[]{:S(2)}, u32[]{:S(2)}) collective-permute-start(bf16[1152,128]{1,0:T(8,128)(2,1)} %get-tuple-element.33), channel_id=1, source_target_pairs={{0,128},{8,904},{16,144},{24,920},{32,160},{40,936},{48,176},{56,9... | collective-permute-start | bytes 884744 | tf_op jit(solution)/shard_map/ppermute | solution.py:229
  105.1 6.5 %copy-start.7 = (bf16[2304,128]{1,0:T(8,128)(2,1)S(1)}, bf16[2304,128]{1,0:T(8,128)(2,1)}, u32[]{:S(2)}) copy-start(bf16[2304,128]{1,0:T(8,128)(2,1)} %copy-done.6) | copy-start | bytes 1769476
  105.1 7.7 %copy-start.15 = (bf16[1152,128]{1,0:T(8,128)(2,1)S(1)}, bf16[1152,128]{1,0:T(8,128)(2,1)}, u32[]{:S(2)}) copy-start(bf16[1152,128]{1,0:T(8,128)(2,1)} %slice.14) | copy-start | bytes 884740
  105.1 63.8 %all-to-all-start.1 = ((bf16[128,2,2176]{2,1,0:T(2,128)(2,1)}), bf16[128,2,2176]{2,1,0:T(2,128)(2,1)}, u32[]{:S(2)}, u32[]{:S(2)}) async-start(bf16[128,2,2176]{2,1,0:T(2,128)(2,1)} %reshape.16), calls=%async_computation.1 | async-start | bytes 2228224 | tf_op jit(solution)/shard_map/all_to_all | solution.py:219
  111.6 3.4 %copy-start.5 = (bf16[2304,128]{1,0:T(8,128)(2,1)S(1)}, bf16[2304,128]{1,0:T(8,128)(2,1)}, u32[]{:S(2)}) copy-start(bf16[2304,128]{1,0:T(8,128)(2,1)} %copy-done.4) | copy-start | bytes 1769476
  112.8 3.3 %copy-start.14 = (bf16[1152,128]{1,0:T(8,128)(2,1)S(1)}, bf16[1152,128]{1,0:T(8,128)(2,1)}, u32[]{:S(2)}) copy-start(bf16[1152,128]{1,0:T(8,128)(2,1)} %slice.13) | copy-start | bytes 884740
  112.8 12.4 %copy-start.3 = (bf16[2304,128]{1,0:T(8,128)(2,1)S(1)}, bf16[2304,128]{1,0:T(8,128)(2,1)}, u32[]{:S(2)}) copy-start(bf16[2304,128]{1,0:T(8,128)(2,1)} %copy-done.2) | copy-start | bytes 1769476
  112.9 12.4 %collective-permute-start.5 = (bf16[2304,128]{1,0:T(8,128)(2,1)S(1)}, bf16[2304,128]{1,0:T(8,128)(2,1)S(1)}, u32[]{:S(2)}, u32[]{:S(2)}) collective-permute-start(bf16[2304,128]{1,0:T(8,128)(2,1)S(1)} %pad_maximum_fusion.1), channel_id=1, source_target_pairs={{0,896},{8,136},{16,912},{24,152},{32,928},{40,168},{48,944},{56,1... | collective-permute-start | bytes 1769480 | tf_op jit(solution)/shard_map/ppermute | solution.py:229
  116.1 16.0 %collective-permute-start.1 = (bf16[2304,128]{1,0:T(8,128)(2,1)S(1)}, bf16[2304,128]{1,0:T(8,128)(2,1)S(1)}, u32[]{:S(2)}, u32[]{:S(2)}) collective-permute-start(bf16[2304,128]{1,0:T(8,128)(2,1)S(1)} %pad_maximum_fusion), channel_id=1, source_target_pairs={{0,128},{8,904},{16,144},{24,920},{32,160},{40,936},{48,176},{56,9... | collective-permute-start | bytes 1769480 | tf_op jit(solution)/shard_map/ppermute | solution.py:229
  125.4 13.5 %collective-permute-start.6 = (bf16[2304,128]{1,0:T(8,128)(2,1)S(1)}, bf16[2304,128]{1,0:T(8,128)(2,1)S(1)}, u32[]{:S(2)}, u32[]{:S(2)}) collective-permute-start(bf16[2304,128]{1,0:T(8,128)(2,1)S(1)} %add_convert_fusion.1), channel_id=1, source_target_pairs={{0,896},{8,136},{16,912},{24,152},{32,928},{40,168},{48,944},{56,1... | collective-permute-start | bytes 1769480 | tf_op jit(solution)/shard_map/ppermute | solution.py:229
  132.2 17.6 %collective-permute-start.2 = (bf16[2304,128]{1,0:T(8,128)(2,1)S(1)}, bf16[2304,128]{1,0:T(8,128)(2,1)S(1)}, u32[]{:S(2)}, u32[]{:S(2)}) collective-permute-start(bf16[2304,128]{1,0:T(8,128)(2,1)S(1)} %add_convert_fusion.3), channel_id=1, source_target_pairs={{0,128},{8,904},{16,144},{24,920},{32,160},{40,936},{48,176},{56,9... | collective-permute-start | bytes 1769480 | tf_op jit(solution)/shard_map/ppermute | solution.py:229
  139.1 16.2 %collective-permute-start.7 = (bf16[2304,128]{1,0:T(8,128)(2,1)S(1)}, bf16[2304,128]{1,0:T(8,128)(2,1)S(1)}, u32[]{:S(2)}, u32[]{:S(2)}) collective-permute-start(bf16[2304,128]{1,0:T(8,128)(2,1)S(1)} %add_convert_fusion), channel_id=1, source_target_pairs={{0,896},{8,136},{16,912},{24,152},{32,928},{40,168},{48,944},{56,1... | collective-permute-start | bytes 1769480 | tf_op jit(solution)/shard_map/ppermute | solution.py:229
  150.0 18.0 %collective-permute-start.3 = (bf16[2304,128]{1,0:T(8,128)(2,1)S(1)}, bf16[2304,128]{1,0:T(8,128)(2,1)S(1)}, u32[]{:S(2)}, u32[]{:S(2)}) collective-permute-start(bf16[2304,128]{1,0:T(8,128)(2,1)S(1)} %add_convert_fusion.2), channel_id=1, source_target_pairs={{0,128},{8,904},{16,144},{24,920},{32,160},{40,936},{48,176},{56,9... | collective-permute-start | bytes 1769480 | tf_op jit(solution)/shard_map/ppermute | solution.py:229
  168.9 1.5 copy-start.9
  168.9 1.5 copy-start.11
  (2 other events, 1.4 us)

commit v4 on v3

--- a/solution.py
+++ b/solution.py
@@ -7,7 +7,7 @@
 
 PLANE = ("node", "local")
 BF16, F32, I32 = jnp.bfloat16, jnp.float32, jnp.int32
-VMEM_LIMIT = 48 << 20
+VMEM_LIMIT, VMEM_MOST = 24 << 20, 60 << 20
 CAP, PIECES, WIDE = 2, 8, 256
 BLOCK = CAP * PIECES
 GROUP = 16
@@ -29,7 +29,7 @@
     return [pl.BlockSpec(memory_space=pltpu.VMEM)] * count
 
 
-def call(body, outs, in_specs, out_specs, scratch=(), cost=None):
+def call(body, outs, in_specs, out_specs, scratch=(), cost=None, limit=VMEM_LIMIT):
     return pl.pallas_call(
         body,
         out_shape=outs,
@@ -37,7 +37,7 @@
         out_specs=out_specs,
         scratch_shapes=scratch,
         cost_estimate=cost,
-        compiler_params=pltpu.CompilerParams(vmem_limit_bytes=VMEM_LIMIT),
+        compiler_params=pltpu.CompilerParams(vmem_limit_bytes=limit),
     )
 
 
@@ -90,18 +90,33 @@
             )
 
 
+def store_part(down, gate_up, ref):
+    at = 0
+    for part in (gate_up, down):
+        rows = part.shape[0]
+        for b in range(part.shape[1] // LANES):
+            ref[at : at + rows, :] = part[:, b * LANES : (b + 1) * LANES]
+            at += rows
+
+
 def expert_body(
-    order_ref, arrived_ref, gate_hbm, up_hbm, down_hbm,
-    slopes_ref, score_ref, far_ahead, far_behind, *refs,
+    order_ref, arrived_hbm, gate_hbm, up_hbm, down_hbm,
+    rows_ref, hidden_ref, slopes_ref, score_ref, far_ref,
+    arrived_ref, w_gate, w_up, w_down, turned_ref, arrived_sems, load_sems,
 ):
-    near, (rows_ref, w_gate, w_up, w_down, down_ref, load_sems) = refs[:-6], refs[-6:]
+    arrivals = [
+        pltpu.make_async_copy(
+            arrived_hbm.at[:, pl.ds(part * BLOCK, BLOCK)], arrived_ref.at[part], arrived_sems.at[part]
+        )
+        for part in range(2)
+    ]
     loads = [
         pltpu.make_async_copy(source, target, load_sems.at[i])
         for i, (source, target) in enumerate(
             ((gate_hbm, w_gate), (up_hbm, w_up), (down_hbm, w_down))
         )
     ]
-    for load in loads:
+    for load in arrivals + loads:
         load.start()
     slots = rows_ref.shape[1]
     hidden = w_gate.shape[1]
@@ -109,8 +124,9 @@
     wanted = (order // CAP % GROUP) * BLOCK + (order // GROUP_SLOTS) * CAP + order % CAP
     shuffle = jnp.where(wanted == iota(order.shape, 1), 1.0, 0.0).astype(BF16)
     for part in range(2):
+        arrivals[part].wait()
         for g in range(slots // GROUP_SLOTS):
-            block = arrived_ref[g * GROUP : (g + 1) * GROUP, part * BLOCK : (part + 1) * BLOCK, :]
+            block = arrived_ref[part, g * GROUP : (g + 1) * GROUP]
             block = dot(shuffle, block.reshape(GROUP * BLOCK, WIDE), 1, 0).astype(BF16)
             for j in range(PIECES):
                 rows_ref[
@@ -131,32 +147,31 @@
     score = jnp.sum(hidden_act.astype(F32) * grad_act, axis=1, keepdims=True)
     score_ref[...] = jnp.broadcast_to(score, score_ref.shape).astype(BF16)
 
+    hidden_ref[...] = hidden_act
+    turned_ref[...] = hidden_act.astype(F32).T.astype(BF16)
     shards = order_ref.shape[0]
     share = hidden // shards
+    target = order_ref[shards // 2]
+    columns = pl.ds(pl.multiple_of(target * WIDE, WIDE), WIDE)
+    gate_up = dot(rows_ref[0, :, columns], slopes_ref[...], 0, 0).astype(BF16)
+    turned = turned_ref[pl.ds(pl.multiple_of(target * share, 16), share), :]
+    down = dot(turned, rows_ref[1], 1, 0).astype(BF16)
+    store_part(down, gate_up, far_ref)
+
+
+def near_body(order_ref, rows_ref, hidden_ref, slopes_ref, *refs):
+    near, down_ref = refs[:-1], refs[-1]
+    shards = order_ref.shape[0]
+    share = hidden_ref.shape[1] // shards
     for n in range(PIECES):
         columns = slice(n * WIDE, (n + 1) * WIDE)
-        down_ref[:, columns] = dot(hidden_act, rows_ref[1, :, columns], 0, 0).astype(BF16)
-    far = shards // 2
-    for offset in (far, *range(far), *range(far + 1, shards)):
+        down_ref[:, columns] = dot(hidden_ref[...], rows_ref[1, :, columns], 0, 0).astype(BF16)
+    for i, offset in enumerate((*range(shards // 2), *range(shards // 2 + 1, shards))):
         target = order_ref[offset]
         columns = pl.ds(pl.multiple_of(target * WIDE, WIDE), WIDE)
         gate_up = dot(rows_ref[0, :, columns], slopes_ref[...], 0, 0).astype(BF16)
         down = down_ref[pl.ds(pl.multiple_of(target * share, 16), share), :]
-        pieces = [gate_up[:, b * LANES : (b + 1) * LANES] for b in range(2 * hidden // LANES)]
-        pieces += [down[:, b * LANES : (b + 1) * LANES] for b in range(down.shape[1] // LANES)]
-        at = 0
-        for piece in pieces:
-            rows = piece.shape[0]
-            if offset != far:
-                near[offset - (offset > far)][at : at + rows, :] = piece
-            else:
-                split = far_ahead.shape[0]
-                first = min(max(split - at, 0), rows)
-                if first:
-                    far_ahead[at : at + first, :] = piece[:first]
-                if first < rows:
-                    far_behind[at + first - split : at + rows - split, :] = piece[first:]
-            at += rows
+        store_part(down, gate_up, near[i])
 
 
 def rows_body(slopes_ref, score_ref, gate_ref, up_ref, out_ref):
@@ -233,22 +248,6 @@
     return (left.astype(F32) + right.astype(F32)).astype(BF16)
 
 
-def reduce_scatter(far_ahead, far_behind, near):
-    forward, backward = ring(0), ring(1)
-    half = far_ahead.shape[0]
-    ahead, behind = forward(far_ahead), backward(far_behind)
-    last = len(near) // 2
-    for d in range(last, 0, -1):
-        to_ahead, to_behind = near[d], near[len(near) - d]
-        if d == last:
-            to_ahead = jnp.concatenate((add(to_ahead[:half], ahead), to_ahead[half:]))
-            to_behind = jnp.concatenate((to_behind[:half], add(to_behind[half:], behind)))
-        else:
-            to_ahead, to_behind = add(to_ahead, ahead), add(to_behind, behind)
-        ahead, behind = forward(to_ahead), backward(to_behind)
-    return near[0], ahead, behind
-
-
 def shards(tokens, grads_out, expert_ids, gates, w_gate, w_up, w_down):
     experts = lax.axis_size("node") * lax.axis_size("local")
     reps = lax.axis_size("rep")
@@ -261,7 +260,7 @@
     packed_rows = (2 * hidden * (width // reps) + (hidden // reps) * width) // LANES
     product = 2 * slots * width * hidden
 
-    hbm = pl.BlockSpec(memory_space=pl.ANY)
+    hbm = pl.BlockSpec(memory_space=pltpu.HBM)
     outgoing, spread = call(
         route_body,
         (shaped(experts, 2 * BLOCK, WIDE), shaped(slots, LANES)),
@@ -274,33 +273,51 @@
             pltpu.SemaphoreType.DMA((3,)),
         ),
         cost=cost(4 * slots * LANES * width, 4 * slots * width),
+        limit=VMEM_MOST,
     )(ids_t, gates_t, tokens, grads_out)
     arrived = exchange(outgoing)
 
     direction = 1 - 2 * (lax.axis_index("node") % 2)
     order = (lax.axis_index("rep") + direction * lax.iota(I32, reps) + reps) % reps
-    slopes, score, far_ahead, far_behind, *near = call(
+    smem = pl.BlockSpec(memory_space=pltpu.SMEM)
+    routed, hidden_act, slopes, score, far = call(
         expert_body,
         (
+            shaped(2, slots, width),
+            shaped(slots, hidden),
             shaped(slots, 2 * hidden),
             shaped(slots, LANES),
-            *[shaped(packed_rows // 2, LANES)] * 2,
-            *[shaped(packed_rows, LANES)] * (reps - 1),
+            shaped(packed_rows, LANES),
         ),
-        [pl.BlockSpec(memory_space=pltpu.SMEM)] + whole(1) + [hbm] * 3,
-        whole(4 + reps - 1),
+        [smem] + [hbm] * 4,
+        whole(5),
         scratch=(
-            pltpu.VMEM((2, slots, width), BF16),
+            pltpu.VMEM((2, experts, BLOCK, WIDE), BF16),
             pltpu.VMEM((width, hidden), BF16),
             pltpu.VMEM((width, hidden), BF16),
             pltpu.VMEM((hidden, width), BF16),
-            pltpu.VMEM((hidden, width), BF16),
+            pltpu.VMEM((hidden, slots), BF16),
+            pltpu.SemaphoreType.DMA((2,)),
             pltpu.SemaphoreType.DMA((3,)),
         ),
-        cost=cost(6 * product, 12 << 20),
+        cost=cost(4 * product, 10 << 20),
+        limit=49 << 20,
     )(order, arrived, w_gate, w_up, w_down)
-
-    sums = reduce_scatter(far_ahead, far_behind, near)
+    forward, backward = ring(0), ring(1)
+    first = forward(far)
+    near = call(
+        near_body,
+        [shaped(packed_rows, LANES)] * (reps - 1),
+        [smem] + whole(3),
+        whole(reps - 1),
+        scratch=(pltpu.VMEM((hidden, width), BF16),),
+        cost=cost(3 * product, 8 << 20),
+    )(order, routed, hidden_act, slopes)
+    ahead = add(near[3], first)
+    slopes, score, _ = lax.optimization_barrier((slopes, score, ahead))
+    ahead, behind = forward(ahead), backward(near[-3])
+    ahead, behind = forward(add(near[2], ahead)), backward(add(near[-2], behind))
+    ahead, behind = forward(add(near[1], ahead)), backward(add(near[-1], behind))
 
     rows = call(
         rows_body,
@@ -318,6 +335,7 @@
         cost=cost(2 * slots * tok * width, 2 << 20),
     )(returned, spread, ids_t, gates_t)
 
+    own, grad_tokens, grad_gates = lax.optimization_barrier((near[0], grad_tokens, grad_gates))
     grad_w_gate, grad_w_up, grad_w_down = call(
         unpack_body,
         (
@@ -328,7 +346,7 @@
         whole(3),
         whole(3),
         cost=cost(0, 2 << 20),
-    )(*sums)
+    )(own, ahead, behind)
     return (
         grad_tokens,
         grad_gates.T,

time: 172 us -> 168 us (0.977); the launches traced: 171 us -> 166 us
  waiting for transfers between devices: 86.2 us -> 79.1 us
  starting transfers between devices: 59.6 us -> 57 us
  other arithmetic: 2.85 us -> 5.45 us
  Pallas kernels: 14.5 us -> 16.7 us
    ppermute x8 -> x7, waiting for transfers between devices: 32.4 us -> 10.3 us  [ring(): return lambda message: lax.ppermute(message, ('rep', 'node'), pairs)]
    all_to_all x2, waiting for transfers between devices: 53.8 us -> 68.8 us  [exchange(): lax.all_to_all(blocks, PLANE, split_axis=0, concat_axis=0, tiled=True)]
    ppermute x8 -> x7, starting transfers between devices: 27.4 us -> 22.8 us  [ring(): return lambda message: lax.ppermute(message, ('rep', 'node'), pairs)]
    convert_element_type x6 -> x5, other arithmetic: 2.76 us -> 5.44 us  [add(): return (left.astype(F32) + right.astype(F32)).astype(BF16)]
    all_to_all x2, starting transfers between devices: 32.2 us -> 34.2 us  [exchange(): lax.all_to_all(blocks, PLANE, split_axis=0, concat_axis=0, tiled=True)]
    pallas_call x1 -> x2, Pallas kernels: 7.57 us -> 8.52 us  [the longest x1 6.44 us: shards(): call(expert_body, (shaped(2, slots, width), shaped(slots, hidden), shaped...]
  transfers between devices with their start and end apart: 10 -> 9, of which waited for: 7 -> 5; matrix products, arithmetic and copies ran while one was open for 3% -> 6% of each run, Pallas kernels for 1% -> 3%
where the time goes in v4:
time: 168 us; the launch traced here: 166 us
  waiting for transfers between devices  79.1 us (47%)
  starting transfers between devices  57 us (34%)
  Pallas kernels  16.7 us (10%)
  local copies, waits for them, and re-layouts  6.43 us (4%)
  other arithmetic  5.45 us (3%)
    all_to_all x2, waiting for transfers between devices, exchange(): lax.all_to_all(blocks, PLANE, split_axis=0, concat_axis=0, tiled=True)  68.8 us
    all_to_all x2, starting transfers between devices, exchange(): lax.all_to_all(blocks, PLANE, split_axis=0, concat_axis=0, tiled=True)  34.2 us
    ppermute x7, starting transfers between devices, ring(): return lambda message: lax.ppermute(message, ('rep', 'node'), pairs)  22.8 us
    ppermute x7, waiting for transfers between devices, ring(): return lambda message: lax.ppermute(message, ('rep', 'node'), pairs)  10.3 us
    pallas_call x1, Pallas kernels, shards(): call(expert_body, (shaped(2, slots, width), shaped(slots, hidden), shaped...  6.44 us
    convert_element_type x5, other arithmetic, add(): return (left.astype(F32) + right.astype(F32)).astype(BF16)  5.44 us
    pallas_call x1, Pallas kernels, shards(): call(route_body, (shaped(experts, 2 * BLOCK, WIDE), shaped(slots, LANES))...  4.93 us
  transfers between devices with their start and end apart: 9, of which 5 were waited for; matrix products, arithmetic and copies ran while one was open for 6% of the time, Pallas kernels for 3%

profile of v4, /device:TPU:1, one launch (start us, length us, event | category | flops | bytes accessed | tf_op | source)
XLA Modules:
  0.0 165.5 jit_solution(13917429732502087037)
XLA Ops:
  0.6 4.9 %shard_map.110 = (bf16[128,32,256]{2,1,0:T(8,128)(2,1)}, bf16[256,128]{1,0:T(8,128)(2,1)}) custom-call(s32[8,16]{1,0:T(8,128)} %bitcast.13, bf16[8,16]{1,0:T(8,128)(2,1)} %bitcast.15, bf16[16,2048]{1,0:T(8,128)(2,1)} %tokens_hbm.1, bf16[16,2048]{1,0:T(8,128)(2,1)} %grads_hbm.1), custom_call_target="tpu_custom_call" | custom-call | flops 268435456 | bytes 2097152 | tf_op jit(solution)/shard_map/pallas_call | solution.py:264
  5.6 26.0 %all-to-all-start = ((bf16[128,32,256]{2,1,0:T(8,128)(2,1)}), bf16[128,32,256]{2,1,0:T(8,128)(2,1)}, u32[]{:S(2)}, u32[]{:S(2)}) async-start(bf16[128,32,256]{2,1,0:T(8,128)(2,1)} %get-tuple-element.29), calls=%async_computation | async-start | bytes 4194304 | tf_op jit(solution)/shard_map/all_to_all | solution.py:234
  31.6 53.8 %all-to-all-done.arrived_hbm = bf16[128,32,256]{2,1,0:T(8,128)(2,1)} async-done(((bf16[128,32,256]{2,1,0:T(8,128)(2,1)}), bf16[128,32,256]{2,1,0:T(8,128)(2,1)}, u32[]{:S(2)}, u32[]{:S(2)}) %all-to-all-start) | async-done | bytes 2097184 | tf_op jit(solution)/shard_map/all_to_all | solution.py:234
  85.4 6.4 %shard_map.111 = (bf16[2,256,2048]{2,1,0:T(8,128)(2,1)}, bf16[256,384]{1,0:T(8,128)(2,1)S(1)}, bf16[256,768]{1,0:T(8,128)(2,1)S(1)}, bf16[256,128]{1,0:T(8,128)(2,1)S(1)}, bf16[2304,128]{1,0:T(8,128)(2,1)S(1)}) custom-call(s32[8]{0:T(128)S(1)} %and_select_fusion.order_ref, bf16[128,32,256]{2,1,0:T(8,128)(2,1)} %all-to-all-done.arrived_hbm, ...), custom_call_target="tpu_custom_call" | custom-call | flops 1610612736 | bytes 10485760 | tf_op jit(solution)/shard_map/pallas_call | solution.py:283
  91.9 4.5 %collective-permute-start = (bf16[2304,128]{1,0:T(8,128)(2,1)S(1)}, bf16[2304,128]{1,0:T(8,128)(2,1)S(1)}, u32[]{:S(2)}, u32[]{:S(2)}) collective-permute-start(bf16[2304,128]{1,0:T(8,128)(2,1)S(1)} %get-tuple-element.36), channel_id=1, source_target_pairs={{0,128},{8,904},{16,144},{24,920},{32,160},{40,936},{48,176},{56,9... | collective-permute-start | bytes 1769480 | tf_op jit(solution)/shard_map/ppermute | solution.py:244
  96.4 1.6 copy-done.14
  98.0 2.1 %shard_map.112 = (bf16[2304,128]{1,0:T(8,128)(2,1)S(1)}, bf16[2304,128]{1,0:T(8,128)(2,1)S(1)}, bf16[2304,128]{1,0:T(8,128)(2,1)S(1)}, bf16[2304,128]{1,0:T(8,12...) custom-call(s32[8]{0:T(128)S(1)} %and_select_fusion.order_ref, ...), custom_call_target="tpu_custom_call" | custom-call | flops 1207959552 | bytes 8388608 | tf_op jit(solution)/shard_map/pallas_call | solution.py:308
  100.1 1.9 %collective-permute-start.4 = (bf16[2304,128]{1,0:T(8,128)(2,1)S(1)}, bf16[2304,128]{1,0:T(8,128)(2,1)S(1)}, u32[]{:S(2)}, u32[]{:S(2)}) collective-permute-start(bf16[2304,128]{1,0:T(8,128)(2,1)S(1)} %get-tuple-element.49), channel_id=1, source_target_pairs={{0,896},{8,136},{16,912},{24,152},{32,928},{40,168},{48,944},{56,1... | collective-permute-start | bytes 1769480 | tf_op jit(solution)/shard_map/ppermute | solution.py:244
  102.0 2.0 %collective-permute-done = bf16[2304,128]{1,0:T(8,128)(2,1)S(1)} collective-permute-done((bf16[2304,128]{1,0:T(8,128)(2,1)S(1)}, bf16[2304,128]{1,0:T(8,128)(2,1)S(1)}, u32[]{:S(2)}, u32[]{:S(2)}) %collective-permute-start) | collective-permute-done | bytes 589856 | tf_op jit(solution)/shard_map/ppermute | solution.py:244
  105.0 5.3 %collective-permute-start.1 = (bf16[2304,128]{1,0:T(8,128)(2,1)}, bf16[2304,128]{1,0:T(8,128)(2,1)}, u32[]{:S(2)}, u32[]{:S(2)}) collective-permute-start(bf16[2304,128]{1,0:T(8,128)(2,1)} %add_convert_fusion.4), channel_id=1, source_target_pairs={{0,128},{8,904},{16,144},{24,920},{32,160},{40,936},{48,176},{56,9... | collective-permute-start | bytes 1769480 | tf_op jit(solution)/shard_map/ppermute | solution.py:244
  110.3 2.9 %collective-permute-done.4 = bf16[2304,128]{1,0:T(8,128)(2,1)S(1)} collective-permute-done((bf16[2304,128]{1,0:T(8,128)(2,1)S(1)}, bf16[2304,128]{1,0:T(8,128)(2,1)S(1)}, u32[]{:S(2)}, u32[]{:S(2)}) %collective-permute-start.4) | collective-permute-done | bytes 589856 | tf_op jit(solution)/shard_map/ppermute | solution.py:244
  114.2 1.9 %collective-permute-start.5 = (bf16[2304,128]{1,0:T(8,128)(2,1)}, bf16[2304,128]{1,0:T(8,128)(2,1)}, u32[]{:S(2)}, u32[]{:S(2)}) collective-permute-start(bf16[2304,128]{1,0:T(8,128)(2,1)} %add_convert_fusion.1), channel_id=1, source_target_pairs={{0,896},{8,136},{16,912},{24,152},{32,928},{40,168},{48,944},{56,1... | collective-permute-start | bytes 1769480 | tf_op jit(solution)/shard_map/ppermute | solution.py:244
  116.1 1.3 shard_map.113
  117.4 1.0 copy-done.2
  118.4 2.3 %reshape.16 = bf16[128,2,2176]{2,1,0:T(2,128)(2,1)} reshape(bf16[256,2176]{1,0:T(8,128)(2,1)} %copy-done.2) | data formatting | bytes 2228224 | tf_op jit(solution)/shard_map/reshape | solution.py:329
  120.7 8.2 %all-to-all-start.1 = ((bf16[128,2,2176]{2,1,0:T(2,128)(2,1)}), bf16[128,2,2176]{2,1,0:T(2,128)(2,1)}, u32[]{:S(2)}, u32[]{:S(2)}) async-start(bf16[128,2,2176]{2,1,0:T(2,128)(2,1)} %reshape.16), calls=%async_computation.1 | async-start | bytes 2228224 | tf_op jit(solution)/shard_map/all_to_all | solution.py:234
  128.9 1.3 add_convert_fusion.3
  130.2 3.4 %collective-permute-start.2 = (bf16[2304,128]{1,0:T(8,128)(2,1)S(1)}, bf16[2304,128]{1,0:T(8,128)(2,1)S(1)}, u32[]{:S(2)}, u32[]{:S(2)}) collective-permute-start(bf16[2304,128]{1,0:T(8,128)(2,1)S(1)} %add_convert_fusion.3), channel_id=1, source_target_pairs={{0,128},{8,904},{16,144},{24,920},{32,160},{40,936},{48,176},{56,9... | collective-permute-start | bytes 1769480 | tf_op jit(solution)/shard_map/ppermute | solution.py:244
  133.6 1.2 add_convert_fusion
  134.9 2.0 %collective-permute-start.6 = (bf16[2304,128]{1,0:T(8,128)(2,1)S(1)}, bf16[2304,128]{1,0:T(8,128)(2,1)S(1)}, u32[]{:S(2)}, u32[]{:S(2)}) collective-permute-start(bf16[2304,128]{1,0:T(8,128)(2,1)S(1)} %add_convert_fusion), channel_id=1, source_target_pairs={{0,896},{8,136},{16,912},{24,152},{32,928},{40,168},{48,944},{56,1... | collective-permute-start | bytes 1769480 | tf_op jit(solution)/shard_map/ppermute | solution.py:244
  136.9 5.4 %collective-permute-done.2 = bf16[2304,128]{1,0:T(8,128)(2,1)S(1)} collective-permute-done((bf16[2304,128]{1,0:T(8,128)(2,1)S(1)}, bf16[2304,128]{1,0:T(8,128)(2,1)S(1)}, u32[]{:S(2)}, u32[]{:S(2)}) %collective-permute-start.2) | collective-permute-done | bytes 589856 | tf_op jit(solution)/shard_map/ppermute | solution.py:244
  143.3 3.8 %collective-permute-start.3 = (bf16[2304,128]{1,0:T(8,128)(2,1)}, bf16[2304,128]{1,0:T(8,128)(2,1)S(1)}, u32[]{:S(2)}, u32[]{:S(2)}) collective-permute-start(bf16[2304,128]{1,0:T(8,128)(2,1)} %add_convert_fusion.2), channel_id=1, source_target_pairs={{0,128},{8,904},{16,144},{24,920},{32,160},{40,936},{48,176},{56,9... | collective-permute-start | bytes 1769480 | tf_op jit(solution)/shard_map/ppermute | solution.py:244
  147.0 15.0 %all-to-all-done.1 = bf16[128,2,2176]{2,1,0:T(2,128)(2,1)} async-done(((bf16[128,2,2176]{2,1,0:T(2,128)(2,1)}), bf16[128,2,2176]{2,1,0:T(2,128)(2,1)}, u32[]{:S(2)}, u32[]{:S(2)}) %all-to-all-start.1) | async-done | bytes 1114144 | tf_op jit(solution)/shard_map/all_to_all | solution.py:234
  162.1 1.5 reshape.17.returned_ref
  (38 shorter events, 5.0 us)
Async XLA Ops:
  5.6 79.8 %copy-start = (bf16[1,2048,384]{2,1,0:T(8,128)(2,1)S(1)}, bf16[1,2048,384]{2,1,0:T(8,128)(2,1)}, u32[]{:S(2)}) copy-start(bf16[1,2048,384]{2,1,0:T(8,128)(2,1)} %param.11) | copy-start | bytes 4718596
  5.6 79.8 %copy-start.1 = (bf16[1,2048,384]{2,1,0:T(8,128)(2,1)S(1)}, bf16[1,2048,384]{2,1,0:T(8,128)(2,1)}, u32[]{:S(2)}) copy-start(bf16[1,2048,384]{2,1,0:T(8,128)(2,1)} %param.12) | copy-start | bytes 4718596
  5.6 79.8 %all-to-all-start = ((bf16[128,32,256]{2,1,0:T(8,128)(2,1)}), bf16[128,32,256]{2,1,0:T(8,128)(2,1)}, u32[]{:S(2)}, u32[]{:S(2)}) async-start(bf16[128,32,256]{2,1,0:T(8,128)(2,1)} %get-tuple-element.29), calls=%async_computation | async-start | bytes 4194304 | tf_op jit(solution)/shard_map/all_to_all | solution.py:234
  91.9 12.1 %collective-permute-start = (bf16[2304,128]{1,0:T(8,128)(2,1)S(1)}, bf16[2304,128]{1,0:T(8,128)(2,1)S(1)}, u32[]{:S(2)}, u32[]{:S(2)}) collective-permute-start(bf16[2304,128]{1,0:T(8,128)(2,1)S(1)} %get-tuple-element.36), channel_id=1, source_target_pairs={{0,128},{8,904},{16,144},{24,920},{32,160},{40,936},{48,176},{56,9... | collective-permute-start | bytes 1769480 | tf_op jit(solution)/shard_map/ppermute | solution.py:244
  96.4 1.6 copy-start.14
  100.1 14.1 %copy-start.3 = (bf16[2304,128]{1,0:T(8,128)(2,1)}, bf16[2304,128]{1,0:T(8,128)(2,1)S(1)}, u32[]{:S(2)}) copy-start(bf16[2304,128]{1,0:T(8,128)(2,1)S(1)} %get-tuple-element.44.own_ref) | copy-start | bytes 1769476
  100.1 14.1 %copy-start.5 = (bf16[2304,128]{1,0:T(8,128)(2,1)}, bf16[2304,128]{1,0:T(8,128)(2,1)S(1)}, u32[]{:S(2)}) copy-start(bf16[2304,128]{1,0:T(8,128)(2,1)S(1)} %get-tuple-element.45) | copy-start | bytes 1769476
  100.1 14.1 %copy-start.7 = (bf16[2304,128]{1,0:T(8,128)(2,1)}, bf16[2304,128]{1,0:T(8,128)(2,1)S(1)}, u32[]{:S(2)}) copy-start(bf16[2304,128]{1,0:T(8,128)(2,1)S(1)} %get-tuple-element.47) | copy-start | bytes 1769476
  100.1 14.1 %copy-start.9 = (bf16[2304,128]{1,0:T(8,128)(2,1)}, bf16[2304,128]{1,0:T(8,128)(2,1)S(1)}, u32[]{:S(2)}) copy-start(bf16[2304,128]{1,0:T(8,128)(2,1)S(1)} %get-tuple-element.46) | copy-start | bytes 1769476
  100.1 13.1 %collective-permute-start.4 = (bf16[2304,128]{1,0:T(8,128)(2,1)S(1)}, bf16[2304,128]{1,0:T(8,128)(2,1)S(1)}, u32[]{:S(2)}, u32[]{:S(2)}) collective-permute-start(bf16[2304,128]{1,0:T(8,128)(2,1)S(1)} %get-tuple-element.49), channel_id=1, source_target_pairs={{0,896},{8,136},{16,912},{24,152},{32,928},{40,168},{48,944},{56,1... | collective-permute-start | bytes 1769480 | tf_op jit(solution)/shard_map/ppermute | solution.py:244
  105.0 23.9 %collective-permute-start.1 = (bf16[2304,128]{1,0:T(8,128)(2,1)}, bf16[2304,128]{1,0:T(8,128)(2,1)}, u32[]{:S(2)}, u32[]{:S(2)}) collective-permute-start(bf16[2304,128]{1,0:T(8,128)(2,1)} %add_convert_fusion.4), channel_id=1, source_target_pairs={{0,128},{8,904},{16,144},{24,920},{32,160},{40,936},{48,176},{56,9... | collective-permute-start | bytes 1769480 | tf_op jit(solution)/shard_map/ppermute | solution.py:244
  114.2 19.4 %collective-permute-start.5 = (bf16[2304,128]{1,0:T(8,128)(2,1)}, bf16[2304,128]{1,0:T(8,128)(2,1)}, u32[]{:S(2)}, u32[]{:S(2)}) collective-permute-start(bf16[2304,128]{1,0:T(8,128)(2,1)} %add_convert_fusion.1), channel_id=1, source_target_pairs={{0,896},{8,136},{16,912},{24,152},{32,928},{40,168},{48,944},{56,1... | collective-permute-start | bytes 1769480 | tf_op jit(solution)/shard_map/ppermute | solution.py:244
  117.4 1.0 copy-start.2
  120.7 8.2 %copy-start.10 = (bf16[2304,128]{1,0:T(8,128)(2,1)S(1)}, bf16[2304,128]{1,0:T(8,128)(2,1)}, u32[]{:S(2)}) copy-start(bf16[2304,128]{1,0:T(8,128)(2,1)} %copy-done.9) | copy-start | bytes 1769476
  120.7 41.3 %all-to-all-start.1 = ((bf16[128,2,2176]{2,1,0:T(2,128)(2,1)}), bf16[128,2,2176]{2,1,0:T(2,128)(2,1)}, u32[]{:S(2)}, u32[]{:S(2)}) async-start(bf16[128,2,2176]{2,1,0:T(2,128)(2,1)} %reshape.16), calls=%async_computation.1 | async-start | bytes 2228224 | tf_op jit(solution)/shard_map/all_to_all | solution.py:234
  128.9 4.7 %copy-start.8 = (bf16[2304,128]{1,0:T(8,128)(2,1)S(1)}, bf16[2304,128]{1,0:T(8,128)(2,1)}, u32[]{:S(2)}) copy-start(bf16[2304,128]{1,0:T(8,128)(2,1)} %copy-done.7) | copy-start | bytes 1769476
  130.2 12.1 %copy-start.6 = (bf16[2304,128]{1,0:T(8,128)(2,1)S(1)}, bf16[2304,128]{1,0:T(8,128)(2,1)}, u32[]{:S(2)}) copy-start(bf16[2304,128]{1,0:T(8,128)(2,1)} %copy-done.5) | copy-start | bytes 1769476
  130.2 12.0 %collective-permute-start.2 = (bf16[2304,128]{1,0:T(8,128)(2,1)S(1)}, bf16[2304,128]{1,0:T(8,128)(2,1)S(1)}, u32[]{:S(2)}, u32[]{:S(2)}) collective-permute-start(bf16[2304,128]{1,0:T(8,128)(2,1)S(1)} %add_convert_fusion.3), channel_id=1, source_target_pairs={{0,128},{8,904},{16,144},{24,920},{32,160},{40,936},{48,176},{56,9... | collective-permute-start | bytes 1769480 | tf_op jit(solution)/shard_map/ppermute | solution.py:244
  134.9 29.7 %collective-permute-start.6 = (bf16[2304,128]{1,0:T(8,128)(2,1)S(1)}, bf16[2304,128]{1,0:T(8,128)(2,1)S(1)}, u32[]{:S(2)}, u32[]{:S(2)}) collective-permute-start(bf16[2304,128]{1,0:T(8,128)(2,1)S(1)} %add_convert_fusion), channel_id=1, source_target_pairs={{0,896},{8,136},{16,912},{24,152},{32,928},{40,168},{48,944},{56,1... | collective-permute-start | bytes 1769480 | tf_op jit(solution)/shard_map/ppermute | solution.py:244
  143.3 20.3 %copy-start.11 = (bf16[256,128]{1,0:T(8,128)(2,1)S(1)}, bf16[256,128]{1,0:T(8,128)(2,1)}, u32[]{:S(2)}) copy-start(bf16[256,128]{1,0:T(8,128)(2,1)} %get-tuple-element.39.spread_ref) | copy-start | bytes 196612
  143.3 20.3 %copy-start.12 = (s32[16,8]{0,1:T(8,128)S(1)}, s32[16,8]{0,1:T(8,128)}, u32[]{:S(2)}) copy-start(s32[16,8]{0,1:T(8,128)} %param.9) | copy-start | bytes 1540
  143.3 20.3 %copy-start.13 = (bf16[16,8]{0,1:T(8,128)(2,1)S(1)}, bf16[16,8]{0,1:T(8,128)(2,1)}, u32[]{:S(2)}) copy-start(bf16[16,8]{0,1:T(8,128)(2,1)} %param.10) | copy-start | bytes 772
  143.3 21.3 %copy-start.4 = (bf16[2304,128]{1,0:T(8,128)(2,1)S(1)}, bf16[2304,128]{1,0:T(8,128)(2,1)}, u32[]{:S(2)}) copy-start(bf16[2304,128]{1,0:T(8,128)(2,1)} %copy-done.3) | copy-start | bytes 1769476
  143.3 21.3 %collective-permute-start.3 = (bf16[2304,128]{1,0:T(8,128)(2,1)}, bf16[2304,128]{1,0:T(8,128)(2,1)S(1)}, u32[]{:S(2)}, u32[]{:S(2)}) collective-permute-start(bf16[2304,128]{1,0:T(8,128)(2,1)} %add_convert_fusion.2), channel_id=1, source_target_pairs={{0,128},{8,904},{16,144},{24,920},{32,160},{40,936},{48,176},{56,9... | collective-permute-start | bytes 1769480 | tf_op jit(solution)/shard_map/ppermute | solution.py:244

commit v5 on v4

--- a/solution.py
+++ b/solution.py
@@ -7,7 +7,7 @@
 
 PLANE = ("node", "local")
 BF16, F32, I32 = jnp.bfloat16, jnp.float32, jnp.int32
-VMEM_LIMIT, VMEM_MOST = 24 << 20, 60 << 20
+VMEM_LIMIT, VMEM_MOST = 24 << 20, 62 << 20
 CAP, PIECES, WIDE = 2, 8, 256
 BLOCK = CAP * PIECES
 GROUP = 16
@@ -159,19 +159,36 @@
     store_part(down, gate_up, far_ref)
 
 
-def near_body(order_ref, rows_ref, hidden_ref, slopes_ref, *refs):
-    near, down_ref = refs[:-1], refs[-1]
+def near_body(order_ref, rows_hbm, hidden_ref, slopes_ref, *refs):
+    near_hbm, (rows_ref, down_ref, packed_ref, load_sems, store_sems) = refs[:-5], refs[-5:]
+    loads = [
+        pltpu.make_async_copy(rows_hbm.at[part], rows_ref.at[part], load_sems.at[part])
+        for part in range(2)
+    ]
+    loads[1].start()
+    loads[0].start()
     shards = order_ref.shape[0]
     share = hidden_ref.shape[1] // shards
+    loads[1].wait()
     for n in range(PIECES):
         columns = slice(n * WIDE, (n + 1) * WIDE)
         down_ref[:, columns] = dot(hidden_ref[...], rows_ref[1, :, columns], 0, 0).astype(BF16)
-    for i, offset in enumerate((*range(shards // 2), *range(shards // 2 + 1, shards))):
-        target = order_ref[offset]
-        columns = pl.ds(pl.multiple_of(target * WIDE, WIDE), WIDE)
-        gate_up = dot(rows_ref[0, :, columns], slopes_ref[...], 0, 0).astype(BF16)
-        down = down_ref[pl.ds(pl.multiple_of(target * share, 16), share), :]
-        store_part(down, gate_up, near[i])
+    loads[0].wait()
+    stores = []
+    far = shards // 2
+    for distance in range(far - 1, -1, -1):
+        for offset in sorted({-distance % shards, distance}, reverse=True):
+            target = order_ref[offset]
+            columns = pl.ds(pl.multiple_of(target * WIDE, WIDE), WIDE)
+            gate_up = dot(rows_ref[0, :, columns], slopes_ref[...], 0, 0).astype(BF16)
+            down = down_ref[pl.ds(pl.multiple_of(target * share, 16), share), :]
+            i = offset - (offset > far)
+            store_part(down, gate_up, packed_ref.at[i])
+            store = pltpu.make_async_copy(packed_ref.at[i], near_hbm[i], store_sems.at[i])
+            store.start()
+            stores.append(store)
+    for store in stores:
+        store.wait()
 
 
 def rows_body(slopes_ref, score_ref, gate_ref, up_ref, out_ref):
@@ -301,21 +318,27 @@
             pltpu.SemaphoreType.DMA((3,)),
         ),
         cost=cost(4 * product, 10 << 20),
-        limit=49 << 20,
+        limit=VMEM_MOST,
     )(order, arrived, w_gate, w_up, w_down)
     forward, backward = ring(0), ring(1)
     first = forward(far)
     near = call(
         near_body,
         [shaped(packed_rows, LANES)] * (reps - 1),
-        [smem] + whole(3),
-        whole(reps - 1),
-        scratch=(pltpu.VMEM((hidden, width), BF16),),
+        [smem, hbm] + whole(2),
+        [hbm] * (reps - 1),
+        scratch=(
+            pltpu.VMEM((2, slots, width), BF16),
+            pltpu.VMEM((hidden, width), BF16),
+            pltpu.VMEM((reps - 1, packed_rows, LANES), BF16),
+            pltpu.SemaphoreType.DMA((2,)),
+            pltpu.SemaphoreType.DMA((reps - 1,)),
+        ),
         cost=cost(3 * product, 8 << 20),
+        limit=VMEM_MOST,
     )(order, routed, hidden_act, slopes)
-    ahead = add(near[3], first)
-    slopes, score, _ = lax.optimization_barrier((slopes, score, ahead))
-    ahead, behind = forward(ahead), backward(near[-3])
+    slopes, score, _ = lax.optimization_barrier((slopes, score, near[-3]))
+    ahead, behind = forward(add(near[3], first)), backward(near[-3])
     ahead, behind = forward(add(near[2], ahead)), backward(add(near[-2], behind))
     ahead, behind = forward(add(near[1], ahead)), backward(add(near[-1], behind))
 
@@ -325,6 +348,7 @@
         whole(4),
         whole(1)[0],
         cost=cost(2 * product, 5 << 20),
+        limit=VMEM_MOST,
     )(slopes, score, w_gate, w_up)
     returned = exchange(rows.reshape(experts, CAP, width + LANES)).reshape(slots, width + LANES)
     grad_tokens, grad_gates = call(

time: 168 us -> 171 us (1.018)
  the two profiles are of different devices: /device:TPU:1 before, /device:TPU:8 now
where the time goes in v5:
time: 171 us; the launch traced here: 170 us
  waiting for transfers between devices  82.8 us (48%)
  starting transfers between devices  56.8 us (33%)
  Pallas kernels  23.6 us (14%)
  local copies, waits for them, and re-layouts  3.85 us (2%)
  other arithmetic  2.14 us (1%)
    all_to_all x2, waiting for transfers between devices, exchange(): lax.all_to_all(blocks, PLANE, split_axis=0, concat_axis=0, tiled=True)  51.3 us
    all_to_all x2, starting transfers between devices, exchange(): lax.all_to_all(blocks, PLANE, split_axis=0, concat_axis=0, tiled=True)  33.2 us
    ppermute x7, waiting for transfers between devices, ring(): return lambda message: lax.ppermute(message, ('rep', 'node'), pairs)  31.5 us
    ppermute x7, starting transfers between devices, ring(): return lambda message: lax.ppermute(message, ('rep', 'node'), pairs)  23.6 us
    pallas_call x1, Pallas kernels, shards(): call(expert_body, (shaped(2, slots, width), shaped(slots, hidden), shaped...  7.09 us
    pallas_call x1, Pallas kernels, shards(): call(near_body, [shaped(packed_rows, LANES)] * (reps - 1), [smem, hbm] +...  5.3 us
    pallas_call x1, Pallas kernels, shards(): call(route_body, (shaped(experts, 2 * BLOCK, WIDE), shaped(slots, LANES))...  4.97 us
    pallas_call x1, Pallas kernels, shards(): call(rows_body, shaped(slots, width + LANES), whole(4), whole(1)[0], cost...  4.35 us
  transfers between devices with their start and end apart: 9, of which 4 were waited for; matrix products, arithmetic and copies ran while one was open for 3% of the time, Pallas kernels for 6%

profile of v5, /device:TPU:8, one launch (start us, length us, event | category | flops | bytes accessed | tf_op | source)
XLA Modules:
  0.0 170.1 jit_solution(15544825406509221103)
XLA Ops:
  0.6 5.0 %shard_map.110 = (bf16[128,32,256]{2,1,0:T(8,128)(2,1)}, bf16[256,128]{1,0:T(8,128)(2,1)}) custom-call(s32[8,16]{1,0:T(8,128)} %bitcast.9, bf16[8,16]{1,0:T(8,128)(2,1)} %bitcast.11, bf16[16,2048]{1,0:T(8,128)(2,1)} %tokens_hbm.1, bf16[16,2048]{1,0:T(8,128)(2,1)} %grads_hbm.1), custom_call_target="tpu_custom_call" | custom-call | flops 268435456 | bytes 2097152 | tf_op jit(solution)/shard_map/pallas_call | solution.py:281
  5.6 25.2 %all-to-all-start = ((bf16[128,32,256]{2,1,0:T(8,128)(2,1)}), bf16[128,32,256]{2,1,0:T(8,128)(2,1)}, u32[]{:S(2)}, u32[]{:S(2)}) async-start(bf16[128,32,256]{2,1,0:T(8,128)(2,1)} %get-tuple-element.29), calls=%async_computation | async-start | bytes 4194304 | tf_op jit(solution)/shard_map/all_to_all | solution.py:251
  30.8 0.5 and_select_fusion.order_ref
  31.3 51.3 %all-to-all-done.arrived_hbm = bf16[128,32,256]{2,1,0:T(8,128)(2,1)} async-done(((bf16[128,32,256]{2,1,0:T(8,128)(2,1)}), bf16[128,32,256]{2,1,0:T(8,128)(2,1)}, u32[]{:S(2)}, u32[]{:S(2)}) %all-to-all-start) | async-done | bytes 2097184 | tf_op jit(solution)/shard_map/all_to_all | solution.py:251
  82.6 7.1 %shard_map.111 = (bf16[2,256,2048]{2,1,0:T(8,128)(2,1)}, bf16[256,384]{1,0:T(8,128)(2,1)}, bf16[256,768]{1,0:T(8,128)(2,1)}, bf16[256,128]{1,0:T(8,128)(2,1)}, bf16[2304,128]{1,0:T(8,128)(2,1)}) custom-call(s32[8]{0:T(128)} %and_select_fusion.order_ref, bf16[128,32,256]{2,1,0:T(8,128)(2,1)} %all-to-all-done.arrived_hbm, bf16[2048,384]{1,0:T(8,128)(2,1)} %bitcast.13, ...), custom_call_target="tpu_custom_call" | custom-call | flops 1610612736 | bytes 10485760 | tf_op jit(solution)/shard_map/pallas_call | solution.py:300
  89.7 2.5 %collective-permute-start = (bf16[2304,128]{1,0:T(8,128)(2,1)}, bf16[2304,128]{1,0:T(8,128)(2,1)S(1)}, u32[]{:S(2)}, u32[]{:S(2)}) collective-permute-start(bf16[2304,128]{1,0:T(8,128)(2,1)} %get-tuple-element.47), channel_id=1, source_target_pairs={{0,128},{8,904},{16,144},{24,920},{32,160},{40,936},{48,176},{56,9... | collective-permute-start | bytes 1769480 | tf_op jit(solution)/shard_map/ppermute | solution.py:261
  92.2 5.3 %shard_map.112 = (bf16[2304,128]{1,0:T(8,128)(2,1)}, bf16[2304,128]{1,0:T(8,128)(2,1)}, bf16[2304,128]{1,0:T(8,128)(2,1)}, bf16[2304,128]{1,0:T(8,128)(2,1)}, bf...) custom-call(s32[8]{0:T(128)} %and_select_fusion.order_ref, ...), custom_call_target="tpu_custom_call" | custom-call | flops 1207959552 | bytes 8388608 | tf_op jit(solution)/shard_map/pallas_call | solution.py:325
  97.6 4.6 %collective-permute-start.4 = (bf16[2304,128]{1,0:T(8,128)(2,1)}, bf16[2304,128]{1,0:T(8,128)(2,1)S(1)}, u32[]{:S(2)}, u32[]{:S(2)}) collective-permute-start(bf16[2304,128]{1,0:T(8,128)(2,1)} %get-tuple-element.35), channel_id=1, source_target_pairs={{0,896},{8,136},{16,912},{24,152},{32,928},{40,168},{48,944},{56,1... | collective-permute-start | bytes 1769480 | tf_op jit(solution)/shard_map/ppermute | solution.py:261
  102.1 4.3 %shard_map.113 = bf16[256,2176]{1,0:T(8,128)(2,1)} custom-call(bf16[256,768]{1,0:T(8,128)(2,1)} %get-tuple-element.36.slopes_ref, bf16[256,128]{1,0:T(8,128)(2,1)} %get-tuple-element.37.score_ref, bf16[2048,384]{1,0:T(8,128)(2,1)} %bitcast.14, bf16[2048,384]{1,0:T(8,128)(2,1)} %bitcast.16), custom_call_target="tpu_custom_call" | custom-call | flops 805306368 | bytes 5242880 | tf_op jit(solution)/shard_map/pallas_call | solution.py:345
  106.5 2.3 %reshape.16 = bf16[128,2,2176]{2,1,0:T(2,128)(2,1)} reshape(bf16[256,2176]{1,0:T(8,128)(2,1)} %shard_map.113) | data formatting | bytes 2228224 | tf_op jit(solution)/shard_map/reshape | solution.py:353
  108.8 8.0 %all-to-all-start.1 = ((bf16[128,2,2176]{2,1,0:T(2,128)(2,1)}), bf16[128,2,2176]{2,1,0:T(2,128)(2,1)}, u32[]{:S(2)}, u32[]{:S(2)}) async-start(bf16[128,2,2176]{2,1,0:T(2,128)(2,1)} %reshape.16), calls=%async_computation.1 | async-start | bytes 2228224 | tf_op jit(solution)/shard_map/all_to_all | solution.py:251
  116.8 0.2 add_convert_fusion.4
  117.0 2.1 %collective-permute-start.1 = (bf16[2304,128]{1,0:T(8,128)(2,1)S(1)}, bf16[2304,128]{1,0:T(8,128)(2,1)S(1)}, u32[]{:S(2)}, u32[]{:S(2)}) collective-permute-start(bf16[2304,128]{1,0:T(8,128)(2,1)S(1)} %add_convert_fusion.4), channel_id=1, source_target_pairs={{0,128},{8,904},{16,144},{24,920},{32,160},{40,936},{48,176},{56,9... | collective-permute-start | bytes 1769480 | tf_op jit(solution)/shard_map/ppermute | solution.py:261
  119.2 5.3 %collective-permute-start.5 = (bf16[2304,128]{1,0:T(8,128)(2,1)S(1)}, bf16[2304,128]{1,0:T(8,128)(2,1)S(1)}, u32[]{:S(2)}, u32[]{:S(2)}) collective-permute-start(bf16[2304,128]{1,0:T(8,128)(2,1)S(1)} %add_convert_fusion.1), channel_id=1, source_target_pairs={{0,896},{8,136},{16,912},{24,152},{32,928},{40,168},{48,944},{56,1... | collective-permute-start | bytes 1769480 | tf_op jit(solution)/shard_map/ppermute | solution.py:261
  124.5 10.9 %collective-permute-done.1 = bf16[2304,128]{1,0:T(8,128)(2,1)S(1)} collective-permute-done((bf16[2304,128]{1,0:T(8,128)(2,1)S(1)}, bf16[2304,128]{1,0:T(8,128)(2,1)S(1)}, u32[]{:S(2)}, u32[]{:S(2)}) %collective-permute-start.1) | collective-permute-done | bytes 589856 | tf_op jit(solution)/shard_map/ppermute | solution.py:261
  135.5 2.1 %collective-permute-start.2 = (bf16[2304,128]{1,0:T(8,128)(2,1)S(1)}, bf16[2304,128]{1,0:T(8,128)(2,1)S(1)}, u32[]{:S(2)}, u32[]{:S(2)}) collective-permute-start(bf16[2304,128]{1,0:T(8,128)(2,1)S(1)} %add_convert_fusion.3), channel_id=1, source_target_pairs={{0,128},{8,904},{16,144},{24,920},{32,160},{40,936},{48,176},{56,9... | collective-permute-start | bytes 1769480 | tf_op jit(solution)/shard_map/ppermute | solution.py:261
  137.8 5.1 %collective-permute-start.6 = (bf16[2304,128]{1,0:T(8,128)(2,1)S(1)}, bf16[2304,128]{1,0:T(8,128)(2,1)S(1)}, u32[]{:S(2)}, u32[]{:S(2)}) collective-permute-start(bf16[2304,128]{1,0:T(8,128)(2,1)S(1)} %add_convert_fusion), channel_id=1, source_target_pairs={{0,896},{8,136},{16,912},{24,152},{32,928},{40,168},{48,944},{56,1... | collective-permute-start | bytes 1769480 | tf_op jit(solution)/shard_map/ppermute | solution.py:261
  142.9 11.9 %collective-permute-done.2 = bf16[2304,128]{1,0:T(8,128)(2,1)S(1)} collective-permute-done((bf16[2304,128]{1,0:T(8,128)(2,1)S(1)}, bf16[2304,128]{1,0:T(8,128)(2,1)S(1)}, u32[]{:S(2)}, u32[]{:S(2)}) %collective-permute-start.2) | collective-permute-done | bytes 589856 | tf_op jit(solution)/shard_map/ppermute | solution.py:261
  154.8 1.0 add_convert_fusion.2
  155.8 2.1 %collective-permute-start.3 = (bf16[2304,128]{1,0:T(8,128)(2,1)}, bf16[2304,128]{1,0:T(8,128)(2,1)S(1)}, u32[]{:S(2)}, u32[]{:S(2)}) collective-permute-start(bf16[2304,128]{1,0:T(8,128)(2,1)} %add_convert_fusion.2), channel_id=1, source_target_pairs={{0,128},{8,904},{16,144},{24,920},{32,160},{40,936},{48,176},{56,9... | collective-permute-start | bytes 1769480 | tf_op jit(solution)/shard_map/ppermute | solution.py:261
  157.9 1.5 reshape.17.returned_ref
  159.4 1.0 shard_map.114
  160.4 8.8 %collective-permute-done.3.ahead_ref = bf16[2304,128]{1,0:T(8,128)(2,1)S(1)} collective-permute-done((bf16[2304,128]{1,0:T(8,128)(2,1)}, bf16[2304,128]{1,0:T(8,128)(2,1)S(1)}, u32[]{:S(2)}, u32[]{:S(2)}) %collective-permute-start.3) | collective-permute-done | bytes 589856 | tf_op jit(solution)/shard_map/ppermute | solution.py:261
  169.1 1.0 shard_map.115
  (26 shorter events, 0.5 us)
Async XLA Ops:
  5.6 77.0 %all-to-all-start = ((bf16[128,32,256]{2,1,0:T(8,128)(2,1)}), bf16[128,32,256]{2,1,0:T(8,128)(2,1)}, u32[]{:S(2)}, u32[]{:S(2)}) async-start(bf16[128,32,256]{2,1,0:T(8,128)(2,1)} %get-tuple-element.29), calls=%async_computation | async-start | bytes 4194304 | tf_op jit(solution)/shard_map/all_to_all | solution.py:251
  89.7 27.0 %collective-permute-start = (bf16[2304,128]{1,0:T(8,128)(2,1)}, bf16[2304,128]{1,0:T(8,128)(2,1)S(1)}, u32[]{:S(2)}, u32[]{:S(2)}) collective-permute-start(bf16[2304,128]{1,0:T(8,128)(2,1)} %get-tuple-element.47), channel_id=1, source_target_pairs={{0,128},{8,904},{16,144},{24,920},{32,160},{40,936},{48,176},{56,9... | collective-permute-start | bytes 1769480 | tf_op jit(solution)/shard_map/ppermute | solution.py:261
  97.6 21.5 %collective-permute-start.4 = (bf16[2304,128]{1,0:T(8,128)(2,1)}, bf16[2304,128]{1,0:T(8,128)(2,1)S(1)}, u32[]{:S(2)}, u32[]{:S(2)}) collective-permute-start(bf16[2304,128]{1,0:T(8,128)(2,1)} %get-tuple-element.35), channel_id=1, source_target_pairs={{0,896},{8,136},{16,912},{24,152},{32,928},{40,168},{48,944},{56,1... | collective-permute-start | bytes 1769480 | tf_op jit(solution)/shard_map/ppermute | solution.py:261
  108.8 8.0 %copy-start.8 = (bf16[2304,128]{1,0:T(8,128)(2,1)S(1)}, bf16[2304,128]{1,0:T(8,128)(2,1)}, u32[]{:S(2)}) copy-start(bf16[2304,128]{1,0:T(8,128)(2,1)} %get-tuple-element.46) | copy-start | bytes 1769476
  108.8 49.1 %all-to-all-start.1 = ((bf16[128,2,2176]{2,1,0:T(2,128)(2,1)}), bf16[128,2,2176]{2,1,0:T(2,128)(2,1)}, u32[]{:S(2)}, u32[]{:S(2)}) async-start(bf16[128,2,2176]{2,1,0:T(2,128)(2,1)} %reshape.16), calls=%async_computation.1 | async-start | bytes 2228224 | tf_op jit(solution)/shard_map/all_to_all | solution.py:251
  116.8 2.3 %copy-start.7 = (bf16[2304,128]{1,0:T(8,128)(2,1)S(1)}, bf16[2304,128]{1,0:T(8,128)(2,1)}, u32[]{:S(2)}) copy-start(bf16[2304,128]{1,0:T(8,128)(2,1)} %get-tuple-element.49) | copy-start | bytes 1769476
  117.0 18.4 %copy-start.6 = (bf16[2304,128]{1,0:T(8,128)(2,1)S(1)}, bf16[2304,128]{1,0:T(8,128)(2,1)}, u32[]{:S(2)}) copy-start(bf16[2304,128]{1,0:T(8,128)(2,1)} %get-tuple-element.45) | copy-start | bytes 1769476
  117.0 18.4 %collective-permute-start.1 = (bf16[2304,128]{1,0:T(8,128)(2,1)S(1)}, bf16[2304,128]{1,0:T(8,128)(2,1)S(1)}, u32[]{:S(2)}, u32[]{:S(2)}) collective-permute-start(bf16[2304,128]{1,0:T(8,128)(2,1)S(1)} %add_convert_fusion.4), channel_id=1, source_target_pairs={{0,128},{8,904},{16,144},{24,920},{32,160},{40,936},{48,176},{56,9... | collective-permute-start | bytes 1769480 | tf_op jit(solution)/shard_map/ppermute | solution.py:261
  119.2 18.4 %copy-start.5 = (bf16[2304,128]{1,0:T(8,128)(2,1)S(1)}, bf16[2304,128]{1,0:T(8,128)(2,1)}, u32[]{:S(2)}) copy-start(bf16[2304,128]{1,0:T(8,128)(2,1)} %get-tuple-element.48) | copy-start | bytes 1769476
  119.2 18.4 %collective-permute-start.5 = (bf16[2304,128]{1,0:T(8,128)(2,1)S(1)}, bf16[2304,128]{1,0:T(8,128)(2,1)S(1)}, u32[]{:S(2)}, u32[]{:S(2)}) collective-permute-start(bf16[2304,128]{1,0:T(8,128)(2,1)S(1)} %add_convert_fusion.1), channel_id=1, source_target_pairs={{0,896},{8,136},{16,912},{24,152},{32,928},{40,168},{48,944},{56,1... | collective-permute-start | bytes 1769480 | tf_op jit(solution)/shard_map/ppermute | solution.py:261
  135.5 19.3 %copy-start.4 = (bf16[2304,128]{1,0:T(8,128)(2,1)S(1)}, bf16[2304,128]{1,0:T(8,128)(2,1)}, u32[]{:S(2)}) copy-start(bf16[2304,128]{1,0:T(8,128)(2,1)} %get-tuple-element.44) | copy-start | bytes 1769476
  135.5 19.3 %collective-permute-start.2 = (bf16[2304,128]{1,0:T(8,128)(2,1)S(1)}, bf16[2304,128]{1,0:T(8,128)(2,1)S(1)}, u32[]{:S(2)}, u32[]{:S(2)}) collective-permute-start(bf16[2304,128]{1,0:T(8,128)(2,1)S(1)} %add_convert_fusion.3), channel_id=1, source_target_pairs={{0,128},{8,904},{16,144},{24,920},{32,160},{40,936},{48,176},{56,9... | collective-permute-start | bytes 1769480 | tf_op jit(solution)/shard_map/ppermute | solution.py:261
  137.8 22.6 %collective-permute-start.6 = (bf16[2304,128]{1,0:T(8,128)(2,1)S(1)}, bf16[2304,128]{1,0:T(8,128)(2,1)S(1)}, u32[]{:S(2)}, u32[]{:S(2)}) collective-permute-start(bf16[2304,128]{1,0:T(8,128)(2,1)S(1)} %add_convert_fusion), channel_id=1, source_target_pairs={{0,896},{8,136},{16,912},{24,152},{32,928},{40,168},{48,944},{56,1... | collective-permute-start | bytes 1769480 | tf_op jit(solution)/shard_map/ppermute | solution.py:261
  155.8 3.6 %copy-start.1 = (bf16[256,128]{1,0:T(8,128)(2,1)S(1)}, bf16[256,128]{1,0:T(8,128)(2,1)}, u32[]{:S(2)}) copy-start(bf16[256,128]{1,0:T(8,128)(2,1)} %get-tuple-element.38.spread_ref) | copy-start | bytes 196612
  155.8 3.6 %copy-start.2 = (s32[16,8]{0,1:T(8,128)S(1)}, s32[16,8]{0,1:T(8,128)}, u32[]{:S(2)}) copy-start(s32[16,8]{0,1:T(8,128)} %param.9) | copy-start | bytes 1540
  155.8 3.6 %copy-start.3 = (bf16[16,8]{0,1:T(8,128)(2,1)S(1)}, bf16[16,8]{0,1:T(8,128)(2,1)}, u32[]{:S(2)}) copy-start(bf16[16,8]{0,1:T(8,128)(2,1)} %param.10) | copy-start | bytes 772
  155.8 13.3 %copy-start = (bf16[2304,128]{1,0:T(8,128)(2,1)S(1)}, bf16[2304,128]{1,0:T(8,128)(2,1)}, u32[]{:S(2)}) copy-start(bf16[2304,128]{1,0:T(8,128)(2,1)} %get-tuple-element.43.own_ref) | copy-start | bytes 1769476
  155.8 13.3 %collective-permute-start.3 = (bf16[2304,128]{1,0:T(8,128)(2,1)}, bf16[2304,128]{1,0:T(8,128)(2,1)S(1)}, u32[]{:S(2)}, u32[]{:S(2)}) collective-permute-start(bf16[2304,128]{1,0:T(8,128)(2,1)} %add_convert_fusion.2), channel_id=1, source_target_pairs={{0,128},{8,904},{16,144},{24,920},{32,160},{40,936},{48,176},{56,9... | collective-permute-start | bytes 1769480 | tf_op jit(solution)/shard_map/ppermute | solution.py:261

commit v6 on v3

--- a/solution.py
+++ b/solution.py
@@ -7,7 +7,7 @@
 
 PLANE = ("node", "local")
 BF16, F32, I32 = jnp.bfloat16, jnp.float32, jnp.int32
-VMEM_LIMIT = 48 << 20
+VMEM_LEAST, VMEM_LIMIT, VMEM_MOST = 16 << 20, 50 << 20, 62 << 20
 CAP, PIECES, WIDE = 2, 8, 256
 BLOCK = CAP * PIECES
 GROUP = 16
@@ -29,7 +29,7 @@
     return [pl.BlockSpec(memory_space=pltpu.VMEM)] * count
 
 
-def call(body, outs, in_specs, out_specs, scratch=(), cost=None):
+def call(body, outs, in_specs, out_specs, scratch=(), cost=None, limit=VMEM_LIMIT):
     return pl.pallas_call(
         body,
         out_shape=outs,
@@ -37,7 +37,7 @@
         out_specs=out_specs,
         scratch_shapes=scratch,
         cost_estimate=cost,
-        compiler_params=pltpu.CompilerParams(vmem_limit_bytes=VMEM_LIMIT),
+        compiler_params=pltpu.CompilerParams(vmem_limit_bytes=limit),
     )
 
 
@@ -90,11 +90,20 @@
             )
 
 
+def store_part(down, gate_up, ref):
+    at = 0
+    for part in (gate_up, down):
+        rows = part.shape[0]
+        for b in range(part.shape[1] // LANES):
+            ref[at : at + rows, :] = part[:, b * LANES : (b + 1) * LANES]
+            at += rows
+
+
 def expert_body(
     order_ref, arrived_ref, gate_hbm, up_hbm, down_hbm,
-    slopes_ref, score_ref, far_ahead, far_behind, *refs,
+    slopes_ref, score_ref, *refs,
 ):
-    near, (rows_ref, w_gate, w_up, w_down, down_ref, load_sems) = refs[:-6], refs[-6:]
+    parts, (rows_ref, w_gate, w_up, w_down, down_ref, load_sems) = refs[:-6], refs[-6:]
     loads = [
         pltpu.make_async_copy(source, target, load_sems.at[i])
         for i, (source, target) in enumerate(
@@ -136,27 +145,12 @@
     for n in range(PIECES):
         columns = slice(n * WIDE, (n + 1) * WIDE)
         down_ref[:, columns] = dot(hidden_act, rows_ref[1, :, columns], 0, 0).astype(BF16)
-    far = shards // 2
-    for offset in (far, *range(far), *range(far + 1, shards)):
+    for offset in range(shards):
         target = order_ref[offset]
         columns = pl.ds(pl.multiple_of(target * WIDE, WIDE), WIDE)
         gate_up = dot(rows_ref[0, :, columns], slopes_ref[...], 0, 0).astype(BF16)
         down = down_ref[pl.ds(pl.multiple_of(target * share, 16), share), :]
-        pieces = [gate_up[:, b * LANES : (b + 1) * LANES] for b in range(2 * hidden // LANES)]
-        pieces += [down[:, b * LANES : (b + 1) * LANES] for b in range(down.shape[1] // LANES)]
-        at = 0
-        for piece in pieces:
-            rows = piece.shape[0]
-            if offset != far:
-                near[offset - (offset > far)][at : at + rows, :] = piece
-            else:
-                split = far_ahead.shape[0]
-                first = min(max(split - at, 0), rows)
-                if first:
-                    far_ahead[at : at + first, :] = piece[:first]
-                if first < rows:
-                    far_behind[at + first - split : at + rows - split, :] = piece[first:]
-            at += rows
+        store_part(down, gate_up, parts[offset])
 
 
 def rows_body(slopes_ref, score_ref, gate_ref, up_ref, out_ref):
@@ -233,22 +227,6 @@
     return (left.astype(F32) + right.astype(F32)).astype(BF16)
 
 
-def reduce_scatter(far_ahead, far_behind, near):
-    forward, backward = ring(0), ring(1)
-    half = far_ahead.shape[0]
-    ahead, behind = forward(far_ahead), backward(far_behind)
-    last = len(near) // 2
-    for d in range(last, 0, -1):
-        to_ahead, to_behind = near[d], near[len(near) - d]
-        if d == last:
-            to_ahead = jnp.concatenate((add(to_ahead[:half], ahead), to_ahead[half:]))
-            to_behind = jnp.concatenate((to_behind[:half], add(to_behind[half:], behind)))
-        else:
-            to_ahead, to_behind = add(to_ahead, ahead), add(to_behind, behind)
-        ahead, behind = forward(to_ahead), backward(to_behind)
-    return near[0], ahead, behind
-
-
 def shards(tokens, grads_out, expert_ids, gates, w_gate, w_up, w_down):
     experts = lax.axis_size("node") * lax.axis_size("local")
     reps = lax.axis_size("rep")
@@ -261,7 +239,7 @@
     packed_rows = (2 * hidden * (width // reps) + (hidden // reps) * width) // LANES
     product = 2 * slots * width * hidden
 
-    hbm = pl.BlockSpec(memory_space=pl.ANY)
+    hbm = pl.BlockSpec(memory_space=pltpu.HBM)
     outgoing, spread = call(
         route_body,
         (shaped(experts, 2 * BLOCK, WIDE), shaped(slots, LANES)),
@@ -274,21 +252,21 @@
             pltpu.SemaphoreType.DMA((3,)),
         ),
         cost=cost(4 * slots * LANES * width, 4 * slots * width),
+        limit=VMEM_MOST,
     )(ids_t, gates_t, tokens, grads_out)
     arrived = exchange(outgoing)
 
     direction = 1 - 2 * (lax.axis_index("node") % 2)
     order = (lax.axis_index("rep") + direction * lax.iota(I32, reps) + reps) % reps
-    slopes, score, far_ahead, far_behind, *near = call(
+    slopes, score, *parts = call(
         expert_body,
         (
             shaped(slots, 2 * hidden),
             shaped(slots, LANES),
-            *[shaped(packed_rows // 2, LANES)] * 2,
-            *[shaped(packed_rows, LANES)] * (reps - 1),
+            *[shaped(packed_rows, LANES)] * reps,
         ),
         [pl.BlockSpec(memory_space=pltpu.SMEM)] + whole(1) + [hbm] * 3,
-        whole(4 + reps - 1),
+        whole(2 + reps),
         scratch=(
             pltpu.VMEM((2, slots, width), BF16),
             pltpu.VMEM((width, hidden), BF16),
@@ -300,7 +278,11 @@
         cost=cost(6 * product, 12 << 20),
     )(order, arrived, w_gate, w_up, w_down)
 
-    sums = reduce_scatter(far_ahead, far_behind, near)
+    forward, backward = ring(0), ring(1)
+    ahead, behind = forward(parts[4]), backward(parts[-3])
+    ahead, behind = forward(add(parts[3], ahead)), backward(add(parts[-2], behind))
+    ahead, behind = forward(add(parts[2], ahead)), backward(add(parts[-1], behind))
+    ahead = forward(add(parts[1], ahead))
 
     rows = call(
         rows_body,
@@ -308,6 +290,7 @@
         whole(4),
         whole(1)[0],
         cost=cost(2 * product, 5 << 20),
+        limit=VMEM_LEAST,
     )(slopes, score, w_gate, w_up)
     returned = exchange(rows.reshape(experts, CAP, width + LANES)).reshape(slots, width + LANES)
     grad_tokens, grad_gates = call(
@@ -316,8 +299,10 @@
         whole(4),
         whole(2),
         cost=cost(2 * slots * tok * width, 2 << 20),
+        limit=VMEM_LEAST,
     )(returned, spread, ids_t, gates_t)
 
+    own, grad_tokens, grad_gates = lax.optimization_barrier((parts[0], grad_tokens, grad_gates))
     grad_w_gate, grad_w_up, grad_w_down = call(
         unpack_body,
         (
@@ -328,7 +313,8 @@
         whole(3),
         whole(3),
         cost=cost(0, 2 << 20),
-    )(*sums)
+        limit=VMEM_LEAST,
+    )(own, ahead, behind)
     return (
         grad_tokens,
         grad_gates.T,

time: 172 us -> 161 us (0.936)
  the two profiles are of different devices: /device:TPU:1 before, /device:TPU:24 now
where the time goes in v6:
time: 161 us; the launch traced here: 160 us
  waiting for transfers between devices  81.4 us (51%)
  starting transfers between devices  55.3 us (34%)
  Pallas kernels  16.2 us (10%)
  other arithmetic  3.74 us (2%)
  local copies, waits for them, and re-layouts  2.79 us (2%)
    all_to_all x2, waiting for transfers between devices, exchange(): lax.all_to_all(blocks, PLANE, split_axis=0, concat_axis=0, tiled=True)  52.3 us
    all_to_all x2, starting transfers between devices, exchange(): lax.all_to_all(blocks, PLANE, split_axis=0, concat_axis=0, tiled=True)  31.9 us
    ppermute x7, waiting for transfers between devices, ring(): return lambda message: lax.ppermute(message, ('rep', 'node'), pairs)  29.1 us
    ppermute x7, starting transfers between devices, ring(): return lambda message: lax.ppermute(message, ('rep', 'node'), pairs)  23.3 us
    pallas_call x1, Pallas kernels, shards(): call(expert_body, (shaped(slots, 2 * hidden), shaped(slots, LANES), *[sha...  8.01 us
    pallas_call x1, Pallas kernels, shards(): call(route_body, (shaped(experts, 2 * BLOCK, WIDE), shaped(slots, LANES))...  4.94 us
    convert_element_type x5, other arithmetic, add(): return (left.astype(F32) + right.astype(F32)).astype(BF16)  3.73 us
  transfers between devices with their start and end apart: 9, of which 5 were waited for; matrix products, arithmetic and copies ran while one was open for 4% of the time, Pallas kernels for 1%

profile of v6, /device:TPU:24, one launch (start us, length us, event | category | flops | bytes accessed | tf_op | source)
XLA Modules:
  0.0 160.2 jit_solution(1912719394719810837)
XLA Ops:
  0.6 4.9 %shard_map.110 = (bf16[128,32,256]{2,1,0:T(8,128)(2,1)}, bf16[256,128]{1,0:T(8,128)(2,1)}) custom-call(s32[8,16]{1,0:T(8,128)} %bitcast.13, bf16[8,16]{1,0:T(8,128)(2,1)} %bitcast.15, bf16[16,2048]{1,0:T(8,128)(2,1)} %tokens_hbm.1, bf16[16,2048]{1,0:T(8,128)(2,1)} %grads_hbm.1), custom_call_target="tpu_custom_call" | custom-call | flops 268435456 | bytes 2097152 | tf_op jit(solution)/shard_map/pallas_call | solution.py:243
  5.6 24.6 %all-to-all-start = ((bf16[128,32,256]{2,1,0:T(8,128)(2,1)}), bf16[128,32,256]{2,1,0:T(8,128)(2,1)}, u32[]{:S(2)}, u32[]{:S(2)}) async-start(bf16[128,32,256]{2,1,0:T(8,128)(2,1)} %get-tuple-element.25), calls=%async_computation | async-start | bytes 4194304 | tf_op jit(solution)/shard_map/all_to_all | solution.py:213
  30.2 52.3 %all-to-all-done.arrived_ref = bf16[128,32,256]{2,1,0:T(8,128)(2,1)} async-done(((bf16[128,32,256]{2,1,0:T(8,128)(2,1)}), bf16[128,32,256]{2,1,0:T(8,128)(2,1)}, u32[]{:S(2)}, u32[]{:S(2)}) %all-to-all-start) | async-done | bytes 2097184 | tf_op jit(solution)/shard_map/all_to_all | solution.py:213
  82.5 8.0 %shard_map.111 = (bf16[256,768]{1,0:T(8,128)(2,1)S(1)}, bf16[256,128]{1,0:T(8,128)(2,1)S(1)}, bf16[2304,128]{1,0:T(8,128)(2,1)S(1)}, bf16[2304,128]{1,0:T(8,128)...) custom-call(s32[8]{0:T(128)S(1)} %and_select_fusion.order_ref, ...), custom_call_target="tpu_custom_call" | custom-call | flops 2415919104 | bytes 12582912 | tf_op jit(solution)/shard_map/pallas_call | solution.py:261
  90.5 2.5 %collective-permute-start = (bf16[2304,128]{1,0:T(8,128)(2,1)}, bf16[2304,128]{1,0:T(8,128)(2,1)}, u32[]{:S(2)}, u32[]{:S(2)}) collective-permute-start(bf16[2304,128]{1,0:T(8,128)(2,1)} %get-tuple-element.38), channel_id=1, source_target_pairs={{0,128},{8,904},{16,144},{24,920},{32,160},{40,936},{48,176},{56,9... | collective-permute-start | bytes 1769480 | tf_op jit(solution)/shard_map/ppermute | solution.py:223
  93.0 4.6 %collective-permute-start.4 = (bf16[2304,128]{1,0:T(8,128)(2,1)}, bf16[2304,128]{1,0:T(8,128)(2,1)}, u32[]{:S(2)}, u32[]{:S(2)}) collective-permute-start(bf16[2304,128]{1,0:T(8,128)(2,1)} %get-tuple-element.41), channel_id=1, source_target_pairs={{0,896},{8,136},{16,912},{24,152},{32,928},{40,168},{48,944},{56,1... | collective-permute-start | bytes 1769480 | tf_op jit(solution)/shard_map/ppermute | solution.py:223
  97.6 1.3 shard_map.112
  98.9 1.3 reshape.16
  100.1 7.4 %all-to-all-start.1 = ((bf16[128,2,2176]{2,1,0:T(2,128)(2,1)}), bf16[128,2,2176]{2,1,0:T(2,128)(2,1)}, u32[]{:S(2)}, u32[]{:S(2)}) async-start(bf16[128,2,2176]{2,1,0:T(2,128)(2,1)} %reshape.16), calls=%async_computation.1 | async-start | bytes 2228224 | tf_op jit(solution)/shard_map/all_to_all | solution.py:213
  107.5 0.7 collective-permute-done
  108.2 1.2 add_convert_fusion.4
  109.4 1.9 %collective-permute-start.1 = (bf16[2304,128]{1,0:T(8,128)(2,1)S(1)}, bf16[2304,128]{1,0:T(8,128)(2,1)S(1)}, u32[]{:S(2)}, u32[]{:S(2)}) collective-permute-start(bf16[2304,128]{1,0:T(8,128)(2,1)S(1)} %add_convert_fusion.4), channel_id=1, source_target_pairs={{0,128},{8,904},{16,144},{24,920},{32,160},{40,936},{48,176},{56,9... | collective-permute-start | bytes 1769480 | tf_op jit(solution)/shard_map/ppermute | solution.py:223
  111.4 1.2 add_convert_fusion.1
  112.6 5.3 %collective-permute-start.5 = (bf16[2304,128]{1,0:T(8,128)(2,1)S(1)}, bf16[2304,128]{1,0:T(8,128)(2,1)S(1)}, u32[]{:S(2)}, u32[]{:S(2)}) collective-permute-start(bf16[2304,128]{1,0:T(8,128)(2,1)S(1)} %add_convert_fusion.1), channel_id=1, source_target_pairs={{0,896},{8,136},{16,912},{24,152},{32,928},{40,168},{48,944},{56,1... | collective-permute-start | bytes 1769480 | tf_op jit(solution)/shard_map/ppermute | solution.py:223
  117.9 8.9 %collective-permute-done.1 = bf16[2304,128]{1,0:T(8,128)(2,1)S(1)} collective-permute-done((bf16[2304,128]{1,0:T(8,128)(2,1)S(1)}, bf16[2304,128]{1,0:T(8,128)(2,1)S(1)}, u32[]{:S(2)}, u32[]{:S(2)}) %collective-permute-start.1) | collective-permute-done | bytes 589856 | tf_op jit(solution)/shard_map/ppermute | solution.py:223
  126.9 1.9 %collective-permute-start.2 = (bf16[2304,128]{1,0:T(8,128)(2,1)S(1)}, bf16[2304,128]{1,0:T(8,128)(2,1)S(1)}, u32[]{:S(2)}, u32[]{:S(2)}) collective-permute-start(bf16[2304,128]{1,0:T(8,128)(2,1)S(1)} %add_convert_fusion.3), channel_id=1, source_target_pairs={{0,128},{8,904},{16,144},{24,920},{32,160},{40,936},{48,176},{56,9... | collective-permute-start | bytes 1769480 | tf_op jit(solution)/shard_map/ppermute | solution.py:223
  129.0 5.1 %collective-permute-start.6 = (bf16[2304,128]{1,0:T(8,128)(2,1)S(1)}, bf16[2304,128]{1,0:T(8,128)(2,1)S(1)}, u32[]{:S(2)}, u32[]{:S(2)}) collective-permute-start(bf16[2304,128]{1,0:T(8,128)(2,1)S(1)} %add_convert_fusion), channel_id=1, source_target_pairs={{0,896},{8,136},{16,912},{24,152},{32,928},{40,168},{48,944},{56,1... | collective-permute-start | bytes 1769480 | tf_op jit(solution)/shard_map/ppermute | solution.py:223
  134.2 10.8 %collective-permute-done.2 = bf16[2304,128]{1,0:T(8,128)(2,1)S(1)} collective-permute-done((bf16[2304,128]{1,0:T(8,128)(2,1)S(1)}, bf16[2304,128]{1,0:T(8,128)(2,1)S(1)}, u32[]{:S(2)}, u32[]{:S(2)}) %collective-permute-start.2) | collective-permute-done | bytes 589856 | tf_op jit(solution)/shard_map/ppermute | solution.py:223
  144.9 1.0 add_convert_fusion.2
  145.9 2.0 %collective-permute-start.3 = (bf16[2304,128]{1,0:T(8,128)(2,1)}, bf16[2304,128]{1,0:T(8,128)(2,1)S(1)}, u32[]{:S(2)}, u32[]{:S(2)}) collective-permute-start(bf16[2304,128]{1,0:T(8,128)(2,1)} %add_convert_fusion.2), channel_id=1, source_target_pairs={{0,128},{8,904},{16,144},{24,920},{32,160},{40,936},{48,176},{56,9... | collective-permute-start | bytes 1769480 | tf_op jit(solution)/shard_map/ppermute | solution.py:223
  148.0 1.5 reshape.17.returned_ref
  149.5 1.0 shard_map.113
  150.5 8.8 %collective-permute-done.3.ahead_ref = bf16[2304,128]{1,0:T(8,128)(2,1)S(1)} collective-permute-done((bf16[2304,128]{1,0:T(8,128)(2,1)}, bf16[2304,128]{1,0:T(8,128)(2,1)S(1)}, u32[]{:S(2)}, u32[]{:S(2)}) %collective-permute-start.3) | collective-permute-done | bytes 589856 | tf_op jit(solution)/shard_map/ppermute | solution.py:223
  159.2 1.0 shard_map.114
  (21 shorter events, 0.4 us)
Async XLA Ops:
  5.6 76.9 %all-to-all-start = ((bf16[128,32,256]{2,1,0:T(8,128)(2,1)}), bf16[128,32,256]{2,1,0:T(8,128)(2,1)}, u32[]{:S(2)}, u32[]{:S(2)}) async-start(bf16[128,32,256]{2,1,0:T(8,128)(2,1)} %get-tuple-element.25), calls=%async_computation | async-start | bytes 4194304 | tf_op jit(solution)/shard_map/all_to_all | solution.py:213
  82.5 15.1 %copy-start = (bf16[1,2048,384]{2,1,0:T(8,128)(2,1)S(1)}, bf16[1,2048,384]{2,1,0:T(8,128)(2,1)}, u32[]{:S(2)}) copy-start(bf16[1,2048,384]{2,1,0:T(8,128)(2,1)} %param.11) | copy-start | bytes 4718596
  82.5 15.1 %copy-start.1 = (bf16[1,2048,384]{2,1,0:T(8,128)(2,1)S(1)}, bf16[1,2048,384]{2,1,0:T(8,128)(2,1)}, u32[]{:S(2)}) copy-start(bf16[1,2048,384]{2,1,0:T(8,128)(2,1)} %param.12) | copy-start | bytes 4718596
  90.5 17.7 %collective-permute-start = (bf16[2304,128]{1,0:T(8,128)(2,1)}, bf16[2304,128]{1,0:T(8,128)(2,1)}, u32[]{:S(2)}, u32[]{:S(2)}) collective-permute-start(bf16[2304,128]{1,0:T(8,128)(2,1)} %get-tuple-element.38), channel_id=1, source_target_pairs={{0,128},{8,904},{16,144},{24,920},{32,160},{40,936},{48,176},{56,9... | collective-permute-start | bytes 1769480 | tf_op jit(solution)/shard_map/ppermute | solution.py:223
  93.0 18.4 %collective-permute-start.4 = (bf16[2304,128]{1,0:T(8,128)(2,1)}, bf16[2304,128]{1,0:T(8,128)(2,1)}, u32[]{:S(2)}, u32[]{:S(2)}) collective-permute-start(bf16[2304,128]{1,0:T(8,128)(2,1)} %get-tuple-element.41), channel_id=1, source_target_pairs={{0,896},{8,136},{16,912},{24,152},{32,928},{40,168},{48,944},{56,1... | collective-permute-start | bytes 1769480 | tf_op jit(solution)/shard_map/ppermute | solution.py:223
  100.1 47.9 %all-to-all-start.1 = ((bf16[128,2,2176]{2,1,0:T(2,128)(2,1)}), bf16[128,2,2176]{2,1,0:T(2,128)(2,1)}, u32[]{:S(2)}, u32[]{:S(2)}) async-start(bf16[128,2,2176]{2,1,0:T(2,128)(2,1)} %reshape.16), calls=%async_computation.1 | async-start | bytes 2228224 | tf_op jit(solution)/shard_map/all_to_all | solution.py:213
  107.5 3.8 %copy-start.6 = (bf16[2304,128]{1,0:T(8,128)(2,1)S(1)}, bf16[2304,128]{1,0:T(8,128)(2,1)}, u32[]{:S(2)}) copy-start(bf16[2304,128]{1,0:T(8,128)(2,1)} %get-tuple-element.40) | copy-start | bytes 1769476
  109.4 17.3 %collective-permute-start.1 = (bf16[2304,128]{1,0:T(8,128)(2,1)S(1)}, bf16[2304,128]{1,0:T(8,128)(2,1)S(1)}, u32[]{:S(2)}, u32[]{:S(2)}) collective-permute-start(bf16[2304,128]{1,0:T(8,128)(2,1)S(1)} %add_convert_fusion.4), channel_id=1, source_target_pairs={{0,128},{8,904},{16,144},{24,920},{32,160},{40,936},{48,176},{56,9... | collective-permute-start | bytes 1769480 | tf_op jit(solution)/shard_map/ppermute | solution.py:223
  112.6 16.3 %copy-start.5 = (bf16[2304,128]{1,0:T(8,128)(2,1)S(1)}, bf16[2304,128]{1,0:T(8,128)(2,1)}, u32[]{:S(2)}) copy-start(bf16[2304,128]{1,0:T(8,128)(2,1)} %get-tuple-element.39) | copy-start | bytes 1769476
  112.6 16.2 %collective-permute-start.5 = (bf16[2304,128]{1,0:T(8,128)(2,1)S(1)}, bf16[2304,128]{1,0:T(8,128)(2,1)S(1)}, u32[]{:S(2)}, u32[]{:S(2)}) collective-permute-start(bf16[2304,128]{1,0:T(8,128)(2,1)S(1)} %add_convert_fusion.1), channel_id=1, source_target_pairs={{0,896},{8,136},{16,912},{24,152},{32,928},{40,168},{48,944},{56,1... | collective-permute-start | bytes 1769480 | tf_op jit(solution)/shard_map/ppermute | solution.py:223
  126.9 18.0 %collective-permute-start.2 = (bf16[2304,128]{1,0:T(8,128)(2,1)S(1)}, bf16[2304,128]{1,0:T(8,128)(2,1)S(1)}, u32[]{:S(2)}, u32[]{:S(2)}) collective-permute-start(bf16[2304,128]{1,0:T(8,128)(2,1)S(1)} %add_convert_fusion.3), channel_id=1, source_target_pairs={{0,128},{8,904},{16,144},{24,920},{32,160},{40,936},{48,176},{56,9... | collective-permute-start | bytes 1769480 | tf_op jit(solution)/shard_map/ppermute | solution.py:223
  129.0 21.5 %collective-permute-start.6 = (bf16[2304,128]{1,0:T(8,128)(2,1)S(1)}, bf16[2304,128]{1,0:T(8,128)(2,1)S(1)}, u32[]{:S(2)}, u32[]{:S(2)}) collective-permute-start(bf16[2304,128]{1,0:T(8,128)(2,1)S(1)} %add_convert_fusion), channel_id=1, source_target_pairs={{0,896},{8,136},{16,912},{24,152},{32,928},{40,168},{48,944},{56,1... | collective-permute-start | bytes 1769480 | tf_op jit(solution)/shard_map/ppermute | solution.py:223
  145.9 3.6 %copy-start.2 = (bf16[256,128]{1,0:T(8,128)(2,1)S(1)}, bf16[256,128]{1,0:T(8,128)(2,1)}, u32[]{:S(2)}) copy-start(bf16[256,128]{1,0:T(8,128)(2,1)} %get-tuple-element.29.spread_ref) | copy-start | bytes 196612
  145.9 3.6 %copy-start.3 = (s32[16,8]{0,1:T(8,128)S(1)}, s32[16,8]{0,1:T(8,128)}, u32[]{:S(2)}) copy-start(s32[16,8]{0,1:T(8,128)} %param.9) | copy-start | bytes 1540
  145.9 3.6 %copy-start.4 = (bf16[16,8]{0,1:T(8,128)(2,1)S(1)}, bf16[16,8]{0,1:T(8,128)(2,1)}, u32[]{:S(2)}) copy-start(bf16[16,8]{0,1:T(8,128)(2,1)} %param.10) | copy-start | bytes 772
  145.9 13.3 %collective-permute-start.3 = (bf16[2304,128]{1,0:T(8,128)(2,1)}, bf16[2304,128]{1,0:T(8,128)(2,1)S(1)}, u32[]{:S(2)}, u32[]{:S(2)}) collective-permute-start(bf16[2304,128]{1,0:T(8,128)(2,1)} %add_convert_fusion.2), channel_id=1, source_target_pairs={{0,128},{8,904},{16,144},{24,920},{32,160},{40,936},{48,176},{56,9... | collective-permute-start | bytes 1769480 | tf_op jit(solution)/shard_map/ppermute | solution.py:223

commit v7 on v6

--- a/solution.py
+++ b/solution.py
@@ -13,6 +13,7 @@
 GROUP = 16
 GROUP_SLOTS = GROUP * CAP
 LANES = 128
+EARLY, LATE = (4, 5, 3), (6, 2, 7, 1, 0)
 
 
 def iota(shape, dim):
@@ -101,9 +102,9 @@
 
 def expert_body(
     order_ref, arrived_ref, gate_hbm, up_hbm, down_hbm,
-    slopes_ref, score_ref, *refs,
+    rows_ref, hidden_ref, slopes_ref, score_ref, *refs,
 ):
-    parts, (rows_ref, w_gate, w_up, w_down, down_ref, load_sems) = refs[:-6], refs[-6:]
+    parts, (w_gate, w_up, w_down, turned_ref, load_sems) = refs[:-5], refs[-5:]
     loads = [
         pltpu.make_async_copy(source, target, load_sems.at[i])
         for i, (source, target) in enumerate(
@@ -140,17 +141,29 @@
     score = jnp.sum(hidden_act.astype(F32) * grad_act, axis=1, keepdims=True)
     score_ref[...] = jnp.broadcast_to(score, score_ref.shape).astype(BF16)
 
-    shards = order_ref.shape[0]
-    share = hidden // shards
+    hidden_ref[...] = hidden_act
+    turned_ref[...] = hidden_act.astype(F32).T.astype(BF16)
+    share = hidden // order_ref.shape[0]
+    for offset, part in zip(EARLY, parts, strict=True):
+        target = order_ref[offset]
+        columns = pl.ds(pl.multiple_of(target * WIDE, WIDE), WIDE)
+        gate_up = dot(rows_ref[0, :, columns], slopes_ref[...], 0, 0).astype(BF16)
+        turned = turned_ref[pl.ds(pl.multiple_of(target * share, 16), share), :]
+        store_part(dot(turned, rows_ref[1], 1, 0).astype(BF16), gate_up, part)
+
+
+def late_body(order_ref, rows_ref, hidden_ref, slopes_ref, *refs):
+    parts, down_ref = refs[:-1], refs[-1]
+    share = hidden_ref.shape[1] // order_ref.shape[0]
     for n in range(PIECES):
         columns = slice(n * WIDE, (n + 1) * WIDE)
-        down_ref[:, columns] = dot(hidden_act, rows_ref[1, :, columns], 0, 0).astype(BF16)
-    for offset in range(shards):
+        down_ref[:, columns] = dot(hidden_ref[...], rows_ref[1, :, columns], 0, 0).astype(BF16)
+    for offset, part in zip(LATE, parts, strict=True):
         target = order_ref[offset]
         columns = pl.ds(pl.multiple_of(target * WIDE, WIDE), WIDE)
         gate_up = dot(rows_ref[0, :, columns], slopes_ref[...], 0, 0).astype(BF16)
         down = down_ref[pl.ds(pl.multiple_of(target * share, 16), share), :]
-        store_part(down, gate_up, parts[offset])
+        store_part(down, gate_up, part)
 
 
 def rows_body(slopes_ref, score_ref, gate_ref, up_ref, out_ref):
@@ -258,30 +271,44 @@
 
     direction = 1 - 2 * (lax.axis_index("node") % 2)
     order = (lax.axis_index("rep") + direction * lax.iota(I32, reps) + reps) % reps
-    slopes, score, *parts = call(
+    smem = pl.BlockSpec(memory_space=pltpu.SMEM)
+    routed, hidden_act, slopes, score, *early = call(
         expert_body,
         (
+            shaped(2, slots, width),
+            shaped(slots, hidden),
             shaped(slots, 2 * hidden),
             shaped(slots, LANES),
-            *[shaped(packed_rows, LANES)] * reps,
+            *[shaped(packed_rows, LANES)] * len(EARLY),
         ),
-        [pl.BlockSpec(memory_space=pltpu.SMEM)] + whole(1) + [hbm] * 3,
-        whole(2 + reps),
+        [smem] + whole(1) + [hbm] * 3,
+        whole(4 + len(EARLY)),
         scratch=(
-            pltpu.VMEM((2, slots, width), BF16),
             pltpu.VMEM((width, hidden), BF16),
             pltpu.VMEM((width, hidden), BF16),
             pltpu.VMEM((hidden, width), BF16),
-            pltpu.VMEM((hidden, width), BF16),
+            pltpu.VMEM((hidden, slots), BF16),
             pltpu.SemaphoreType.DMA((3,)),
         ),
-        cost=cost(6 * product, 12 << 20),
+        cost=cost(4 * product, 12 << 20),
     )(order, arrived, w_gate, w_up, w_down)
-
+    parts = dict(zip(EARLY, early, strict=True))
     forward, backward = ring(0), ring(1)
-    ahead, behind = forward(parts[4]), backward(parts[-3])
-    ahead, behind = forward(add(parts[3], ahead)), backward(add(parts[-2], behind))
-    ahead, behind = forward(add(parts[2], ahead)), backward(add(parts[-1], behind))
+    ahead, behind = forward(parts[4]), backward(parts[5])
+    to_ahead = add(parts[3], ahead)
+    later, _ = lax.optimization_barrier((slopes, to_ahead))
+    late = call(
+        late_body,
+        [shaped(packed_rows, LANES)] * len(LATE),
+        [smem] + whole(3),
+        whole(len(LATE)),
+        scratch=(pltpu.VMEM((hidden, width), BF16),),
+        cost=cost(3 * product, 8 << 20),
+        limit=VMEM_LEAST,
+    )(order, routed, hidden_act, later)
+    parts |= dict(zip(LATE, late, strict=True))
+    ahead, behind = forward(to_ahead), backward(add(parts[6], behind))
+    ahead, behind = forward(add(parts[2], ahead)), backward(add(parts[7], behind))
     ahead = forward(add(parts[1], ahead))
 
     rows = call(

time: 161 us -> 158 us (0.981)
  the two profiles are of different devices: /device:TPU:24 before, /device:TPU:7 now
where the time goes in v7:
time: 158 us; the launch traced here: 157 us
  waiting for transfers between devices  76.2 us (48%)
  starting transfers between devices  54 us (34%)
  Pallas kernels  17.1 us (11%)
  local copies, waits for them, and re-layouts  5.09 us (3%)
  other arithmetic  3.8 us (2%)
    all_to_all x2, waiting for transfers between devices, exchange(): lax.all_to_all(blocks, PLANE, split_axis=0, concat_axis=0, tiled=True)  53.8 us
    all_to_all x2, starting transfers between devices, exchange(): lax.all_to_all(blocks, PLANE, split_axis=0, concat_axis=0, tiled=True)  31.4 us
    ppermute x7, starting transfers between devices, ring(): return lambda message: lax.ppermute(message, ('rep', 'node'), pairs)  22.6 us
    ppermute x7, waiting for transfers between devices, ring(): return lambda message: lax.ppermute(message, ('rep', 'node'), pairs)  22.4 us
    pallas_call x1, Pallas kernels, shards(): call(expert_body, (shaped(2, slots, width), shaped(slots, hidden), shaped...  7.1 us
    pallas_call x1, Pallas kernels, shards(): call(route_body, (shaped(experts, 2 * BLOCK, WIDE), shaped(slots, LANES))...  4.95 us
    convert_element_type x5, other arithmetic, add(): return (left.astype(F32) + right.astype(F32)).astype(BF16)  3.78 us
  transfers between devices with their start and end apart: 9, of which 5 were waited for; matrix products, arithmetic and copies ran while one was open for 4% of the time, Pallas kernels for 3%

profile of v7, /device:TPU:7, one launch (start us, length us, event | category | flops | bytes accessed | tf_op | source)
XLA Modules:
  0.0 157.0 jit_solution(14595270001006803076)
XLA Ops:
  0.6 5.0 %shard_map.110 = (bf16[128,32,256]{2,1,0:T(8,128)(2,1)}, bf16[256,128]{1,0:T(8,128)(2,1)}) custom-call(s32[8,16]{1,0:T(8,128)} %bitcast.13, bf16[8,16]{1,0:T(8,128)(2,1)} %bitcast.15, bf16[16,2048]{1,0:T(8,128)(2,1)} %tokens_hbm.1, bf16[16,2048]{1,0:T(8,128)(2,1)} %grads_hbm.1), custom_call_target="tpu_custom_call" | custom-call | flops 268435456 | bytes 2097152 | tf_op jit(solution)/shard_map/pallas_call | solution.py:256
  5.6 25.0 %all-to-all-start = ((bf16[128,32,256]{2,1,0:T(8,128)(2,1)}), bf16[128,32,256]{2,1,0:T(8,128)(2,1)}, u32[]{:S(2)}, u32[]{:S(2)}) async-start(bf16[128,32,256]{2,1,0:T(8,128)(2,1)} %get-tuple-element.28), calls=%async_computation | async-start | bytes 4194304 | tf_op jit(solution)/shard_map/all_to_all | solution.py:226
  30.7 53.8 %all-to-all-done.arrived_ref = bf16[128,32,256]{2,1,0:T(8,128)(2,1)} async-done(((bf16[128,32,256]{2,1,0:T(8,128)(2,1)}), bf16[128,32,256]{2,1,0:T(8,128)(2,1)}, u32[]{:S(2)}, u32[]{:S(2)}) %all-to-all-start) | async-done | bytes 2097184 | tf_op jit(solution)/shard_map/all_to_all | solution.py:226
  84.5 7.1 %shard_map.111 = (bf16[2,256,2048]{2,1,0:T(8,128)(2,1)}, bf16[256,384]{1,0:T(8,128)(2,1)S(1)}, bf16[256,768]{1,0:T(8,128)(2,1)S(1)}, bf16[256,128]{1,0:T(8,128)(...) custom-call(s32[8]{0:T(128)S(1)} %and_select_fusion.order_ref, ...), custom_call_target="tpu_custom_call" | custom-call | flops 1610612736 | bytes 12582912 | tf_op jit(solution)/shard_map/pallas_call | solution.py:275
  91.6 2.2 %collective-permute-start = (bf16[2304,128]{1,0:T(8,128)(2,1)}, bf16[2304,128]{1,0:T(8,128)(2,1)}, u32[]{:S(2)}, u32[]{:S(2)}) collective-permute-start(bf16[2304,128]{1,0:T(8,128)(2,1)} %get-tuple-element.33), channel_id=1, source_target_pairs={{0,128},{8,904},{16,144},{24,920},{32,160},{40,936},{48,176},{56,9... | collective-permute-start | bytes 1769480 | tf_op jit(solution)/shard_map/ppermute | solution.py:236
  93.7 4.3 %collective-permute-start.4 = (bf16[2304,128]{1,0:T(8,128)(2,1)}, bf16[2304,128]{1,0:T(8,128)(2,1)}, u32[]{:S(2)}, u32[]{:S(2)}) collective-permute-start(bf16[2304,128]{1,0:T(8,128)(2,1)} %get-tuple-element.47), channel_id=1, source_target_pairs={{0,896},{8,136},{16,912},{24,152},{32,928},{40,168},{48,944},{56,1... | collective-permute-start | bytes 1769480 | tf_op jit(solution)/shard_map/ppermute | solution.py:236
  98.1 1.3 shard_map.113
  100.1 1.2 reshape.16
  101.4 6.4 %all-to-all-start.1 = ((bf16[128,2,2176]{2,1,0:T(2,128)(2,1)}), bf16[128,2,2176]{2,1,0:T(2,128)(2,1)}, u32[]{:S(2)}, u32[]{:S(2)}) async-start(bf16[128,2,2176]{2,1,0:T(2,128)(2,1)} %reshape.16), calls=%async_computation.1 | async-start | bytes 2228224 | tf_op jit(solution)/shard_map/all_to_all | solution.py:226
  107.8 1.3 add_convert_fusion.4
  109.0 2.1 %collective-permute-start.1 = (bf16[2304,128]{1,0:T(8,128)(2,1)S(1)}, bf16[2304,128]{1,0:T(8,128)(2,1)S(1)}, u32[]{:S(2)}, u32[]{:S(2)}) collective-permute-start(bf16[2304,128]{1,0:T(8,128)(2,1)S(1)} %add_convert_fusion.4), channel_id=1, source_target_pairs={{0,128},{8,904},{16,144},{24,920},{32,160},{40,936},{48,176},{56,9... | collective-permute-start | bytes 1769480 | tf_op jit(solution)/shard_map/ppermute | solution.py:236
  111.2 1.6 %copy-done.7 = bf16[2,256,2048]{2,1,0:T(8,128)(2,1)S(1)} copy-done((bf16[2,256,2048]{2,1,0:T(8,128)(2,1)S(1)}, bf16[2,256,2048]{2,1,0:T(8,128)(2,1)}, u32[]{:S(2)}) %copy-start.7) | copy-done | bytes 2097176
  112.8 1.8 %shard_map.112 = (bf16[2304,128]{1,0:T(8,128)(2,1)S(1)}, bf16[2304,128]{1,0:T(8,128)(2,1)S(1)}, bf16[2304,128]{1,0:T(8,128)(2,1)S(1)}, bf16[2304,128]{1,0:T(8,128)(2,1)S(1)}, bf16[2304,128]{1,0:T(8,128)(2,1)S(1)}) custom-call(s32[8]{0:T(128)S(1)} %and_select_fusion.order_ref, bf16[2,256,2048]{2,1,0:T(8,128)(2,1)S(1)} %copy-done.7, ...), custom_call_target="tpu_custom_call" | custom-call | flops 1207959552 | bytes 8388608 | tf_op jit(solution)/shard_map/pallas_call | solution.py:300
  114.6 1.2 add_convert_fusion.1
  115.8 4.6 %collective-permute-start.5 = (bf16[2304,128]{1,0:T(8,128)(2,1)S(1)}, bf16[2304,128]{1,0:T(8,128)(2,1)S(1)}, u32[]{:S(2)}, u32[]{:S(2)}) collective-permute-start(bf16[2304,128]{1,0:T(8,128)(2,1)S(1)} %add_convert_fusion.1), channel_id=1, source_target_pairs={{0,896},{8,136},{16,912},{24,152},{32,928},{40,168},{48,944},{56,1... | collective-permute-start | bytes 1769480 | tf_op jit(solution)/shard_map/ppermute | solution.py:236
  121.4 1.9 %collective-permute-start.2 = (bf16[2304,128]{1,0:T(8,128)(2,1)S(1)}, bf16[2304,128]{1,0:T(8,128)(2,1)S(1)}, u32[]{:S(2)}, u32[]{:S(2)}) collective-permute-start(bf16[2304,128]{1,0:T(8,128)(2,1)S(1)} %add_convert_fusion.3), channel_id=1, source_target_pairs={{0,128},{8,904},{16,144},{24,920},{32,160},{40,936},{48,176},{56,9... | collective-permute-start | bytes 1769480 | tf_op jit(solution)/shard_map/ppermute | solution.py:236
  123.4 4.6 %collective-permute-done.5 = bf16[2304,128]{1,0:T(8,128)(2,1)S(1)} collective-permute-done((bf16[2304,128]{1,0:T(8,128)(2,1)S(1)}, bf16[2304,128]{1,0:T(8,128)(2,1)S(1)}, u32[]{:S(2)}, u32[]{:S(2)}) %collective-permute-start.5) | collective-permute-done | bytes 589856 | tf_op jit(solution)/shard_map/ppermute | solution.py:236
  128.1 5.4 %collective-permute-start.6 = (bf16[2304,128]{1,0:T(8,128)(2,1)S(1)}, bf16[2304,128]{1,0:T(8,128)(2,1)S(1)}, u32[]{:S(2)}, u32[]{:S(2)}) collective-permute-start(bf16[2304,128]{1,0:T(8,128)(2,1)S(1)} %add_convert_fusion), channel_id=1, source_target_pairs={{0,896},{8,136},{16,912},{24,152},{32,928},{40,168},{48,944},{56,1... | collective-permute-start | bytes 1769480 | tf_op jit(solution)/shard_map/ppermute | solution.py:236
  133.6 4.9 %collective-permute-done.2 = bf16[2304,128]{1,0:T(8,128)(2,1)S(1)} collective-permute-done((bf16[2304,128]{1,0:T(8,128)(2,1)S(1)}, bf16[2304,128]{1,0:T(8,128)(2,1)S(1)}, u32[]{:S(2)}, u32[]{:S(2)}) %collective-permute-start.2) | collective-permute-done | bytes 589856 | tf_op jit(solution)/shard_map/ppermute | solution.py:236
  138.5 1.0 add_convert_fusion.2
  139.5 2.0 %collective-permute-start.3 = (bf16[2304,128]{1,0:T(8,128)(2,1)}, bf16[2304,128]{1,0:T(8,128)(2,1)S(1)}, u32[]{:S(2)}, u32[]{:S(2)}) collective-permute-start(bf16[2304,128]{1,0:T(8,128)(2,1)} %add_convert_fusion.2), channel_id=1, source_target_pairs={{0,128},{8,904},{16,144},{24,920},{32,160},{40,936},{48,176},{56,9... | collective-permute-start | bytes 1769480 | tf_op jit(solution)/shard_map/ppermute | solution.py:236
  141.6 1.5 reshape.17.returned_ref
  143.1 1.0 shard_map.114
  144.1 12.0 %collective-permute-done.3.ahead_ref = bf16[2304,128]{1,0:T(8,128)(2,1)S(1)} collective-permute-done((bf16[2304,128]{1,0:T(8,128)(2,1)}, bf16[2304,128]{1,0:T(8,128)(2,1)S(1)}, u32[]{:S(2)}, u32[]{:S(2)}) %collective-permute-start.3) | collective-permute-done | bytes 589856 | tf_op jit(solution)/shard_map/ppermute | solution.py:236
  (24 shorter events, 3.0 us)
Async XLA Ops:
  5.6 78.9 %copy-start = (bf16[1,2048,384]{2,1,0:T(8,128)(2,1)S(1)}, bf16[1,2048,384]{2,1,0:T(8,128)(2,1)}, u32[]{:S(2)}) copy-start(bf16[1,2048,384]{2,1,0:T(8,128)(2,1)} %param.11) | copy-start | bytes 4718596
  5.6 78.9 %all-to-all-start = ((bf16[128,32,256]{2,1,0:T(8,128)(2,1)}), bf16[128,32,256]{2,1,0:T(8,128)(2,1)}, u32[]{:S(2)}, u32[]{:S(2)}) async-start(bf16[128,32,256]{2,1,0:T(8,128)(2,1)} %get-tuple-element.28), calls=%async_computation | async-start | bytes 4194304 | tf_op jit(solution)/shard_map/all_to_all | solution.py:226
  84.5 13.6 %copy-start.1 = (bf16[1,2048,384]{2,1,0:T(8,128)(2,1)S(1)}, bf16[1,2048,384]{2,1,0:T(8,128)(2,1)}, u32[]{:S(2)}) copy-start(bf16[1,2048,384]{2,1,0:T(8,128)(2,1)} %param.12) | copy-start | bytes 4718596
  91.6 16.2 %collective-permute-start = (bf16[2304,128]{1,0:T(8,128)(2,1)}, bf16[2304,128]{1,0:T(8,128)(2,1)}, u32[]{:S(2)}, u32[]{:S(2)}) collective-permute-start(bf16[2304,128]{1,0:T(8,128)(2,1)} %get-tuple-element.33), channel_id=1, source_target_pairs={{0,128},{8,904},{16,144},{24,920},{32,160},{40,936},{48,176},{56,9... | collective-permute-start | bytes 1769480 | tf_op jit(solution)/shard_map/ppermute | solution.py:236
  93.7 20.8 %collective-permute-start.4 = (bf16[2304,128]{1,0:T(8,128)(2,1)}, bf16[2304,128]{1,0:T(8,128)(2,1)}, u32[]{:S(2)}, u32[]{:S(2)}) collective-permute-start(bf16[2304,128]{1,0:T(8,128)(2,1)} %get-tuple-element.47), channel_id=1, source_target_pairs={{0,896},{8,136},{16,912},{24,152},{32,928},{40,168},{48,944},{56,1... | collective-permute-start | bytes 1769480 | tf_op jit(solution)/shard_map/ppermute | solution.py:236
  99.4 0.8 copy-start.2
  101.4 40.2 %all-to-all-start.1 = ((bf16[128,2,2176]{2,1,0:T(2,128)(2,1)}), bf16[128,2,2176]{2,1,0:T(2,128)(2,1)}, u32[]{:S(2)}, u32[]{:S(2)}) async-start(bf16[128,2,2176]{2,1,0:T(2,128)(2,1)} %reshape.16), calls=%async_computation.1 | async-start | bytes 2228224 | tf_op jit(solution)/shard_map/all_to_all | solution.py:226
  107.8 3.4 %copy-start.3 = (bf16[256,768]{1,0:T(8,128)(2,1)S(1)}, bf16[256,768]{1,0:T(8,128)(2,1)}, u32[]{:S(2)}) copy-start(bf16[256,768]{1,0:T(8,128)(2,1)} %copy-done.2) | copy-start | bytes 1179652
  109.0 12.2 %collective-permute-start.1 = (bf16[2304,128]{1,0:T(8,128)(2,1)S(1)}, bf16[2304,128]{1,0:T(8,128)(2,1)S(1)}, u32[]{:S(2)}, u32[]{:S(2)}) collective-permute-start(bf16[2304,128]{1,0:T(8,128)(2,1)S(1)} %add_convert_fusion.4), channel_id=1, source_target_pairs={{0,128},{8,904},{16,144},{24,920},{32,160},{40,936},{48,176},{56,9... | collective-permute-start | bytes 1769480 | tf_op jit(solution)/shard_map/ppermute | solution.py:236
  111.2 1.6 %copy-start.7 = (bf16[2,256,2048]{2,1,0:T(8,128)(2,1)S(1)}, bf16[2,256,2048]{2,1,0:T(8,128)(2,1)}, u32[]{:S(2)}) copy-start(bf16[2,256,2048]{2,1,0:T(8,128)(2,1)} %get-tuple-element.29.rows_ref) | copy-start | bytes 6291460
  115.8 12.2 %collective-permute-start.5 = (bf16[2304,128]{1,0:T(8,128)(2,1)S(1)}, bf16[2304,128]{1,0:T(8,128)(2,1)S(1)}, u32[]{:S(2)}, u32[]{:S(2)}) collective-permute-start(bf16[2304,128]{1,0:T(8,128)(2,1)S(1)} %add_convert_fusion.1), channel_id=1, source_target_pairs={{0,896},{8,136},{16,912},{24,152},{32,928},{40,168},{48,944},{56,1... | collective-permute-start | bytes 1769480 | tf_op jit(solution)/shard_map/ppermute | solution.py:236
  121.4 17.1 %collective-permute-start.2 = (bf16[2304,128]{1,0:T(8,128)(2,1)S(1)}, bf16[2304,128]{1,0:T(8,128)(2,1)S(1)}, u32[]{:S(2)}, u32[]{:S(2)}) collective-permute-start(bf16[2304,128]{1,0:T(8,128)(2,1)S(1)} %add_convert_fusion.3), channel_id=1, source_target_pairs={{0,128},{8,904},{16,144},{24,920},{32,160},{40,936},{48,176},{56,9... | collective-permute-start | bytes 1769480 | tf_op jit(solution)/shard_map/ppermute | solution.py:236
  128.1 15.9 %collective-permute-start.6 = (bf16[2304,128]{1,0:T(8,128)(2,1)S(1)}, bf16[2304,128]{1,0:T(8,128)(2,1)S(1)}, u32[]{:S(2)}, u32[]{:S(2)}) collective-permute-start(bf16[2304,128]{1,0:T(8,128)(2,1)S(1)} %add_convert_fusion), channel_id=1, source_target_pairs={{0,896},{8,136},{16,912},{24,152},{32,928},{40,168},{48,944},{56,1... | collective-permute-start | bytes 1769480 | tf_op jit(solution)/shard_map/ppermute | solution.py:236
  139.5 3.6 %copy-start.4 = (bf16[256,128]{1,0:T(8,128)(2,1)S(1)}, bf16[256,128]{1,0:T(8,128)(2,1)}, u32[]{:S(2)}) copy-start(bf16[256,128]{1,0:T(8,128)(2,1)} %get-tuple-element.37.spread_ref) | copy-start | bytes 196612
  139.5 3.6 %copy-start.5 = (s32[16,8]{0,1:T(8,128)S(1)}, s32[16,8]{0,1:T(8,128)}, u32[]{:S(2)}) copy-start(s32[16,8]{0,1:T(8,128)} %param.9) | copy-start | bytes 1540
  139.5 3.6 %copy-start.6 = (bf16[16,8]{0,1:T(8,128)(2,1)S(1)}, bf16[16,8]{0,1:T(8,128)(2,1)}, u32[]{:S(2)}) copy-start(bf16[16,8]{0,1:T(8,128)(2,1)} %param.10) | copy-start | bytes 772
  139.5 16.5 %collective-permute-start.3 = (bf16[2304,128]{1,0:T(8,128)(2,1)}, bf16[2304,128]{1,0:T(8,128)(2,1)S(1)}, u32[]{:S(2)}, u32[]{:S(2)}) collective-permute-start(bf16[2304,128]{1,0:T(8,128)(2,1)} %add_convert_fusion.2), channel_id=1, source_target_pairs={{0,128},{8,904},{16,144},{24,920},{32,160},{40,936},{48,176},{56,9... | collective-permute-start | bytes 1769480 | tf_op jit(solution)/shard_map/ppermute | solution.py:236
